TPU v7x, 32 devices: a whole 2x2x4 slice. The times are simulated.
32 devices in a mesh: dp: 4 (over z), seq: 8 (over y, x, core).
Axes of the slice: x: 2, y: 2, z: 4, core: 2. Of those that a mesh axis runs over, the one named last changes fastest.
Arguments:
- tokens: bfloat16 [4, 8192, 768], P('dp', 'seq'), may hold values from -6 to 6
- cotangent: bfloat16 [4, 8192, 768], P('dp', 'seq'), may hold values from -6 to 6
- first_gain: float32 [768], replicated, may hold values from 0.25 to 1.75
- first_shift: float32 [768], replicated, may hold values from -1.75 to 1.75
- joint_weight: bfloat16 [768, 2304], replicated, may hold values from -0.21875 to 0.21875
- query_bias: float32 [768], replicated, may hold values from -3 to 3
- value_bias: float32 [768], replicated, may hold values from -3 to 3
- score_weight: bfloat16 [768, 12], replicated, may hold values from -0.3125 to 0.3125
- out_weight: bfloat16 [768, 768], replicated, may hold values from -1.75 to 1.75
- out_bias: float32 [768], replicated, may hold values from -3 to 3
- second_gain: float32 [768], replicated, may hold values from 0.25 to 1.75
- second_shift: float32 [768], replicated, may hold values from -1.75 to 1.75
- expand_weight: bfloat16 [768, 3072], replicated, may hold values from -0.21875 to 0.21875
- expand_bias: float32 [3072], replicated, may hold values from -3 to 3
- reduce_weight: bfloat16 [3072, 768], replicated, may hold values from -0.109375 to 0.109375
- reduce_bias: float32 [768], replicated, may hold values from -3 to 3
- picks: int32 [4, 8, 8, 8], P('dp', 'seq'), may hold values from 0 to 1023
- quota: int32 [4, 8, 8], P('dp', 'seq'), may hold values from 0 to 8, as said below
Outputs:
- layer_out: bfloat16 [4, 8192, 768], P('dp', 'seq')
- token_grad: float32 [4, 8192, 768], P('dp', 'seq')
- first_gain_grad: float32 [768], replicated
- first_shift_grad: float32 [768], replicated
- joint_weight_grad: float32 [768, 2304], replicated
- query_bias_grad: float32 [768], replicated
- value_bias_grad: float32 [768], replicated
- score_weight_grad: float32 [768, 12], replicated
- out_weight_grad: float32 [768, 768], replicated
- out_bias_grad: float32 [768], replicated
- second_gain_grad: float32 [768], replicated
- second_shift_grad: float32 [768], replicated
- expand_weight_grad: float32 [768, 3072], replicated
- expand_bias_grad: float32 [3072], replicated
- reduce_weight_grad: float32 [3072, 768], replicated
- reduce_bias_grad: float32 [768], replicated
Inputs may be any that keep to these rules, and one draw needn't show every extreme that they name: quota[s, d] is zero where s > d; the last query block takes 8 keys from every block. `picks`: only entries with c < quota[s, d] are read.
All inputs are finite; a program needn't handle non-finite values.
Results may differ from a plain program's by a relative error of at most 0.011.
Values may be sent and summed in bfloat16 or wider, within the bound.
No kernel may reach another device: no remote copies, remote signals or barrier semaphores. Data moves between devices by JAX's collectives and lax.ppermute only.
A program may use at most 192 MiB of HBM per device.

v0:
```python
import math

import jax
import jax.numpy as jnp
from jax import lax
from jax.sharding import PartitionSpec as P

WIN = 64
PICK = 8


epsilon = 1e-05
very_low = -1e30


def passed_along(value, axis, steps):
    count = lax.axis_size(axis)
    leading, last = (max(0, -steps), min(count, count - steps))
    return lax.ppermute(value, axis, [(source, source + steps) for source in range(leading, last)])


def layer_norm_parts(values, gain, shift):
    average = jnp.mean(values, axis=-1, keepdims=True)
    centred = values - average
    variance = jnp.mean(centred * centred, axis=-1, keepdims=True)
    inverse = lax.rsqrt(variance + epsilon)
    unit = centred * inverse
    return (unit * gain + shift, unit, inverse)


def layer_norm_back(grad_out, unit, inverse, gain):
    grad_unit = grad_out * gain
    mean_grad = jnp.mean(grad_unit, axis=-1, keepdims=True)
    mean_cross = jnp.mean(grad_unit * unit, axis=-1, keepdims=True)
    grad_in = (grad_unit - mean_grad - unit * mean_cross) * inverse
    return (grad_in, jnp.sum(grad_out * unit, axis=0), jnp.sum(grad_out, axis=0))


def gelu_tanh(values):
    return (
        0.5
        * values
        * (1.0 + jnp.tanh(0.7978845608028654 * (values + 0.044715 * values * values * values)))
    )


def cross(left, right):
    return lax.dot_general(
        left, right, (((0,), (0,)), ((), ())), preferred_element_type=jnp.float32
    )


def times_transposed(left, right):
    return lax.dot_general(
        left, right, (((1,), (1,)), ((), ())), preferred_element_type=jnp.float32
    )


def pair_tiles(values, tiles, window):
    shaped = values.reshape((tiles + 1, window) + values.shape[1:])
    return jnp.concatenate([shaped[:-1], shaped[1:]], axis=1)


def arrange(rim, packed, far_packed, far_pos, place, heads, head_size):
    rows = packed.shape[0]
    width = heads * head_size
    tiles = rows // WIN
    near = pair_tiles(jnp.concatenate([rim, packed], axis=0), tiles, WIN)
    near_key = near[..., :width].reshape(tiles, 2 * WIN, heads, head_size)
    near_value = near[..., width : 2 * width].reshape(tiles, 2 * WIN, heads, head_size)
    near_score = near[..., 2 * width :].astype(jnp.float32)
    far_flat = far_packed.reshape(-1, far_packed.shape[-1])
    far_key = far_flat[:, :width].reshape(-1, heads, head_size)
    far_value = far_flat[:, width : 2 * width].reshape(-1, heads, head_size)
    far_score = far_flat[:, 2 * width :].astype(jnp.float32)
    start = place * rows
    ext_pos = start - WIN + jnp.arange(rows + WIN, dtype=jnp.int32)
    near_pos = pair_tiles(ext_pos, tiles, WIN)
    query_pos = (start + jnp.arange(rows, dtype=jnp.int32)).reshape(tiles, WIN)
    near_mask = (
        (near_pos[:, None, :] <= query_pos[:, :, None])
        & (near_pos[:, None, :] > query_pos[:, :, None] - WIN)
        & (near_pos[:, None, :] >= 0)
    )[:, None]
    far_mask = (far_pos.reshape(-1)[None, None, :] <= query_pos[:, :, None] - WIN)[:, None]
    return (near_key, near_value, near_score, far_key, far_value, far_score, near_mask, far_mask)


def attention_logits(query_tiles, keys_set, scale):
    near_key, near_value, near_score, far_key, far_value, far_score, near_mask, far_mask = keys_set
    near_raw = jnp.einsum(
        "tqhd,tkhd->thqk", query_tiles, near_key, preferred_element_type=jnp.float32
    )
    far_raw = jnp.einsum("tqhd,khd->thqk", query_tiles, far_key, preferred_element_type=jnp.float32)
    near_gate = jnp.transpose(jax.nn.log_sigmoid(near_score), (0, 2, 1))[:, :, None, :]
    far_gate = jnp.transpose(jax.nn.log_sigmoid(far_score))[None, :, None, :]
    near_logit = jnp.where(near_mask, near_raw * scale + near_gate, very_low)
    far_logit = jnp.where(far_mask, far_raw * scale + far_gate, very_low)
    return (near_logit, far_logit)


def attention_back(query_tiles, keys_set, grad_mixed, log_total, scale):
    near_key, near_value, near_score, far_key, far_value, far_score, near_mask, far_mask = keys_set
    near_logit, far_logit = attention_logits(query_tiles, keys_set, scale)
    near_prob = jnp.exp(near_logit - log_total[..., None])
    far_prob = jnp.exp(far_logit - log_total[..., None])
    near_low = near_prob.astype(jnp.bfloat16)
    far_low = far_prob.astype(jnp.bfloat16)
    grad_near_prob = jnp.einsum(
        "tqhd,tkhd->thqk", grad_mixed, near_value, preferred_element_type=jnp.float32
    )
    grad_far_prob = jnp.einsum(
        "tqhd,khd->thqk", grad_mixed, far_value, preferred_element_type=jnp.float32
    )
    delta = jnp.sum(near_prob * grad_near_prob, axis=-1) + jnp.sum(
        far_prob * grad_far_prob, axis=-1
    )
    grad_near_logit = near_prob * (grad_near_prob - delta[..., None])
    grad_far_logit = far_prob * (grad_far_prob - delta[..., None])
    near_raw_low = (grad_near_logit * scale).astype(jnp.bfloat16)
    far_raw_low = (grad_far_logit * scale).astype(jnp.bfloat16)
    grad_query = jnp.einsum(
        "thqk,tkhd->tqhd", near_raw_low, near_key, preferred_element_type=jnp.float32
    )
    grad_query = grad_query + jnp.einsum(
        "thqk,khd->tqhd", far_raw_low, far_key, preferred_element_type=jnp.float32
    )
    grad_near_key = jnp.einsum(
        "thqk,tqhd->tkhd", near_raw_low, query_tiles, preferred_element_type=jnp.float32
    )
    grad_near_value = jnp.einsum(
        "thqk,tqhd->tkhd", near_low, grad_mixed, preferred_element_type=jnp.float32
    )
    grad_near_score = jnp.transpose(jnp.sum(grad_near_logit, axis=2), (0, 2, 1)) * jax.nn.sigmoid(
        -near_score
    )
    grad_far_key = jnp.einsum(
        "thqk,tqhd->khd", far_raw_low, query_tiles, preferred_element_type=jnp.float32
    )
    grad_far_value = jnp.einsum(
        "thqk,tqhd->khd", far_low, grad_mixed, preferred_element_type=jnp.float32
    )
    grad_far_score = jnp.transpose(jnp.sum(grad_far_logit, axis=(0, 2))) * jax.nn.sigmoid(
        -far_score
    )
    tiles = grad_near_key.shape[0]
    span = grad_near_key.shape[1]
    near_pack = jnp.concatenate(
        [
            grad_near_key.reshape(tiles, span, -1),
            grad_near_value.reshape(tiles, span, -1),
            grad_near_score,
        ],
        axis=-1,
    )
    slots = grad_far_key.shape[0]
    far_pack = jnp.concatenate(
        [grad_far_key.reshape(slots, -1), grad_far_value.reshape(slots, -1), grad_far_score],
        axis=-1,
    )
    return (grad_query, near_pack, far_pack)


def per_device(
    tokens,
    cotangent,
    first_gain,
    first_shift,
    joint_weight,
    query_bias,
    value_bias,
    score_weight,
    out_weight,
    out_bias,
    second_gain,
    second_shift,
    expand_weight,
    expand_bias,
    reduce_weight,
    reduce_bias,
    picks,
    quota,
):
    rows = tokens.shape[1]
    width = tokens.shape[2]
    heads = score_weight.shape[1]
    head_size = width // heads
    tiles = rows // WIN
    blocks = lax.axis_size("seq")
    place = lax.axis_index("seq")
    scale = 1.0 / math.sqrt(head_size)
    inputs = tokens[0].astype(jnp.float32)
    normed, unit_one, inverse_one = layer_norm_parts(inputs, first_gain, first_shift)
    normed_low = normed.astype(jnp.bfloat16)
    joint = jnp.dot(normed_low, joint_weight, preferred_element_type=jnp.float32)
    query = (joint[:, :width] + query_bias).astype(jnp.bfloat16)
    keys = joint[:, width : 2 * width].astype(jnp.bfloat16)
    values = (joint[:, 2 * width :] + value_bias).astype(jnp.bfloat16)
    score = jnp.dot(normed_low, score_weight, preferred_element_type=jnp.float32).astype(
        jnp.bfloat16
    )
    packed = jnp.concatenate([keys, values, score], axis=1)
    channels = packed.shape[1]
    pick_rows = picks[0, 0]
    flat_rows = pick_rows.reshape(-1)
    live = jnp.arange(PICK, dtype=jnp.int32)[None, :] < quota[0, 0][:, None]
    positions = jnp.where(live, place * rows + pick_rows, 2 * rows * blocks)
    sent = packed[flat_rows].reshape(blocks, PICK, channels)
    rim = passed_along(packed[rows - WIN :], "seq", 1)
    far_packed, far_pos = (
        lax.all_to_all(sent, "seq", split_axis=0, concat_axis=0, tiled=True),
        lax.all_to_all(positions, "seq", split_axis=0, concat_axis=0, tiled=True),
    )
    keys_set = arrange(rim, packed, far_packed, far_pos, place, heads, head_size)
    query_tiles = query.reshape(tiles, WIN, heads, head_size)
    near_logit, far_logit = attention_logits(query_tiles, keys_set, scale)
    top = jnp.maximum(jnp.max(near_logit, axis=-1), jnp.max(far_logit, axis=-1))
    total = jnp.sum(jnp.exp(near_logit - top[..., None]), axis=-1) + jnp.sum(
        jnp.exp(far_logit - top[..., None]), axis=-1
    )
    log_total = top + jnp.log(total)
    near_low = jnp.exp(near_logit - log_total[..., None]).astype(jnp.bfloat16)
    far_low = jnp.exp(far_logit - log_total[..., None]).astype(jnp.bfloat16)
    mixed = jnp.einsum("thqk,tkhd->tqhd", near_low, keys_set[1], preferred_element_type=jnp.float32)
    mixed = mixed + jnp.einsum(
        "thqk,khd->tqhd", far_low, keys_set[4], preferred_element_type=jnp.float32
    )
    mixed_low = mixed.reshape(rows, width).astype(jnp.bfloat16)
    attn = jnp.dot(mixed_low, out_weight, preferred_element_type=jnp.float32) + out_bias
    resid = inputs + attn
    normed_two, unit_two, inverse_two = layer_norm_parts(resid, second_gain, second_shift)
    normed_two_low = normed_two.astype(jnp.bfloat16)
    pre = jnp.dot(normed_two_low, expand_weight, preferred_element_type=jnp.float32) + expand_bias
    activated, gelu_pull = jax.vjp(gelu_tanh, pre)
    hidden_low = activated.astype(jnp.bfloat16)
    layer_out = (
        resid + jnp.dot(hidden_low, reduce_weight, preferred_element_type=jnp.float32) + reduce_bias
    ).astype(jnp.bfloat16)
    grad_out_low = cotangent[0]
    grad_out = grad_out_low.astype(jnp.float32)
    reduce_bias_grad = jnp.sum(grad_out, axis=0)
    grad_hidden = times_transposed(grad_out_low, reduce_weight)
    grad_pre_low = gelu_pull(grad_hidden)[0].astype(jnp.bfloat16)
    expand_bias_grad = jnp.sum(grad_pre_low.astype(jnp.float32), axis=0)
    grad_normed_two = times_transposed(grad_pre_low, expand_weight)
    grad_resid_norm, second_gain_grad, second_shift_grad = layer_norm_back(
        grad_normed_two, unit_two, inverse_two, second_gain
    )
    grad_resid = grad_out + grad_resid_norm
    grad_attn_low = grad_resid.astype(jnp.bfloat16)
    out_bias_grad = jnp.sum(grad_attn_low.astype(jnp.float32), axis=0)
    grad_mixed_low = (
        times_transposed(grad_attn_low, out_weight)
        .astype(jnp.bfloat16)
        .reshape(tiles, WIN, heads, head_size)
    )
    rim_back_set = passed_along(packed[rows - WIN :], "seq", 1)
    far_again, pos_again = (
        lax.all_to_all(sent, "seq", split_axis=0, concat_axis=0, tiled=True),
        lax.all_to_all(positions, "seq", split_axis=0, concat_axis=0, tiled=True),
    )
    keys_back = arrange(rim_back_set, packed, far_again, pos_again, place, heads, head_size)
    grad_query, near_pack, far_pack = attention_back(
        query_tiles, keys_back, grad_mixed_low, log_total, scale
    )
    grad_query_low = grad_query.reshape(rows, width).astype(jnp.bfloat16)
    zero_tile = jnp.zeros((1, WIN, channels), jnp.float32)
    extended = jnp.concatenate([near_pack[:, :WIN], zero_tile], axis=0) + jnp.concatenate(
        [zero_tile, near_pack[:, WIN:]], axis=0
    )
    rim_grad = extended[0]
    own_grad = extended[1:].reshape(rows, channels)
    far_grad_low = far_pack.astype(jnp.bfloat16).reshape(blocks, PICK, channels)
    back_far = lax.all_to_all(far_grad_low, "seq", split_axis=0, concat_axis=0, tiled=True)
    back_rim = passed_along(rim_grad.astype(jnp.bfloat16), "seq", -1)
    own_total = own_grad + jnp.concatenate(
        [jnp.zeros((rows - WIN, channels), jnp.float32), back_rim.astype(jnp.float32)], axis=0
    )
    own_total = own_total.at[flat_rows].add(
        back_far.reshape(blocks * PICK, channels).astype(jnp.float32)
    )
    grad_packed_low = own_total.astype(jnp.bfloat16)
    grad_key_low = grad_packed_low[:, :width]
    grad_value_low = grad_packed_low[:, width : 2 * width]
    grad_score_low = grad_packed_low[:, 2 * width :]
    grad_joint_low = jnp.concatenate([grad_query_low, grad_key_low, grad_value_low], axis=1)
    query_bias_grad = jnp.sum(grad_query_low.astype(jnp.float32), axis=0)
    value_bias_grad = jnp.sum(grad_value_low.astype(jnp.float32), axis=0)
    score_weight_grad = cross(normed_low, grad_score_low)
    grad_normed = times_transposed(grad_joint_low, joint_weight) + times_transposed(
        grad_score_low, score_weight
    )
    grad_input_norm, first_gain_grad, first_shift_grad = layer_norm_back(
        grad_normed, unit_one, inverse_one, first_gain
    )
    token_grad = (grad_resid + grad_input_norm)[None]
    joint_weight_grad = cross(normed_low, grad_joint_low)
    out_weight_grad = cross(mixed_low, grad_attn_low)
    expand_weight_grad = cross(normed_two_low, grad_pre_low)
    reduce_weight_grad = cross(hidden_low, grad_out_low)
    (
        first_gain_grad,
        first_shift_grad,
        joint_weight_grad,
        query_bias_grad,
        value_bias_grad,
        score_weight_grad,
        out_weight_grad,
        out_bias_grad,
        second_gain_grad,
        second_shift_grad,
        expand_weight_grad,
        expand_bias_grad,
        reduce_weight_grad,
        reduce_bias_grad,
    ) = lax.psum(
        (
            first_gain_grad,
            first_shift_grad,
            joint_weight_grad,
            query_bias_grad,
            value_bias_grad,
            score_weight_grad,
            out_weight_grad,
            out_bias_grad,
            second_gain_grad,
            second_shift_grad,
            expand_weight_grad,
            expand_bias_grad,
            reduce_weight_grad,
            reduce_bias_grad,
        ),
        ("dp", "seq"),
    )
    return (
        layer_out[None],
        token_grad,
        first_gain_grad,
        first_shift_grad,
        joint_weight_grad,
        query_bias_grad,
        value_bias_grad,
        score_weight_grad,
        out_weight_grad,
        out_bias_grad,
        second_gain_grad,
        second_shift_grad,
        expand_weight_grad,
        expand_bias_grad,
        reduce_weight_grad,
        reduce_bias_grad,
    )


def solution(mesh):
    placed = (
        P("dp", "seq", None),
        P("dp", "seq", None),
        P(),
        P(),
        P(),
        P(),
        P(),
        P(),
        P(),
        P(),
        P(),
        P(),
        P(),
        P(),
        P(),
        P(),
        P("dp", "seq", None, None),
        P("dp", "seq", None),
    )
    return jax.shard_map(
        per_device,
        mesh=mesh,
        in_specs=placed,
        out_specs=(
            P("dp", "seq", None),
            P("dp", "seq", None),
            P(),
            P(),
            P(),
            P(),
            P(),
            P(),
            P(),
            P(),
            P(),
            P(),
            P(),
            P(),
            P(),
            P(),
        ),
        check_vma=False,
    )
```

profile of v0, /device:TPU:0, one launch (start us, length us, event | category | flops | bytes accessed | tf_op | source)
XLA Modules:
  0.0 1000.0 jit_solution(8566734394154111945)
XLA Ops:
  58.0 9.3 copy.263
  83.8 7.7 fusion.147
  98.8 9.3 copy.262
  116.5 6.9 fusion.148
  152.7 8.4 fusion.143
  161.1 10.5 %fusion.73 = f32[3072,768]{1,0:T(8,128)} fusion(bf16[1,1024,768]{2,1,0:T(8,128)(2,1)S(1)} %copy-done.30, f32[1024,3072]{1,0:T(8,128)S(1)} %fusion.143, f32[3072]{0:T(1024)S(1)} %copy-done.62), kind=kOutput, calls=%fused_computation.117 | convolution fusion | flops 4863295488 | bytes 23605248 | tf_op jit(solution)/shard_map/dot_general | solution.py:48
  171.6 18.3 %convert_reduce_fusion = (f32[3072]{0:T(1024)}, bf16[1024,3072]{1,0:T(8,128)(2,1)}) fusion(bf16[3072,768]{1,0:T(8,128)(2,1)} %param.32, bf16[1,1024,768]{2,1,0:T(8,128)(2,1)} %param.19, f32[1024,3072]{1,0:T(8,128)S(1)} %fusion.143, f32[3072]{0:T(1024)S(1)} %copy-done.62), kind=kOutput, calls=%fused_computation.13 | convolution fusion | flops 4916769792 | bytes 25190400 | tf_op jit(solution)/shard_map/dot_general | solution.py:54
  189.9 10.5 %fusion.150 = (f32[768]{0:T(1024)}, f32[1024,768]{1,0:T(8,128)}) fusion(bf16[1024,3072]{1,0:T(8,128)(2,1)} %get-tuple-element.170, bf16[768,3072]{1,0:T(8,128)(2,1)} %param.30), kind=kOutput, calls=%fused_computation.212 | convolution fusion | flops 4832623616 | bytes 14158848 | tf_op jit(solution)/shard_map/dot_general | solution.py:54
  200.4 8.2 fusion.142
  239.9 9.1 multiply_reduce_fusion
  271.3 9.7 multiply_convert_fusion.2
  283.9 7.4 fusion.54
  291.3 6.5 copy.297
  297.8 9.9 pad_maximum_fusion
  307.8 11.4 %fusion.144 = (f32[16,64,1548]{2,1,0:T(8,128)}, f32[16,64,1548]{2,1,0:T(8,128)}) fusion(f32[16,128,1548]{2,1,0:T(8,128)} %pad_maximum_fusion), kind=kLoop, calls=%fused_computation.206 | loop fusion | bytes 25362432 | tf_op jit(solution)/shard_map/slice | solution.py:269
  343.4 8.5 convert_reduce_fusion.1
  371.4 7.4 scatter_custom_fusion
  386.6 7.0 fusion.28
  393.7 9.6 fusion.38
  403.3 12.0 %fusion.78 = bf16[1,1024,768]{1,2,0:T(8,128)(2,1)} fusion(f32[768]{0:T(1024)} %param.33, f32[1024,768]{0,1:T(8,128)} %copy-done.6, bf16[3072,768]{1,0:T(8,128)(2,1)} %param.32, f32[1024,3072]{1,0:T(8,128)} %copy-done.18, f32[3072]{0:T(1024)} %param.31), kind=kOutput, calls=%fused_computation.122 | convolution fusion | flops 4865654784 | bytes 22035456 | tf_op jit(solution)/shard_map/dot_general | solution.py:237
  428.1 94.8 %all-reduce.8.cloned.1.call-done = (f32[768]{0:T(1024)}, f32[768]{0:T(1024)}, f32[768]{0:T(1024)}, f32[768]{0:T(1024)}, f32[768,12]{0,1:T(8,128)}, /*index=5*/f3...) async-done(((f32[768]{0:T(1024)}, f32[768]{0:T(1024)}, f32[768]{0:T(1024)}, f32[768]{0:T(1024)}, f32[768,12]{0,1:T(8,128)}, ...) | async-done | bytes 73744 | tf_op jit(solution)/shard_map/psum | solution.py:316
  522.9 441.9 %all-reduce.10.cloned.1.call-done = (f32[768,2304]{1,0:T(8,128)}, f32[768,768]{1,0:T(8,128)}, f32[768,3072]{1,0:T(8,128)}, f32[3072,768]{1,0:T(8,128)}) async-done(((f32[768,2304]{1,0:T(8,128)}, f32[768,768]{1,0:T(8,128)}, f32[768,3072]{1,0:T(8,128)}, f32[3072,768]{1,0:T(8,128)}), (f32[768,2304]{1,0:T(8,128)}, f32[768,768]{1,0:T(8,128)}, f32[768,3072]{1,0:T(8,128)}, ...) | async-done | bytes 28311568 | tf_op jit(solution)/shard_map/psum | solution.py:316
  967.4 6.6 copy.431
  979.0 8.8 copy.439
  (275 shorter events, 245.0 us)
Async XLA Ops:
  7.2 17.4 %copy-start = (bf16[768,2304]{1,0:T(8,128)(2,1)S(1)}, bf16[768,2304]{1,0:T(8,128)(2,1)}, u32[]{:S(2)}) copy-start(bf16[768,2304]{1,0:T(8,128)(2,1)} %param.22) | copy-start | bytes 10616836
  7.2 13.0 %copy-start.47 = (f32[768]{0:T(1024)S(1)}, f32[768]{0:T(1024)}, u32[]{:S(2)}) copy-start(f32[768]{0:T(1024)} %param.20) | copy-start | bytes 9220
  7.2 13.0 %copy-start.51 = (f32[768]{0:T(1024)S(1)}, f32[768]{0:T(1024)}, u32[]{:S(2)}) copy-start(f32[768]{0:T(1024)} %param.21) | copy-start | bytes 9220
  8.7 58.6 %all-to-all-start = ((s32[8,1,8]{2,1,0:T(1,128)}), s32[8,1,8]{2,1,0:T(1,128)}, u32[]{:S(2)}, u32[]{:S(2)}) async-start(s32[8,1,8]{2,1,0:T(1,128)} %bitcast.8), calls=%async_computation | async-start | bytes 8192 | tf_op jit(solution)/shard_map/all_to_all | solution.py:212
  35.6 57.6 %collective-permute-start = (bf16[64,1548]{1,0:T(8,128)(2,1)}, bf16[64,1548]{1,0:T(8,128)(2,1)}, u32[]{:S(2)}, u32[]{:S(2)}) collective-permute-start(bf16[64,1548]{1,0:T(8,128)(2,1)} %slice.111), channel_id=1, source_target_pairs={{0,1},{1,2},{2,3},{3,4},{4,5},{5,6},{6,7},{8,9},{9,10},{10,11},{11... | collective-permute-start | bytes 594440 | tf_op jit(solution)/shard_map/ppermute | solution.py:19
  67.3 10.9 %all-to-all-start.1 = ((bf16[8,8,1548]{2,1,0:T(8,128)(2,1)}), bf16[8,8,1548]{2,1,0:T(8,128)(2,1)}, u32[]{:S(2)}, u32[]{:S(2)}) async-start(bf16[8,8,1548]{2,1,0:T(8,128)(2,1)} %bitcast.194), calls=%async_computation.1 | async-start | bytes 425984 | tf_op jit(solution)/shard_map/all_to_all | solution.py:211
  116.4 16.9 %copy-start.10 = (bf16[16,128,768]{1,0,2:T(8,128)(2,1)}, bf16[16,128,768]{1,0,2:T(8,128)(2,1)S(1)}, u32[]{:S(2)}) copy-start(bf16[16,128,768]{1,0,2:T(8,128)(2,1)S(1)} %get-tuple-element.145) | copy-start | bytes 9437188
  123.4 9.8 copy-start.1
  152.2 48.2 %copy-start.6 = (f32[1024,768]{0,1:T(8,128)}, f32[1024,768]{0,1:T(8,128)S(1)}, u32[]{:S(2)}) copy-start(f32[1024,768]{0,1:T(8,128)S(1)} %get-tuple-element.159) | copy-start | bytes 9437188
  161.1 10.5 %copy-start.18 = (f32[1024,3072]{1,0:T(8,128)}, f32[1024,3072]{1,0:T(8,128)S(1)}, u32[]{:S(2)}) copy-start(f32[1024,3072]{1,0:T(8,128)S(1)} %fusion.143) | copy-start | bytes 37748740
  189.9 10.5 %copy-start.64 = (bf16[1024,3072]{1,0:T(8,128)(2,1)S(1)}, bf16[1024,3072]{1,0:T(8,128)(2,1)}, u32[]{:S(2)}) copy-start(bf16[1024,3072]{1,0:T(8,128)(2,1)} %get-tuple-element.170) | copy-start | bytes 18874372
  234.1 15.0 %slice-start.4 = ((s8[6291456]{0:T(1024)(128)(4,1)}), s8[4194304]{0:T(1024)(128)(4,1)S(1)}, s32[]{:S(2)}) async-start(s8[6291456]{0:T(1024)(128)(4,1)} %bitcast.180), calls=%async_computation.9 | async-start | bytes 8388608
  234.1 19.5 %slice-start.2 = ((s8[6291456]{0:T(1024)(128)(4,1)}), s8[4194304]{0:T(1024)(128)(4,1)S(1)}, s32[]{:S(2)}) async-start(s8[6291456]{0:T(1024)(128)(4,1)} %bitcast.178), calls=%async_computation.7 | async-start | bytes 8388608
  239.9 9.2 slice-start.5
  239.9 9.2 copy-start.2
  239.9 13.7 %slice-start.3 = ((s8[6291456]{0:T(1024)(128)(4,1)}), s8[2097152]{0:T(1024)(128)(4,1)S(1)}, s32[]{:S(2)}) async-start(s8[6291456]{0:T(1024)(128)(4,1)} %bitcast.178), calls=%async_computation.8 | async-start | bytes 4194304
  271.3 9.7 copy-start.36
  338.0 33.4 %all-to-all-start.2 = ((bf16[8,8,1548]{2,1,0:T(8,128)(2,1)}), bf16[8,8,1548]{2,1,0:T(8,128)(2,1)}, u32[]{:S(2)}, u32[]{:S(2)}) async-start(bf16[8,8,1548]{2,1,0:T(8,128)(2,1)} %pad_maximum_fusion.10), calls=%async_computation.2 | async-start | bytes 425984 | tf_op jit(solution)/shard_map/all_to_all | solution.py:274
  342.1 180.9 %all-reduce.8.cloned.1.call-start = ((), (), s32[]{:S(2)}) async-start(), calls=%async_computation.3 | async-start | bytes 188416 | tf_op jit(solution)/shard_map/psum | solution.py:316
  342.1 23.1 %collective-permute-start.1 = (bf16[64,1548]{1,0:T(8,128)(2,1)}, bf16[64,1548]{1,0:T(8,128)(2,1)}, u32[]{:S(2)}, u32[]{:S(2)}) collective-permute-start(bf16[64,1548]{1,0:T(8,128)(2,1)} %fusion.106), channel_id=1, source_target_pairs={{1,0},{2,1},{3,2},{4,3},{5,4},{6,5},{7,6},{9,8},{10,9},{11,10},{12... | collective-permute-start | bytes 594440 | tf_op jit(solution)/shard_map/ppermute | solution.py:19
  393.7 571.1 %all-reduce.10.cloned.1.call-start = ((), (), s32[]{:S(2)}) async-start(), calls=%async_computation.4 | async-start | bytes 56623104 | tf_op jit(solution)/shard_map/psum | solution.py:316
  975.8 12.6 %slice-start.6 = ((s8[9437184]{0:T(1024)(128)(4,1)}), s8[4194304]{0:T(1024)(128)(4,1)S(1)}, s32[]{:S(2)}) async-start(s8[9437184]{0:T(1024)(128)(4,1)} %bitcast.190), calls=%async_computation.11 | async-start | bytes 8388608
  979.0 9.4 slice-start.7
  979.0 9.4 slice-start.8
  (57 other events, 249.8 us)
Sparse Core Ops, SparseCore 0:
  393.8 129.0 all-reduce.7
  531.6 433.1 all-reduce.9
where the time goes:
time: 1010 us; the launch traced here: 1000 us
  waiting for transfers between devices  540 us (53%)
  matrix products  169 us (17%)
  local copies, waits for them, and re-layouts  161 us (16%)
  other arithmetic  96.4 us (10%)
  starting transfers between devices  18.2 us (2%)
  between operations  15.2 us (2%)
    psum x2, waiting for transfers between devices, per_device(): lax.psum((first_gain_grad, first_shift_grad, joint_weight_grad, query_bia...  537 us
    unnamed x167, local copies, waits for them, and re-layouts  50.3 us
    dot_general x5, matrix products, times_transposed(): lax.dot_general(left, right, (((1,), (1,)), ((), ())), preferred_element_...  39 us
    dot_general x5, matrix products, cross(): lax.dot_general(left, right, (((0,), (0,)), ((), ())), preferred_element_...  32.3 us
  transfers between devices with their start and end apart: 7, of which 3 were waited for; matrix products, arithmetic and copies ran while one was open for 13% of the time, Pallas kernels for 0%

commit v1 on v0

v1 whole, which is shorter than its diff:
```python
import functools
import math

import jax
import jax.numpy as jnp
from jax import lax
from jax.experimental import pallas as pl
from jax.experimental.pallas import tpu as pltpu
from jax.sharding import PartitionSpec as P

WIN = 64
PICK = 8
LANES = 128
PACK = 4
DIGIT = 32
TOKEN = (8, 128)
epsilon = 1e-05
very_low = -1e30
bf16 = jnp.bfloat16
f32 = jnp.float32


def nt(left, right):
    return lax.dot_general(left, right, (((1,), (1,)), ((), ())), preferred_element_type=f32)


def tn(left, right):
    return lax.dot_general(left, right, (((0,), (0,)), ((), ())), preferred_element_type=f32)


def nn(left, right):
    return jnp.dot(left, right, preferred_element_type=f32)


def three_parts(value):
    high = value.astype(bf16)
    rest = value - high.astype(f32)
    middle = rest.astype(bf16)
    low = (rest - middle.astype(f32)).astype(bf16)
    return high, middle, low


def head_spread(group, head_size, width):
    row = lax.broadcasted_iota(jnp.int32, (LANES, width), 0)
    lane = lax.broadcasted_iota(jnp.int32, (LANES, width), 1)
    return jnp.where(row == group * PACK + lane // WIN, 1.0, 0.0).astype(bf16)


def stack_heads(tile, head_size, factor):
    width = tile.shape[1]
    lane = lax.broadcasted_iota(jnp.int32, tile.shape, 1) // head_size
    scaled = tile * jnp.asarray(factor, tile.dtype)
    zero = jnp.zeros_like(scaled)
    return jnp.concatenate([jnp.where(lane == h, scaled, zero) for h in range(PACK)], axis=0)


def pick_heads(full, head_size):
    lane = lax.broadcasted_iota(jnp.int32, (WIN, full.shape[1]), 1) // head_size
    out = full[0:WIN]
    for h in range(1, PACK):
        out = jnp.where(lane == h, full[h * WIN : (h + 1) * WIN], out)
    return out


def gates_into(gate_ref, group, place, score_ref, rim_score_ref, far_score_ref, head_size, rows, slots):
    width = PACK * WIN
    spread = head_spread(group, head_size, width)

    def expand(score):
        gate = jax.nn.log_sigmoid(score.astype(f32))
        return sum(nn(part, spread) for part in three_parts(gate))

    gate_ref[0:WIN, :] = jnp.where(place == 0, very_low, expand(rim_score_ref[...]))
    gate_ref[WIN : WIN + rows, :] = expand(score_ref[...])
    gate_ref[WIN + rows :, :] = expand(far_score_ref[...])


def near_bias(width):
    key = lax.broadcasted_iota(jnp.int32, (2 * WIN, width), 0)
    query = lax.broadcasted_iota(jnp.int32, (2 * WIN, width), 1) % WIN
    return (key <= query + WIN) & (key > query)


def tile_logits(i, keys_cat, query_stack, gate_ref, far_pos, place, rows, near_ok):
    width = PACK * WIN
    raw = nt(keys_cat, query_stack)
    gate_near = gate_ref[pl.ds(pl.multiple_of(i * WIN, WIN), 2 * WIN), :]
    gate_far = gate_ref[WIN + rows :, :]
    slots = gate_far.shape[0]
    near = jnp.where(near_ok, raw[: 2 * WIN] + gate_near, very_low)
    lane = lax.broadcasted_iota(jnp.int32, (slots, LANES), 1) % WIN
    far_ok = far_pos <= lane + (place * rows + i * WIN - WIN)
    far_raw = raw[2 * WIN :] + gate_far
    far = jnp.concatenate(
        [
            jnp.where(far_ok, far_raw[:, c * LANES : (c + 1) * LANES], very_low)
            for c in range(width // LANES)
        ],
        axis=1,
    )
    return jnp.concatenate([near, far], axis=0)


def launch(kernel, name, work, grid, in_specs, out_specs, out_shape, scratch, limit, operands, after=(), prefetch=(),
           free=()):
    count, extra = len(operands), len(after)

    def body(*refs):
        lead = len(prefetch)
        rest = refs[lead + count + extra :]
        rest[len(shapes)][...] = jnp.zeros(TOKEN, f32)
        kernel(*refs[: lead + count], *rest[: len(shapes)], *rest[len(shapes) + 1 :])

    def place(at, value, spec):
        if spec.memory_space == pltpu.SMEM or at in free:
            return value
        return pltpu.with_memory_space_constraint(value, pltpu.HBM)

    operands = [place(at, value, spec) for at, (value, spec) in enumerate(zip(operands, in_specs))]
    after = [pltpu.with_memory_space_constraint(value, pltpu.HBM) for value in after]
    shapes, kept = out_shape, len(free) > 0 and name == "advance"
    out = pl.pallas_call(
        body,
        grid_spec=pltpu.PrefetchScalarGridSpec(
            num_scalar_prefetch=len(prefetch),
            grid=grid,
            in_specs=list(in_specs) + [pl.BlockSpec(memory_space=pl.ANY)] * extra,
            out_specs=list(out_specs) + [same(*TOKEN)],
            scratch_shapes=scratch,
        ),
        out_shape=[shape if kept else pltpu.HBM(shape.shape, shape.dtype) for shape in shapes] + [pltpu.HBM(TOKEN, f32)],
        compiler_params=pltpu.CompilerParams(vmem_limit_bytes=limit * 2**20),
        cost_estimate=pl.CostEstimate(flops=int(work * 1.15e9), bytes_accessed=2**20, transcendentals=0),
        name=name,
    )(*prefetch, *operands, *after)
    return list(out)


def passed_along(value, axis, steps):
    count = lax.axis_size(axis)
    leading, last = (max(0, -steps), min(count, count - steps))
    return lax.ppermute(value, axis, [(source, source + steps) for source in range(leading, last)])


def normalise(values):
    average = jnp.mean(values, axis=-1, keepdims=True)
    centred = values - average
    variance = jnp.mean(centred * centred, axis=-1, keepdims=True)
    inverse = lax.rsqrt(variance + epsilon)
    return (centred * inverse, inverse)


def normalise_back(grad_out, unit, inverse, gain):
    grad_unit = grad_out * gain
    mean_grad = jnp.mean(grad_unit, axis=-1, keepdims=True)
    mean_cross = jnp.mean(grad_unit * unit, axis=-1, keepdims=True)
    return (grad_unit - mean_grad - unit * mean_cross) * inverse


def row(ref):
    return ref[...].reshape(1, -1)


def column_sums(values):
    return jnp.sum(values, axis=0, keepdims=True)


def accumulate(ref, update):
    step = pl.program_id(0)

    @pl.when(step == 0)
    def _():
        ref[...] = update

    @pl.when(step > 0)
    def _():
        ref[...] += update


def project_kernel(
    steps, tokens_ref, picks_ref, live_ref, gain_ref, shift_ref, joint_ref, query_bias_ref, value_bias_ref,
    score_weight_ref, normed_ref, q_ref, k_ref, v_ref, score_ref, rim_ref, sent_ref, gathered,
):
    step = pl.program_id(0)
    tile, width = tokens_ref.shape
    unit, _ = normalise(tokens_ref[...].astype(f32))
    normed = (unit * row(gain_ref) + row(shift_ref)).astype(bf16)
    normed_ref[...] = normed
    q_ref[...] = (nn(normed, joint_ref[:, :width]) + row(query_bias_ref)).astype(bf16)
    keys = nn(normed, joint_ref[:, width : 2 * width]).astype(bf16)
    values = (nn(normed, joint_ref[:, 2 * width :]) + row(value_bias_ref)).astype(bf16)
    score = nn(normed, score_weight_ref[...]).astype(bf16)
    heads = score.shape[1]
    k_ref[...] = keys
    v_ref[...] = values
    score_ref[...] = jnp.zeros_like(score_ref)
    score_ref[:, :heads] = score
    picks = picks_ref[...]
    slots = picks.shape[0]
    chosen = picks - step * tile == lax.broadcasted_iota(jnp.int32, (slots, tile), 1)
    chosen = jnp.where(chosen, 1.0, 0.0).astype(bf16)
    parts = ((0, keys), (width, values), (2 * width, score_ref[...]))

    @pl.when(step == 0)
    def _():
        gathered[...] = jnp.zeros_like(gathered)

    for start, part in parts:
        gathered[:, start : start + part.shape[1]] += nn(chosen, part)

    @pl.when(step == steps - 1)
    def _():
        for start, part in parts:
            rim_ref[:, start : start + part.shape[1]] = part[tile - WIN :]
        sent_ref[...] = gathered[...].astype(bf16)
        lane = lax.broadcasted_iota(jnp.int32, (slots, LANES), 1)
        coded = jnp.where(lane == heads, picks // DIGIT, jnp.where(lane == heads + 1, picks % DIGIT, live_ref[...]))
        last = gathered[:, 2 * width :]
        sent_ref[:, 2 * width :] = jnp.where(
            (lane >= heads) & (lane < heads + 3), coded.astype(f32), last
        ).astype(bf16)


def same(*shape):
    return pl.BlockSpec(shape, lambda *_: (0,) * len(shape))


def tiled(*shape):
    return pl.BlockSpec(shape, lambda r, *_: (r,) + (0,) * (len(shape) - 1))


def project(tokens, picks, live, gain, shift, joint, query_bias, value_bias, score_weight, tile=256):
    rows, width = tokens.shape
    slots = picks.shape[0]
    channels = 2 * width + LANES
    steps = rows // tile
    S = jax.ShapeDtypeStruct
    return launch(
        functools.partial(project_kernel, steps),
        "project", 8, (steps,),
        [
            tiled(tile, width), same(slots, 1), same(slots, 1), same(width), same(width), same(*joint.shape), same(width),
            same(width), same(*score_weight.shape),
        ],
        [tiled(tile, width)] * 4 + [tiled(tile, LANES), same(WIN, channels), same(slots, channels)],
        [S((rows, width), bf16)] * 4 + [S((rows, LANES), bf16), S((WIN, channels), bf16), S((slots, channels), bf16)],
        [pltpu.VMEM((slots, channels), f32)], 24,
        (tokens, picks, live, gain, shift, joint, query_bias, value_bias, score_weight),
    )


def far_positions(far_score, heads, place_rows, blocks):
    wide = far_score.astype(f32)
    slot = lax.broadcasted_iota(jnp.int32, (far_score.shape[0], 1), 0)
    at = (wide[:, heads : heads + 1] * DIGIT + wide[:, heads + 1 : heads + 2]).astype(jnp.int32)
    return jnp.where(
        wide[:, heads + 2 : heads + 3] > 0.5, (slot // PICK) * place_rows + at, 2 * place_rows * blocks
    )


def load_block(group, place_ref, k_ref, v_ref, score_ref, rim_refs, far_refs, keys, values, gate_ref, head_size):
    rows, width = k_ref.shape
    rim_k_ref, rim_v_ref, rim_score_ref = rim_refs
    far_score_ref = far_refs[2]
    slots = far_score_ref.shape[0]
    keys[0:WIN, :] = rim_k_ref[...]
    keys[WIN:, :] = k_ref[...]
    values[0:WIN, :] = rim_v_ref[...]
    values[WIN:, :] = v_ref[...]
    gates_into(gate_ref, group, place_ref[0], score_ref, rim_score_ref, far_score_ref, head_size, rows, slots)


def attend_kernel(
    heads, head_size, unroll, place_ref, q_ref, k_ref, v_ref, score_ref,
    rim_k_ref, rim_v_ref, rim_score_ref, far_k_ref, far_v_ref, far_score_ref,
    mixed_ref, total_ref, keys, values, gate_ref,
):
    group = pl.program_id(0)
    place = place_ref[0]
    rows, width = q_ref.shape
    slots = far_k_ref.shape[0]
    load_block(
        group, place_ref, k_ref, v_ref, score_ref, (rim_k_ref, rim_v_ref, rim_score_ref),
        (far_k_ref, far_v_ref, far_score_ref), keys, values, gate_ref, head_size,
    )
    near_ok = near_bias(width)
    far_pos = jnp.broadcast_to(far_positions(far_score_ref[...], heads, rows, slots // PICK), (slots, LANES))

    @pl.loop(0, rows // WIN, unroll=unroll)
    def _(i):
        at = pl.ds(pl.multiple_of(i * WIN, WIN), WIN)
        span = pl.ds(pl.multiple_of(i * WIN, WIN), 2 * WIN)
        keys_cat = jnp.concatenate([keys[span, :], far_k_ref[...]], axis=0)
        values_cat = jnp.concatenate([values[span, :], far_v_ref[...]], axis=0)
        stack = stack_heads(q_ref[at, :], head_size, 1.0 / math.sqrt(head_size))
        logit = tile_logits(i, keys_cat, stack, gate_ref, far_pos, place, rows, near_ok)
        top = jnp.max(logit, axis=0, keepdims=True)
        power = jnp.exp(logit - top)
        total = jnp.sum(power, axis=0, keepdims=True)
        prob = (power * (1.0 / total)).astype(bf16)
        total_ref[0, pl.ds(i, 1), :] = top + jnp.log(total)
        mixed_ref[at, :] = pick_heads(tn(prob, values_cat), head_size).astype(bf16)


def far_specs(slots, width, groups, offset=0):
    return [
        pl.BlockSpec((slots, width), lambda g: (0, g + offset)),
        pl.BlockSpec((slots, width), lambda g: (0, groups + g + offset)),
        pl.BlockSpec((slots, LANES), lambda g: (0, 2 * groups * width // LANES)),
    ]


def attend(place, q, k, v, score, rim, far, heads, unroll=8):
    rows, model = q.shape
    slots = far.shape[0]
    width = PACK * WIN
    groups = model // width
    cols = pl.BlockSpec((rows, width), lambda g: (0, g))
    return launch(
        functools.partial(attend_kernel, heads, WIN, unroll),
        "attend", 12, (groups,),
        [pl.BlockSpec(memory_space=pltpu.SMEM), cols, cols, cols, pl.BlockSpec((rows, LANES), lambda g: (0, 0))]
        + far_specs(WIN, width, groups) + far_specs(slots, width, groups),
        [cols, pl.BlockSpec((1, rows // WIN, width), lambda g: (g, 0, 0))],
        [
            jax.ShapeDtypeStruct((rows, model), bf16),
            jax.ShapeDtypeStruct((groups, rows // WIN, width), f32),
        ],
        [
            pltpu.VMEM((WIN + rows, width), bf16),
            pltpu.VMEM((WIN + rows, width), bf16),
            pltpu.VMEM((WIN + rows + slots, width), f32),
        ],
        32, (place, q, k, v, score, rim, rim, rim, far, far, far),
    )


def attend_back_kernel(
    heads, head_size, unroll, place_ref, q_ref, k_ref, v_ref, grad_ref, total_ref, score_ref,
    rim_k_ref, rim_v_ref, rim_score_ref, far_k_ref, far_v_ref, far_score_ref,
    dq_ref, dk_ref, dv_ref, ds_ref, rim_out, far_out,
    keys, values, gate_ref, dkeys, dvalues, dscore, rim_ds, far_ds,
):
    group = pl.program_id(0)
    model = (rim_out.shape[1] - LANES) // 2
    place = place_ref[0]
    rows, width = q_ref.shape
    slots = far_k_ref.shape[0]
    load_block(
        group, place_ref, k_ref, v_ref, score_ref, (rim_k_ref, rim_v_ref, rim_score_ref),
        (far_k_ref, far_v_ref, far_score_ref), keys, values, gate_ref, head_size,
    )
    near_ok = near_bias(width)
    far_pos = jnp.broadcast_to(far_positions(far_score_ref[...], heads, rows, slots // PICK), (slots, LANES))
    for ref in (dkeys, dvalues, dscore):
        ref[...] = jnp.zeros_like(ref)

    @pl.loop(0, rows // WIN, unroll=unroll)
    def _(i):
        at = pl.ds(pl.multiple_of(i * WIN, WIN), WIN)
        span = pl.ds(pl.multiple_of(i * WIN, WIN), 2 * WIN)
        keys_cat = jnp.concatenate([keys[span, :], far_k_ref[...]], axis=0)
        values_cat = jnp.concatenate([values[span, :], far_v_ref[...]], axis=0)
        stack = stack_heads(q_ref[at, :], head_size, 1.0 / math.sqrt(head_size))
        grad_stack = stack_heads(grad_ref[at, :], head_size, 1.0)
        logit = tile_logits(i, keys_cat, stack, gate_ref, far_pos, place, rows, near_ok)
        prob = jnp.exp(logit - total_ref[0, pl.ds(i, 1), :])
        grad_prob = nt(values_cat, grad_stack)
        delta = jnp.sum(prob * grad_prob, axis=0, keepdims=True)
        grad_logit = prob * (grad_prob - delta)
        low = grad_logit.astype(bf16)
        dq_ref[at, :] = (pick_heads(tn(low, keys_cat), head_size) * (1.0 / math.sqrt(head_size))).astype(bf16)
        for ref, update in (
            (dkeys, nn(low, stack)),
            (dvalues, nn(prob.astype(bf16), grad_stack)),
            (dscore, grad_logit),
        ):
            ref[span, :] += update[: 2 * WIN]
            ref[WIN + rows :, :] += update[2 * WIN :]

    dk_ref[...] = dkeys[WIN : WIN + rows, :]
    dv_ref[...] = dvalues[WIN : WIN + rows, :]
    for out, start, count in ((rim_out, 0, WIN), (far_out, WIN + rows, slots)):
        for base, ref in ((0, dkeys), (model, dvalues)):
            at = pl.ds(pl.multiple_of(base + group * width, LANES), width)
            out[:, at] = ref[start : start + count, :].astype(bf16)
    gather = head_spread(group, head_size, width)
    for out_ref, score, start, count in (
        (rim_ds, rim_score_ref, 0, WIN),
        (ds_ref, score_ref, WIN, rows),
        (far_ds, far_score_ref, WIN + rows, slots),
    ):
        sums = dscore[start : start + count, :]
        high = sums.astype(bf16)
        rest = (sums - high.astype(f32)).astype(bf16)
        update = (nt(high, gather) + nt(rest, gather)) * jax.nn.sigmoid(-score[...].astype(f32))
        accumulate(out_ref, update)
    rim_out[:, 2 * model :] = rim_ds[...].astype(bf16)
    far_out[:, 2 * model :] = far_ds[...].astype(bf16)


def attend_back(place, q, k, v, grad, total, score, rim, far, heads, after=(), unroll=4):
    rows, model = q.shape
    slots, channels = far.shape
    width = PACK * WIN
    groups = model // width
    cols = pl.BlockSpec((rows, width), lambda g: (0, g))
    S = jax.ShapeDtypeStruct
    return launch(
        functools.partial(attend_back_kernel, heads, WIN, unroll),
        "attend_back", 28, (groups,),
        [
            pl.BlockSpec(memory_space=pltpu.SMEM),
            cols, cols, cols, cols,
            pl.BlockSpec((1, rows // WIN, width), lambda g: (g, 0, 0)),
            same(rows, LANES),
        ] + far_specs(WIN, width, groups) + far_specs(slots, width, groups),
        [cols, cols, cols, same(rows, LANES), same(WIN, channels), same(slots, channels)],
        [
            S((rows, model), bf16), S((rows, model), f32), S((rows, model), f32), S((rows, LANES), f32),
            S((WIN, channels), bf16), S((slots, channels), bf16),
        ],
        [
            pltpu.VMEM((WIN + rows, width), bf16),
            pltpu.VMEM((WIN + rows, width), bf16),
        ] + [pltpu.VMEM((WIN + rows + slots, width), f32)] * 4
        + [pltpu.VMEM((WIN, LANES), f32), pltpu.VMEM((slots, LANES), f32)],
        44, (place, q, k, v, grad, total, score, rim, rim, rim, far, far, far), after,
    )


cubic = 0.044715
root = 0.7978845608028654


def feed_kernel(
    tile, pieces, blocks_one, blocks_two, mine_ref, mixed_ref, tokens_ref, cot_ref, out_weight_ref, out_bias_ref, gain_ref,
    shift_ref, expand_bias_ref, expand_hbm, reduce_hbm,
    resid_ref, hidden_ref, grad_pre_ref, sums_ref, send_one, keep_one, send_two, keep_two,
    expand, reduce, normed, hidden, grad_pre, arrived,
):
    step = pl.program_id(0)
    rows, width = cot_ref.shape
    inner = expand.shape[1]
    span = inner // pieces
    steps = rows // tile
    mine = mine_ref[0]

    def fetches():
        result = []
        for piece in range(pieces):
            at = pl.ds(piece * span, span)
            result.append(pltpu.make_async_copy(expand_hbm.at[:, at], expand.at[:, at], arrived.at[2 * piece]))
            result.append(pltpu.make_async_copy(reduce_hbm.at[at, :], reduce.at[at, :], arrived.at[2 * piece + 1]))
        return result

    @pl.when(step == 0)
    def _():
        for fetch in fetches():
            fetch.start()

    def feed_tile(first):
        here = pl.ds(pl.multiple_of(step * tile, tile), tile)
        cot = cot_ref[here, :]
        resid = tokens_ref[...].astype(f32) + nn(mixed_ref[...], out_weight_ref[...]) + row(out_bias_ref)
        resid_ref[...] = resid
        unit, _ = normalise(resid)
        low = (unit * row(gain_ref) + row(shift_ref)).astype(bf16)
        normed[here, :] = low
        sums = []
        for piece in range(pieces):
            at = slice(piece * span, (piece + 1) * span)
            if first:
                for fetch in fetches()[2 * piece : 2 * piece + 2]:
                    fetch.wait()
            pre = nn(low, expand[:, at]) + row(expand_bias_ref)[:, at]
            back = nt(cot, reduce[at, :])
            squared = pre * pre
            half = 0.5 + 0.5 * jnp.tanh(pre * (root + root * cubic * squared))
            active = pre * half
            slope = half + (active - active * half) * (2.0 * root + 6.0 * root * cubic * squared)
            active = active.astype(bf16)
            hidden[here, at] = active
            hidden_ref[:, at] = active
            grad = (back * slope).astype(bf16)
            grad_pre[here, at] = grad
            grad_pre_ref[:, at] = grad
            sums.append(column_sums(grad.astype(f32)))
        accumulate(sums_ref, jnp.concatenate(sums, axis=1))

    @pl.when(step == 0)
    def _():
        feed_tile(True)

    @pl.when((step > 0) & (step < steps))
    def _():
        feed_tile(False)

    def block(at, half):
        return jnp.where(at < half, at + (1 - mine) * half, at - half + mine * half)

    def outers(start, half, left, right, send, keep):
        size = send.shape[0]
        at = step - start

        @pl.when((at >= 0) & (at < 2 * half))
        def _():
            lanes = pl.ds(pl.multiple_of(block(at, half) * size, LANES), size)
            update = tn(left[:, lanes], right[...]).astype(bf16)

            @pl.when(at < half)
            def _():
                send[...] = update

            @pl.when(at >= half)
            def _():
                keep[...] = update

    outers(steps, blocks_one, hidden, cot_ref, send_one, keep_one)
    outers(steps + 2 * blocks_one, blocks_two, normed, grad_pre, send_two, keep_two)


def feed(
    mine, mixed, tokens, cot, out_weight, out_bias, gain, shift, expand, expand_bias, reduce,
    tile=256, pieces=4, blocks_one=3, blocks_two=1,
):
    rows, width = tokens.shape
    inner = expand.shape[1]
    steps = rows // tile
    size_one, size_two = inner // (2 * blocks_one), width // (2 * blocks_two)
    S = jax.ShapeDtypeStruct

    def early(*shape):
        return pl.BlockSpec(shape, lambda r, *_: (jnp.minimum(r, steps - 1), 0))

    def late(start, count, *shape):
        return pl.BlockSpec(shape, lambda r, *_: (jnp.clip(r - start, 0, count - 1), 0))

    middle = steps + 2 * blocks_one
    return launch(
        functools.partial(feed_kernel, tile, pieces, blocks_one, blocks_two),
        "feed", 28, (middle + 2 * blocks_two,),
        [early(tile, width)] * 2 + [
            same(rows, width), same(width, width), same(width), same(width), same(width), same(inner),
            pl.BlockSpec(memory_space=pl.ANY), pl.BlockSpec(memory_space=pl.ANY),
        ],
        [
            early(tile, width), early(tile, inner), early(tile, inner), same(1, inner),
            late(steps, blocks_one, size_one, width), late(steps + blocks_one, blocks_one, size_one, width),
            late(middle, blocks_two, size_two, inner), late(middle + blocks_two, blocks_two, size_two, inner),
        ],
        [
            S((rows, width), f32), S((rows, inner), bf16), S((rows, inner), bf16), S((1, inner), f32),
            S((inner // 2, width), bf16), S((inner // 2, width), bf16),
            S((width // 2, inner), bf16), S((width // 2, inner), bf16),
        ],
        [
            pltpu.VMEM((width, inner), bf16), pltpu.VMEM((inner, width), bf16), pltpu.VMEM((rows, width), bf16),
            pltpu.VMEM((rows, inner), bf16), pltpu.VMEM((rows, inner), bf16), pltpu.SemaphoreType.DMA((2 * pieces,)),
        ],
        60, (mixed, tokens, cot, out_weight, out_bias, gain, shift, expand_bias, expand, reduce), (), (mine,),
    )


def feed_back_kernel(
    resid_ref, cot_ref, grad_pre_ref, out_weight_ref, gain_ref, expand_ref,
    grad_resid_ref, grad_attn_ref, grad_mixed_ref, sums_ref,
):
    cot = cot_ref[...].astype(f32)
    unit, inverse = normalise(resid_ref[...])
    grad_normed = nt(grad_pre_ref[...], expand_ref[...])
    grad_resid = cot + normalise_back(grad_normed, unit, inverse, row(gain_ref))
    grad_resid_ref[...] = grad_resid
    grad_attn = grad_resid.astype(bf16)
    grad_attn_ref[...] = grad_attn
    grad_mixed_ref[...] = nt(grad_attn, out_weight_ref[...]).astype(bf16)
    accumulate(
        sums_ref,
        jnp.concatenate(
            [
                column_sums(grad_attn.astype(f32)),
                column_sums(grad_normed * unit),
                column_sums(grad_normed),
                column_sums(cot),
            ],
            axis=0,
        ),
    )


def feed_back(resid, cot, grad_pre, out_weight, gain, expand, after=(), tile=256):
    rows, width = resid.shape
    inner = expand.shape[1]
    S = jax.ShapeDtypeStruct
    return launch(
        feed_back_kernel, "feed_back", 11, (rows // tile,),
        [tiled(tile, width)] * 2 + [tiled(tile, inner), same(width, width), same(width), same(width, inner)],
        [tiled(tile, width)] * 3 + [same(4, width)],
        [S((rows, width), f32), S((rows, width), bf16), S((rows, width), bf16), S((4, width), f32)],
        [], 40, (resid, cot, grad_pre, out_weight, gain, expand), after,
    )


def finish_kernel(resid_ref, hidden_ref, reduce_ref, bias_ref, out_ref):
    out_ref[...] = (resid_ref[...] + nn(hidden_ref[...], reduce_ref[...]) + row(bias_ref)).astype(bf16)


def finish(resid, hidden, reduce, bias, after=(), tile=256):
    rows, width = resid.shape
    inner = reduce.shape[0]
    return launch(
        finish_kernel, "finish", 7, (rows // tile,),
        [tiled(tile, width), tiled(tile, inner), same(inner, width), same(width)],
        [tiled(tile, width)], [jax.ShapeDtypeStruct((rows, width), bf16)],
        [], 40, (resid, hidden, reduce, bias), after,
    )


def pair_outer_kernel(mine_ref, a_ref, b_ref, c_ref, *refs):
    d_ref, send_ref, keep_ref = refs
    one = tn(a_ref[...], b_ref[...]).astype(bf16)
    two = tn(c_ref[...], d_ref[...]).astype(bf16)
    mine = mine_ref[0]
    send_ref[...] = jnp.where(mine == 0, two, one)
    keep_ref[...] = jnp.where(mine == 0, one, two)


def pair_outer(mine, a, b, c, d, name, work, after=()):
    rows, m = a.shape
    S = jax.ShapeDtypeStruct
    return launch(
        pair_outer_kernel, name, work, (1,),
        [same(rows, m)] * 4, [same(m, m)] * 2, [S((m, m), bf16)] * 2,
        [], 40, (a, b, c, d), after, (mine,),
    )


def join_keys_kernel(
    tile, mine_ref, dk_ref, dv_ref, ds_ref, rim_ref, far_ref, picks_ref, normed_ref,
    dk_out, dv_out, ds_out, send_ref, keep_ref, both,
):
    step = pl.program_id(0)
    rows, width = normed_ref.shape
    steps = rows // tile
    slots = far_ref.shape[0]
    mine = mine_ref[0]

    @pl.when(step < steps)
    def _():
        chosen = picks_ref[...] - step * tile == lax.broadcasted_iota(jnp.int32, (tile, slots), 0)
        chosen = jnp.where(chosen, 1.0, 0.0).astype(bf16)
        at_end = jnp.where(step == steps - 1, 1.0, 0.0)
        here = pl.ds(pl.multiple_of(step * tile, tile), tile)

        def whole(own, start):
            span = own.shape[1]
            total = own + nn(chosen, far_ref[:, start : start + span])
            rim = rim_ref[:, start : start + span].astype(f32) * at_end
            return jnp.concatenate([total[: tile - WIN], total[tile - WIN :] + rim], axis=0).astype(bf16)

        dk = whole(dk_ref[...], 0)
        dv = whole(dv_ref[...], width)
        dk_out[...] = dk
        dv_out[...] = dv
        ds_out[...] = whole(ds_ref[...], 2 * width)
        both[here, :width] = dk
        both[here, width:] = dv

    half = width // 2
    for turn, ref in ((0, send_ref), (1, keep_ref)):
        @pl.when(step == steps + turn)
        def _():
            at = (1 - mine) if turn == 0 else mine
            ref[...] = tn(normed_ref[:, pl.ds(pl.multiple_of(at * half, LANES), half)], both[...]).astype(bf16)


def join_keys(mine, dk, dv, ds, rim, far, picks, normed, after=(), tile=256):
    rows, width = dk.shape
    slots, channels = far.shape
    S = jax.ShapeDtypeStruct
    steps = rows // tile

    def early(*shape):
        return pl.BlockSpec(shape, lambda r, *_: (jnp.minimum(r, steps - 1), 0))

    return launch(
        functools.partial(join_keys_kernel, tile),
        "join_keys", 8, (steps + 2,),
        [
            early(tile, width), early(tile, width), early(tile, LANES),
            same(WIN, channels), same(slots, channels), same(1, slots), same(rows, width),
        ],
        [early(tile, width), early(tile, width), early(tile, LANES)] + [same(width // 2, 2 * width)] * 2,
        [S((rows, width), bf16), S((rows, width), bf16), S((rows, LANES), bf16)]
        + [S((width // 2, 2 * width), bf16)] * 2,
        [pltpu.VMEM((rows, 2 * width), bf16)], 40, (dk, dv, ds, rim, far, picks, normed), after, (mine,),
    )


def join_tokens_kernel(
    tokens_ref, resid_ref, dq_ref, dk_ref, dv_ref, ds_ref, gain_ref, shift_ref, joint_ref, score_weight_ref,
    token_ref, sums_ref, score_grad_ref,
):
    width = tokens_ref.shape[1]
    heads = score_weight_ref.shape[1]
    unit, inverse = normalise(tokens_ref[...].astype(f32))
    gain = row(gain_ref)
    normed = (unit * gain + row(shift_ref)).astype(bf16)
    dq, dk, dv, ds = dq_ref[...], dk_ref[...], dv_ref[...], ds_ref[...]
    grad_normed = (
        nt(dq, joint_ref[:, :width])
        + nt(dk, joint_ref[:, width : 2 * width])
        + nt(dv, joint_ref[:, 2 * width :])
        + nt(ds[:, :heads], score_weight_ref[...])
    )
    token_ref[...] = resid_ref[...] + normalise_back(grad_normed, unit, inverse, gain)
    accumulate(
        sums_ref,
        jnp.concatenate(
            [
                column_sums(grad_normed * unit),
                column_sums(grad_normed),
                column_sums(dq.astype(f32)),
                column_sums(dv.astype(f32)),
            ],
            axis=0,
        ),
    )
    accumulate(score_grad_ref, tn(ds, normed)[: score_grad_ref.shape[0]])


def join_tokens(tokens, resid, dq, dk, dv, ds, gain, shift, joint, score_weight, after=(), tile=256):
    rows, width = tokens.shape
    heads = score_weight.shape[1]
    S = jax.ShapeDtypeStruct
    return launch(
        join_tokens_kernel, "join_tokens", 9, (rows // tile,),
        [tiled(tile, width)] * 5 + [
            tiled(tile, LANES), same(width), same(width), same(*joint.shape), same(*score_weight.shape),
        ],
        [tiled(tile, width), same(4, width), same(heads, width)],
        [S((rows, width), f32), S((4, width), f32), S((heads, width), f32)],
        [], 40, (tokens, resid, dq, dk, dv, ds, gain, shift, joint, score_weight), after,
    )


def swap(value, axis, bit):
    count = lax.axis_size(axis)
    return lax.ppermute(value, axis, [(i, i ^ bit) for i in range(count)])


def side(axis, bit):
    return (lax.axis_index(axis) // bit) % 2


def axis_bits(axis):
    count, bits, bit = lax.axis_size(axis), [], 1
    while bit < count:
        bits.append((axis, bit))
        bit *= 2
    return bits


def woven(*lists):
    result = []
    for step in range(max(map(len, lists))):
        for items in lists:
            result += items[step : step + 1]
    return result


def orders():
    near, far = axis_bits("seq"), axis_bits("dp")
    first, rest = near[:1], near[1:]
    return (
        first + rest + far,
        first + woven(rest[::-1], far),
    )


def cut(value, pieces):
    return value.reshape(pieces, value.shape[0] // pieces, value.shape[1])


class Chain:
    def __init__(self, send, keep, order):
        self.order, self.level, self.down = order, 0, True
        half = 2 ** (len(order) - 1)
        self.send, self.keep = cut(send, half), cut(keep, half)
        self.mine = [side(*where).astype(jnp.int32) for where in order]

    def got(self):
        return swap(self.send, *self.order[self.level])


def added(one, two):
    return (one[...].astype(f32) + two[...].astype(f32)).astype(bf16)


class Total:
    def __init__(self, value, order):
        self.send, self.order, self.level = value, order, 0

    def got(self):
        return swap(self.send, *self.order[self.level])


def advance_kernel(plan, bits_ref, *refs):
    refs = list(refs)
    outs = refs[sum(4 if kind == "split" else 2 for kind in plan) :]
    for kind in plan:
        if kind == "split":
            for _ in range(2):
                outs.pop(0)[...] = added(refs.pop(0), refs.pop(0))
        elif kind == "sum":
            outs.pop(0)[...] = refs.pop(0)[...] + refs.pop(0)[...]
        elif kind == "close":
            outs.pop(0)[...] = added(refs.pop(0), refs.pop(0))
        else:
            out = outs.pop(0)
            for which in range(2):
                out[which] = refs.pop(0)[...]


def advance(chains, after=()):
    plan, operands, in_specs, out_specs, shapes, bits, free = [], [], [], [], [], [], []
    depth = len(chains[0].order)
    for chain in chains:
        if isinstance(chain, Total):
            plan.append("sum")
            continue
        last = chain.down and chain.level == depth - 1
        plan.append("close" if last else "split" if chain.down else "stack")
    sizes = [chain.send.shape[0] // (2 if kind == "split" else 1) for chain, kind in zip(chains, plan)]
    steps = min([4] + [size for size, kind in zip(sizes, plan) if kind != "sum"])
    S = jax.ShapeDtypeStruct

    def half_of(which, other, block, tail):
        def index(g, bits_ref):
            mine = bits_ref[which]
            return ((1 - mine if other else mine) * steps + g, 0, 0)

        return pl.BlockSpec((block,) + tail, index)

    for chain, kind, size in zip(chains, plan, sizes):
        got, tail = chain.got(), chain.send.shape[1:]
        block = size // steps
        if kind == "sum":
            free += [len(operands), len(operands) + 1]
            operands += [chain.send, got]
            in_specs += [same(*chain.send.shape)] * 2
            out_specs += [same(*chain.send.shape)]
            shapes += [S(chain.send.shape, f32)]
        elif kind == "split":
            which = len(bits)
            bits.append(chain.mine[chain.level + 1])
            places = len(operands)
            free += [places + 1, places + 3] if chain.level == 0 else range(places, places + 4)
            for other in (True, False):
                operands += [chain.keep, got]
                in_specs += [half_of(which, other, block, tail)] * 2
            out_specs += [tiled(block, *tail)] * 2
            shapes += [S((size,) + tail, bf16)] * 2
        elif kind == "close":
            free += [len(operands), len(operands) + 1]
            operands += [chain.keep, got]
            in_specs += [tiled(block, *tail)] * 2
            out_specs += [tiled(block, *tail)]
            shapes += [S((size,) + tail, bf16)]
        else:
            free += [len(operands), len(operands) + 1]
            operands += [chain.send, got]
            in_specs += [tiled(block, *tail)] * 2
            out_specs += [pl.BlockSpec((2, block) + tail, lambda g, *_: (0, g, 0, 0))]
            shapes += [S((2, size) + tail, bf16)]
    bits = jnp.stack(bits) if bits else jnp.zeros((1,), jnp.int32)
    outs = launch(
        functools.partial(advance_kernel, plan), "advance", 2, (steps,), in_specs, out_specs, shapes, [], 40, operands,
        after, (bits,), free,
    )
    for chain, kind in zip(chains, plan):
        if kind == "split":
            chain.send, chain.keep = outs[:2]
            chain.level += 1
            outs = outs[2:]
        elif kind == "sum":
            chain.send = outs[0]
            chain.level += 1
            outs = outs[1:]
        else:
            chain.send = outs[0].reshape((-1,) + chain.send.shape[1:])
            outs = outs[1:]
            if kind == "close":
                chain.down = False
            else:
                chain.level -= 1
    return outs[0]


def ends(chain):
    return chain.send, chain.got()


def own_place(order):
    place = 0
    for axis, bit in order:
        place = place * 2 + side(axis, bit)
    return place.astype(jnp.int32).reshape(1)


def piece_of(own, p, count, value_ref, other_ref):
    half = count // 2
    at = jnp.bitwise_xor(own & (half - 1), p & (half - 1))
    far_side = jnp.bitwise_xor(own, p) >= half
    return jnp.where(far_side, other_ref[at], value_ref[at]).astype(f32)


def widen_kernel(group, count, own_ref, value_ref, other_ref, out_ref):
    own, first = own_ref[0], pl.program_id(0) * group
    for i in range(group):
        out_ref[i] = piece_of(own, first + i, count, value_ref, other_ref)


def widen(own, value, other, name, after=(), group=4):
    half, size, n = value.shape
    count = 2 * half
    out, token = launch(
        functools.partial(widen_kernel, group, count), name, 5, (count // group,),
        [same(half, size, n)] * 2, [tiled(group, size, n)], [jax.ShapeDtypeStruct((count, size, n), f32)],
        [], 40, (value, other), after, (own,), (0, 1),
    )
    return out.reshape(count * size, n), token


def widen_pair_kernel(group, count, own_one_ref, own_two_ref, v_one, o_one, v_two, o_two, first_ref, joint_ref):
    own_one, own_two = own_one_ref[0], own_two_ref[0]
    half, base = count // 2, pl.program_id(0) * group
    width, size = v_one.shape[2], v_two.shape[1]
    for i in range(group):
        p = base + i
        first_ref[i] = piece_of(own_one, p, count, v_one, o_one)
        piece = piece_of(own_one, half + p, count, v_one, o_one)
        for j in range(2):
            joint_ref[2 * i + j, :, :width] = piece[j * size : (j + 1) * size]
            joint_ref[2 * i + j, :, width:] = piece_of(own_two, 2 * p + j, count, v_two, o_two)


def widen_pair(own_one, own_two, v_one, o_one, v_two, o_two, group=4):
    half, size, width = v_one.shape
    count = 2 * half
    small, rest = v_two.shape[1:]
    S = jax.ShapeDtypeStruct
    first, joint, _ = launch(
        functools.partial(widen_pair_kernel, group, count), "widen_joint", 5, (half // group,),
        [same(*v_one.shape)] * 2 + [same(*v_two.shape)] * 2,
        [tiled(group, size, width), tiled(2 * group, small, width + rest)],
        [S((half, size, width), f32), S((count, small, width + rest), f32)],
        [], 40, (v_one, o_one, v_two, o_two), (), (own_one, own_two), (0, 1, 2, 3),
    )
    return first.reshape(half * size, width), joint.reshape(count * small, width + rest)


def per_device(
    tokens, cotangent, first_gain, first_shift, joint_weight, query_bias, value_bias, score_weight, out_weight, out_bias,
    second_gain, second_shift, expand_weight, expand_bias, reduce_weight, reduce_bias, picks, quota,
):
    rows, width = tokens.shape[1:]
    heads = score_weight.shape[1]
    inner = expand_weight.shape[1]
    blocks = lax.axis_size("seq")
    slots = blocks * PICK
    here = lax.axis_index("seq").astype(jnp.int32).reshape(1)
    first, second = orders()
    mine = side(*first[0]).astype(jnp.int32).reshape(1)
    inputs, grad_out = tokens[0], cotangent[0]
    live = (jnp.arange(PICK, dtype=jnp.int32)[None, :] < quota[0, 0][:, None]).astype(jnp.int32)
    flat = picks[0, 0].reshape(-1)
    normed, q, k, v, score, rim_sent, sent, _ = project(
        inputs, flat[:, None], live.reshape(-1, 1), first_gain, first_shift, joint_weight, query_bias, value_bias,
        score_weight,
    )
    channels = sent.shape[1]
    rim = passed_along(rim_sent, "seq", 1)
    far = lax.all_to_all(
        sent.reshape(blocks, PICK, channels), "seq", split_axis=0, concat_axis=0, tiled=True
    ).reshape(slots, channels)
    mixed, total, _ = attend(here, q, k, v, score, rim, far, heads)
    resid, hidden, grad_pre, expand_sums, *halves, _ = feed(
        mine, mixed, inputs, grad_out, out_weight, out_bias, second_gain, second_shift, expand_weight, expand_bias,
        reduce_weight,
    )
    reduced, expanded = Chain(*halves[:2], first), Chain(*halves[2:], second)
    one = [reduced, expanded]
    grad_resid, grad_attn, grad_mixed, sums_two, stage = feed_back(
        resid, grad_out, grad_pre, out_weight, second_gain, expand_weight
    )
    stage = advance(one, (stage,))
    dq, dk_own, dv_own, ds_own, rim_grad, far_grad, stage = attend_back(
        here, q, k, v, grad_mixed, total, score, rim, far, heads, (stage,)
    )
    stage = advance(one, (stage,))
    rim_back = passed_along(rim_grad, "seq", -1)
    far_back = lax.all_to_all(
        far_grad.reshape(blocks, PICK, channels), "seq", split_axis=0, concat_axis=0, tiled=True
    ).reshape(slots, channels)
    *halves, stage = pair_outer(mine, mixed, grad_attn, normed, dq, "pair_outer", 6, (stage,))
    paired = Chain(*halves, first)
    stage = advance(one, (stage,))
    dk, dv, ds, *halves, stage = join_keys(mine, dk_own, dv_own, ds_own, rim_back, far_back, flat[None, :], normed, (stage,))
    keyed = Chain(*halves, second)
    two = [paired, keyed]
    stage = advance(one + two, (stage,))
    token_grad, sums_one, score_grad, stage = join_tokens(
        inputs, grad_resid, dq, dk, dv, ds, first_gain, first_shift, joint_weight, score_weight, (stage,)
    )
    small = Total(
        jnp.concatenate([sums_one, sums_two, expand_sums.reshape(inner // width, width), score_grad], axis=0), first
    )
    stage = advance(one + two, (stage,))
    layer_out, stage = finish(resid, hidden, reduce_weight, reduce_bias, (stage,))

    def with_small(chains):
        return chains + ([small] if small.level < len(first) else [])

    while one[0].level > 0 or one[0].down:
        stage = advance(with_small(one + two), (stage,))
    reduce_weight_grad, stage = widen(own_place(first), *ends(reduced), "widen_reduce", (stage,))
    while two[0].level > 1 or two[0].down:
        stage = advance(with_small(two), (stage,))
    expand_weight_grad, stage = widen(own_place(second), *ends(expanded), "widen_expand", (stage,))
    while two[0].level > 0 or two[0].down:
        stage = advance(with_small(two), (stage,))
    out_weight_grad, joint_weight_grad = widen_pair(own_place(first), own_place(second), *ends(paired), *ends(keyed))
    small = small.send
    gain_one, shift_one, query_sum, value_sum, out_sum, gain_two, shift_two, reduce_sum = (small[i] for i in range(8))
    past = 8 + inner // width
    return (
        layer_out[None],
        token_grad[None],
        gain_one,
        shift_one,
        joint_weight_grad,
        query_sum,
        value_sum,
        small[past : past + heads].T,
        out_weight_grad,
        out_sum,
        gain_two,
        shift_two,
        expand_weight_grad,
        small[8:past].reshape(inner),
        reduce_weight_grad,
        reduce_sum,
    )


def solution(mesh):
    placed = (
        P("dp", "seq", None),
        P("dp", "seq", None),
        P(),
        P(),
        P(),
        P(),
        P(),
        P(),
        P(),
        P(),
        P(),
        P(),
        P(),
        P(),
        P(),
        P(),
        P("dp", "seq", None, None),
        P("dp", "seq", None),
    )
    return jax.shard_map(
        per_device,
        mesh=mesh,
        in_specs=placed,
        out_specs=(
            P("dp", "seq", None),
            P("dp", "seq", None),
            P(),
            P(),
            P(),
            P(),
            P(),
            P(),
            P(),
            P(),
            P(),
            P(),
            P(),
            P(),
            P(),
            P(),
        ),
        check_vma=False,
    )
```

time: 1010 us -> 344 us (0.34)
  waiting for transfers between devices: 540 us -> 80.2 us
  Pallas kernels: 0 us -> 188 us
  matrix products: 169 us -> 0 us
  local copies, waits for them, and re-layouts: 161 us -> 10 us
  other arithmetic: 96.4 us -> 3.9 us
  starting transfers between devices: 18.2 us -> 59.9 us
  between operations: 15.2 us -> 0.92 us
    psum x2 -> x0, waiting for transfers between devices: 537 us -> none  [per_device(): lax.psum((first_gain_grad, first_shift_grad, joint_weight_grad, query_bia...]
    pallas_call x0 -> x24, Pallas kernels: none -> 188 us  [launch(): pl.pallas_call(body, grid_spec=pltpu.PrefetchScalarGridSpec(num_scalar_pr...]
    dot_general x27 -> x0, matrix products: 169 us -> none  [the longest x5 39 us: times_transposed(): lax.dot_general(left, right, (((1,), (1,)), ((), ())), preferred_element_...]
    ppermute x0 -> x45, waiting for transfers between devices: none -> 73.8 us  [swap(): return lax.ppermute(value, axis, [(i, i ^ bit) for i in range(count)])]
    unnamed x167 -> x15, local copies, waits for them, and re-layouts: 50.3 us -> 3.63 us
    ppermute x0 -> x45, starting transfers between devices: none -> 46.5 us  [swap(): return lax.ppermute(value, axis, [(i, i ^ bit) for i in range(count)])]
    slice x10 -> x2, local copies, waits for them, and re-layouts: 35.7 us -> 0.66 us  [the longest x1 0.66 us: per_device(): small[i]]
    convert_element_type x7 -> x1, local copies, waits for them, and re-layouts: 29 us -> 0.69 us  [per_device(): (jnp.arange(PICK, dtype=jnp.int32)[None, :] < quota[0, 0][:, None]).astyp...]
  transfers between devices with their start and end apart: 7 -> 49, of which waited for: 3 -> 23; matrix products, arithmetic and copies ran while one was open for 13% -> 2% of each run, Pallas kernels for 0% -> 31%
where the time goes in v1:
time: 344 us; the launch traced here: 343 us
  Pallas kernels  188 us (55%)
  waiting for transfers between devices  80.2 us (23%)
  starting transfers between devices  59.9 us (17%)
  local copies, waits for them, and re-layouts  10 us (3%)
  other arithmetic  3.9 us (1%)
    pallas_call x24, Pallas kernels, launch(): pl.pallas_call(body, grid_spec=pltpu.PrefetchScalarGridSpec(num_scalar_pr...  188 us
    ppermute x45, waiting for transfers between devices, swap(): return lax.ppermute(value, axis, [(i, i ^ bit) for i in range(count)])  73.8 us
    ppermute x45, starting transfers between devices, swap(): return lax.ppermute(value, axis, [(i, i ^ bit) for i in range(count)])  46.5 us
  transfers between devices with their start and end apart: 49, of which 23 were waited for; matrix products, arithmetic and copies ran while one was open for 2% of the time, Pallas kernels for 31%

profile of v1, /device:TPU:0, one launch (start us, length us, event | category | flops | bytes accessed | tf_op | source)
XLA Modules:
  0.0 343.4 jit_solution(17848182517015458891)
XLA Ops:
  5.0 10.8 %project.1 = (bf16[1024,768]{1,0:T(8,128)(2,1)}, bf16[1024,768]{1,0:T(8,128)(2,1)}, bf16[1024,768]{1,0:T(8,128)(2,1)}, bf16[1024,768]{1,0:T(8,128)(2,1)}, bf16[1...) custom-call(bf16[1024,768]{1,0:T(8,128)(2,1)} %bitcast.100, ...), custom_call_target="tpu_custom_call" | custom-call | flops 9200000000 | bytes 1048576 | tf_op jit(solution)/shard_map/project/pallas_call | solution.py:122
  18.2 5.0 %all-to-all-start = ((bf16[8,8,1664]{2,1,0:T(8,128)(2,1)}), bf16[8,8,1664]{2,1,0:T(8,128)(2,1)S(1)}, u32[]{:S(2)}, u32[]{:S(2)}) async-start(bf16[8,8,1664]{2,1,0:T(8,128)(2,1)} %bitcast.94), calls=%async_computation | async-start | bytes 425984 | tf_op jit(solution)/shard_map/all_to_all | solution.py:984
  23.3 6.4 %all-to-all-done = bf16[8,8,1664]{2,1,0:T(8,128)(2,1)S(1)} async-done(((bf16[8,8,1664]{2,1,0:T(8,128)(2,1)}), bf16[8,8,1664]{2,1,0:T(8,128)(2,1)S(1)}, u32[]{:S(2)}, u32[]{:S(2)}) %all-to-all-start) | async-done | bytes 213024 | tf_op jit(solution)/shard_map/all_to_all | solution.py:984
  30.4 13.6 %attend.1 = (bf16[1024,768]{1,0:T(8,128)(2,1)}, f32[3,16,256]{2,1,0:T(8,128)}, f32[8,128]{1,0:T(8,128)}) custom-call(s32[1]{0:T(128)} %bitcast.1.refs_0_, bf16[1024,768]{1,0:T(8,128)(2,1)} %get-tuple-element.134.refs_1_, bf16[1024,768]{1,0:T(8,128)(2,1)} %get-tuple-element.135.refs_2_, bf16[1024,768]{1,0:T(8,128)(2,1)} %get-tuple-element.136.refs_3_, ...), custom_call_target="tpu_custom_call" | custom-call | flops 13799999488 | bytes 1048576 | tf_op jit(solution)/shard_map/attend/pallas_call | solution.py:122
  44.0 37.2 %feed.1 = (f32[1024,768]{1,0:T(8,128)}, bf16[1024,3072]{1,0:T(8,128)(2,1)}, bf16[1024,3072]{1,0:T(8,128)(2,1)}, f32[1,3072]{1,0:T(1,128)}, bf16[1536,768]{1,0:T(...) custom-call(s32[1]{0:T(128)} %bitcast.refs_0_, ...), custom_call_target="tpu_custom_call" | custom-call | flops 32199999488 | bytes 1048576 | tf_op jit(solution)/shard_map/feed/pallas_call | solution.py:122
  82.7 15.7 %feed_back.1 = (f32[1024,768]{1,0:T(8,128)}, bf16[1024,768]{1,0:T(8,128)(2,1)}, bf16[1024,768]{1,0:T(8,128)(2,1)}, f32[4,768]{1,0:T(4,128)}, f32[8,128]{1,0:T(8,128)}) custom-call(f32[1024,768]{1,0:T(8,128)} %get-tuple-element.141.refs_0_, bf16[1024,768]{1,0:T(8,128)(2,1)} %bitcast.99, bf16[1024,3072]{1,0:T(8,128)(2,1)} %get-tuple-element.147.refs_2_, ...), custom_call_target="tpu_custom_call" | custom-call | flops 12650000384 | bytes 1048576 | tf_op jit(solution)/shard_map/feed_back/pallas_call | solution.py:122
  98.4 5.4 %advance.12 = (bf16[8,96,768]{2,1,0:T(8,128)(2,1)}, bf16[8,96,768]{2,1,0:T(8,128)(2,1)S(1)}, bf16[8,24,3072]{2,1,0:T(8,128)(2,1)}, bf16[8,24,3072]{2,1,0:T(8,128)(2,1)S(1)}, f32[8,128]{1,0:T(8,128)}) custom-call(s32[2]{0:T(128)S(1)} %pad_add_fusion.3.refs_0_, bf16[16,96,768]{2,1,0:T(8,128)(2,1)} %bitcast.79, ...), custom_call_target="tpu_custom_call" | custom-call | flops 2300000000 | bytes 1048576 | tf_op jit(solution)/shard_map/advance/pallas_call | solution.py:122
  105.3 30.1 %attend_back.1 = (bf16[1024,768]{1,0:T(8,128)(2,1)}, f32[1024,768]{1,0:T(8,128)}, f32[1024,768]{1,0:T(8,128)}, f32[1024,128]{1,0:T(8,128)}, bf16[64,1664]{1,0:T(...) custom-call(s32[1]{0:T(128)} %bitcast.1.refs_0_, bf16[1024,768]{1,0:T(8,128)(2,1)} %get-tuple-element.134.refs_1_, ...), custom_call_target="tpu_custom_call" | custom-call | flops 32199999488 | bytes 1048576 | tf_op jit(solution)/shard_map/attend_back/pallas_call | solution.py:122
  136.7 4.8 %all-to-all-start.1 = ((bf16[8,8,1664]{2,1,0:T(8,128)(2,1)}), bf16[8,8,1664]{2,1,0:T(8,128)(2,1)}, u32[]{:S(2)}, u32[]{:S(2)}) async-start(bf16[8,8,1664]{2,1,0:T(8,128)(2,1)} %bitcast.93), calls=%async_computation.1 | async-start | bytes 425984 | tf_op jit(solution)/shard_map/all_to_all | solution.py:1003
  148.2 6.9 %pair_outer.1 = (bf16[768,768]{1,0:T(8,128)(2,1)}, bf16[768,768]{1,0:T(8,128)(2,1)}, f32[8,128]{1,0:T(8,128)}) custom-call(s32[1]{0:T(128)} %bitcast.refs_0_, bf16[1024,768]{1,0:T(8,128)(2,1)} %get-tuple-element.140.refs_1_, bf16[1024,768]{1,0:T(8,128)(2,1)} %get-tuple-element.161.refs_2_, bf16[1024,768]{1,0:T(8,128)(2,1)} %get-tuple-element.162.refs_3_.refs_7_, ...), custom_call_target="tpu_custom_call" | custom-call | flops 6899999744 | bytes 1048576 | tf_op jit(solution)/shard_map/pair_outer/pallas_call | solution.py:122
  155.0 5.6 %collective-permute-done.5.refs_2_.refs_4_ = bf16[4,96,768]{2,1,0:T(8,128)(2,1)S(1)} collective-permute-done((bf16[4,96,768]{2,1,0:T(8,128)(2,1)S(1)}, bf16[4,96,768]{2,1,0:T(8,128)(2,1)S(1)}, u32[]{:S(2)}, u32[]{:S(2)}) %collective-permute-start.5) | collective-permute-done | bytes 589856 | tf_op jit(solution)/shard_map/ppermute | solution.py:749
  163.1 10.7 %join_keys.1 = (bf16[1024,768]{1,0:T(8,128)(2,1)}, bf16[1024,768]{1,0:T(8,128)(2,1)}, bf16[1024,128]{1,0:T(8,128)(2,1)}, bf16[384,1536]{1,0:T(8,128)(2,1)}, bf16[384,1536]{1,0:T(8,128)(2,1)}, /*index=5*/f32[8,128]{1,0:T(8,128)}) custom-call(s32[1]{0:T(128)} %bitcast.refs_0_, f32[1024,768]{1,0:T(8,128)} %get-tuple-element.172.refs_1_, ...), custom_call_target="tpu_custom_call" | custom-call | flops 9200000000 | bytes 1048576 | tf_op jit(solution)/shard_map/join_keys/pallas_call | solution.py:122
  192.7 11.4 %join_tokens.1 = (f32[1024,768]{1,0:T(8,128)}, f32[4,768]{1,0:T(4,128)}, f32[12,768]{1,0:T(8,128)}, f32[8,128]{1,0:T(8,128)}) custom-call(bf16[1024,768]{1,0:T(8,128)(2,1)} %bitcast.102, f32[1024,768]{1,0:T(8,128)} %get-tuple-element.189.refs_1_, bf16[1024,768]{1,0:T(8,128)(2,1)} %get-tuple-element.163.refs_4_.refs_2_, ...), custom_call_target="tpu_custom_call" | custom-call | flops 10350000128 | bytes 1048576 | tf_op jit(solution)/shard_map/join_tokens/pallas_call | solution.py:122
  211.5 9.9 %finish.1 = (bf16[1024,768]{1,0:T(8,128)(2,1)}, f32[8,128]{1,0:T(8,128)}) custom-call(f32[1024,768]{1,0:T(8,128)} %get-tuple-element.141.refs_0_, bf16[1024,3072]{1,0:T(8,128)(2,1)} %get-tuple-element.142.refs_1_, bf16[3072,768]{1,0:T(8,128)(2,1)} %refs_2_.1, f32[768]{0:T(1024)} %refs_3_.5, f32[8,128]{1,0:T(8,128)} %get-tuple-element.195.refs_4_), custom_call_target="tpu_custom_call" | custom-call | flops 8049999872 | bytes 1048576 | tf_op jit(solution)/shard_map/finish/pallas_call | solution.py:122
  229.8 10.4 %collective-permute-done.25.refs_14_ = f32[24,768]{1,0:T(8,128)S(1)} collective-permute-done((f32[24,768]{1,0:T(8,128)S(1)}, f32[24,768]{1,0:T(8,128)S(1)}, u32[]{:S(2)}, u32[]{:S(2)}) %collective-permute-start.25) | collective-permute-done | bytes 73760 | tf_op jit(solution)/shard_map/ppermute | solution.py:749
  246.7 8.6 %collective-permute-done.28.refs_6_ = bf16[1,48,768]{2,1,0:T(8,128)(2,1)S(1)} collective-permute-done((bf16[1,48,768]{2,1,0:T(8,128)(2,1)S(1)}, bf16[1,48,768]{2,1,0:T(8,128)(2,1)S(1)}, u32[]{:S(2)}, u32[]{:S(2)}) %collective-permute-start.28) | collective-permute-done | bytes 73760 | tf_op jit(solution)/shard_map/ppermute | solution.py:749
  269.1 15.3 %collective-permute-done.31.refs_2_ = bf16[8,96,768]{2,1,0:T(8,128)(2,1)S(1)} collective-permute-done((bf16[8,96,768]{2,1,0:T(8,128)(2,1)S(1)}, bf16[8,96,768]{2,1,0:T(8,128)(2,1)S(1)}, u32[]{:S(2)}, u32[]{:S(2)}) %collective-permute-start.31) | collective-permute-done | bytes 1179680 | tf_op jit(solution)/shard_map/ppermute | solution.py:749
  291.2 3.3 collective-permute-done.39.refs_2_
  294.5 7.1 %widen_reduce.1 = (f32[32,96,768]{2,1,0:T(8,128)}, f32[8,128]{1,0:T(8,128)}) custom-call(s32[1]{0:T(128)} %bitcast.31.refs_0_, bf16[16,96,768]{2,1,0:T(8,128)(2,1)} %bitcast.32.refs_1_, bf16[16,96,768]{2,1,0:T(8,128)(2,1)} %collective-permute-done.39.refs_2_, f32[8,128]{1,0:T(8,128)} %get-tuple-element.235.refs_3_), custom_call_target="tpu_custom_call" | custom-call | flops 5750000128 | bytes 1048576 | tf_op jit(solution)/shard_map/widen_reduce/pallas_call | solution.py:122
  304.8 6.7 %collective-permute-done.40.refs_2_ = bf16[4,48,768]{2,1,0:T(8,128)(2,1)S(1)} collective-permute-done((bf16[4,48,768]{2,1,0:T(8,128)(2,1)S(1)}, bf16[4,48,768]{2,1,0:T(8,128)(2,1)S(1)}, u32[]{:S(2)}, u32[]{:S(2)}) %collective-permute-start.40) | collective-permute-done | bytes 294944 | tf_op jit(solution)/shard_map/ppermute | solution.py:749
  316.2 6.4 %widen_expand.1 = (f32[32,24,3072]{2,1,0:T(8,128)}, f32[8,128]{1,0:T(8,128)}) custom-call(s32[1]{0:T(128)} %bitcast.33.refs_0_.refs_1_, bf16[16,24,3072]{2,1,0:T(8,128)(2,1)S(1)} %bitcast.52, bf16[16,24,3072]{2,1,0:T(8,128)(2,1)} %collective-permute-done.44.refs_2_, f32[8,128]{1,0:T(8,128)} %get-tuple-element.244.refs_3_), custom_call_target="tpu_custom_call" | custom-call | flops 5750000128 | bytes 1048576 | tf_op jit(solution)/shard_map/widen_expand/pallas_call | solution.py:122
  322.7 5.9 %collective-permute-done.42.refs_2_ = bf16[8,48,768]{2,1,0:T(8,128)(2,1)} collective-permute-done((bf16[8,48,768]{2,1,0:T(8,128)(2,1)S(1)}, bf16[8,48,768]{2,1,0:T(8,128)(2,1)}, u32[]{:S(2)}, u32[]{:S(2)}) %collective-permute-start.42) | collective-permute-done | bytes 589856 | tf_op jit(solution)/shard_map/ppermute | solution.py:749
  330.2 3.1 advance.23
  337.9 5.5 %widen_joint.1 = (f32[16,48,768]{2,1,0:T(8,128)}, f32[32,24,2304]{2,1,0:T(8,128)}, f32[8,128]{1,0:T(8,128)}) custom-call(s32[1]{0:T(128)} %bitcast.31.refs_0_, s32[1]{0:T(128)} %bitcast.33.refs_0_.refs_1_, bf16[16,48,768]{2,1,0:T(8,128)(2,1)S(1)} %bitcast.58, bf16[16,48,768]{2,1,0:T(8,128)(2,1)} %collective-permute-done.45.refs_3_, ...), custom_call_target="tpu_custom_call" | custom-call | flops 5750000128 | bytes 1048576 | tf_op jit(solution)/shard_map/widen_joint/pallas_call | solution.py:122
  (130 shorter events, 96.6 us)
Async XLA Ops:
  81.3 17.1 %collective-permute-start.1 = (bf16[16,96,768]{2,1,0:T(8,128)(2,1)}, bf16[16,96,768]{2,1,0:T(8,128)(2,1)S(1)}, u32[]{:S(2)}, u32[]{:S(2)}) collective-permute-start(bf16[16,96,768]{2,1,0:T(8,128)(2,1)} %bitcast.97), channel_id=1, source_target_pairs={{0,1},{1,0},{2,3},{3,2},{4,5},{5,4},{6,7},{7,6},{8,9},{9,8},{10,11... | collective-permute-start | bytes 7077896 | tf_op jit(solution)/shard_map/ppermute | solution.py:749
  81.3 17.0 %collective-permute-start.2 = (bf16[16,24,3072]{2,1,0:T(8,128)(2,1)}, bf16[16,24,3072]{2,1,0:T(8,128)(2,1)}, u32[]{:S(2)}, u32[]{:S(2)}) collective-permute-start(bf16[16,24,3072]{2,1,0:T(8,128)(2,1)} %bitcast.96), channel_id=1, source_target_pairs={{0,1},{1,0},{2,3},{3,2},{4,5},{5,4},{6,7},{7,6},{8,9},{9,8},{10,11... | collective-permute-start | bytes 7077896 | tf_op jit(solution)/shard_map/ppermute | solution.py:749
  103.8 37.7 %collective-permute-start.3 = (bf16[8,96,768]{2,1,0:T(8,128)(2,1)}, bf16[8,96,768]{2,1,0:T(8,128)(2,1)S(1)}, u32[]{:S(2)}, u32[]{:S(2)}) collective-permute-start(bf16[8,96,768]{2,1,0:T(8,128)(2,1)} %get-tuple-element.150), channel_id=1, source_target_pairs={{0,2},{1,3},{2,0},{3,1},{4,6},{5,7},{6,4},{7,5},{8,10},{9,11},{10,... | collective-permute-start | bytes 3538952 | tf_op jit(solution)/shard_map/ppermute | solution.py:749
  104.4 37.1 %collective-permute-start.4 = (bf16[8,24,3072]{2,1,0:T(8,128)(2,1)}, bf16[8,24,3072]{2,1,0:T(8,128)(2,1)S(1)}, u32[]{:S(2)}, u32[]{:S(2)}) collective-permute-start(bf16[8,24,3072]{2,1,0:T(8,128)(2,1)} %get-tuple-element.152), channel_id=1, source_target_pairs={{0,4},{1,5},{2,6},{3,7},{4,0},{5,1},{6,2},{7,3},{8,12},{9,13},{10,... | collective-permute-start | bytes 3538952 | tf_op jit(solution)/shard_map/ppermute | solution.py:749
  135.4 27.7 %collective-permute-start.10 = (bf16[64,1664]{1,0:T(8,128)(2,1)}, bf16[64,1664]{1,0:T(8,128)(2,1)}, u32[]{:S(2)}, u32[]{:S(2)}) collective-permute-start(bf16[64,1664]{1,0:T(8,128)(2,1)} %get-tuple-element.175), channel_id=1, source_target_pairs={{1,0},{2,1},{3,2},{4,3},{5,4},{6,5},{7,6},{9,8},{10,9},{11,10},{12... | collective-permute-start | bytes 638984 | tf_op jit(solution)/shard_map/ppermute | solution.py:142
  136.7 26.4 %all-to-all-start.1 = ((bf16[8,8,1664]{2,1,0:T(8,128)(2,1)}), bf16[8,8,1664]{2,1,0:T(8,128)(2,1)}, u32[]{:S(2)}, u32[]{:S(2)}) async-start(bf16[8,8,1664]{2,1,0:T(8,128)(2,1)} %bitcast.93), calls=%async_computation.1 | async-start | bytes 425984 | tf_op jit(solution)/shard_map/all_to_all | solution.py:1003
  144.4 16.2 %collective-permute-start.5 = (bf16[4,96,768]{2,1,0:T(8,128)(2,1)S(1)}, bf16[4,96,768]{2,1,0:T(8,128)(2,1)S(1)}, u32[]{:S(2)}, u32[]{:S(2)}) collective-permute-start(bf16[4,96,768]{2,1,0:T(8,128)(2,1)S(1)} %get-tuple-element.158), channel_id=1, source_target_pairs={{0,4},{1,5},{2,6},{3,7},{4,0},{5,1},{6,2},{7,3},{8,12},{9,13},{10,... | collective-permute-start | bytes 1769480 | tf_op jit(solution)/shard_map/ppermute | solution.py:749
  146.6 15.0 %collective-permute-start.6 = (bf16[4,24,3072]{2,1,0:T(8,128)(2,1)S(1)}, bf16[4,24,3072]{2,1,0:T(8,128)(2,1)S(1)}, u32[]{:S(2)}, u32[]{:S(2)}) collective-permute-start(bf16[4,24,3072]{2,1,0:T(8,128)(2,1)S(1)} %get-tuple-element.160), channel_id=1, source_target_pairs={{0,8},{8,0},{16,24},{24,16},{1,9},{9,1},{17,25},{25,17},{2,10},{10... | collective-permute-start | bytes 1769480 | tf_op jit(solution)/shard_map/ppermute | solution.py:749
  155.0 29.8 %collective-permute-start.9 = (bf16[16,48,768]{2,1,0:T(8,128)(2,1)}, bf16[16,48,768]{2,1,0:T(8,128)(2,1)S(1)}, u32[]{:S(2)}, u32[]{:S(2)}) collective-permute-start(bf16[16,48,768]{2,1,0:T(8,128)(2,1)} %bitcast.103), channel_id=1, source_target_pairs={{0,1},{1,0},{2,3},{3,2},{4,5},{5,4},{6,7},{7,6},{8,9},{9,8},{10,11... | collective-permute-start | bytes 3538952 | tf_op jit(solution)/shard_map/ppermute | solution.py:749
  187.6 17.4 %collective-permute-start.14 = (bf16[8,48,768]{2,1,0:T(8,128)(2,1)S(1)}, bf16[8,48,768]{2,1,0:T(8,128)(2,1)S(1)}, u32[]{:S(2)}, u32[]{:S(2)}) collective-permute-start(bf16[8,48,768]{2,1,0:T(8,128)(2,1)S(1)} %get-tuple-element.186), channel_id=1, source_target_pairs={{0,2},{1,3},{2,0},{3,1},{4,6},{5,7},{6,4},{7,5},{8,10},{9,11},{10,... | collective-permute-start | bytes 1769480 | tf_op jit(solution)/shard_map/ppermute | solution.py:749
  189.4 15.6 %collective-permute-start.15 = (bf16[8,24,1536]{2,1,0:T(8,128)(2,1)S(1)}, bf16[8,24,1536]{2,1,0:T(8,128)(2,1)S(1)}, u32[]{:S(2)}, u32[]{:S(2)}) collective-permute-start(bf16[8,24,1536]{2,1,0:T(8,128)(2,1)S(1)} %get-tuple-element.188), channel_id=1, source_target_pairs={{0,4},{1,5},{2,6},{3,7},{4,0},{5,1},{6,2},{7,3},{8,12},{9,13},{10,... | collective-permute-start | bytes 1769480 | tf_op jit(solution)/shard_map/ppermute | solution.py:749
  189.7 15.3 %collective-permute-start.12 = (bf16[1,96,768]{2,1,0:T(8,128)(2,1)S(1)}, bf16[1,96,768]{2,1,0:T(8,128)(2,1)S(1)}, u32[]{:S(2)}, u32[]{:S(2)}) collective-permute-start(bf16[1,96,768]{2,1,0:T(8,128)(2,1)S(1)} %get-tuple-element.182), channel_id=1, source_target_pairs={{0,16},{8,24},{16,0},{24,8},{1,17},{9,25},{17,1},{25,9},{2,18},{10... | collective-permute-start | bytes 442376 | tf_op jit(solution)/shard_map/ppermute | solution.py:749
  204.9 16.5 %collective-permute-start.20 = (f32[24,768]{1,0:T(8,128)S(1)}, f32[24,768]{1,0:T(8,128)S(1)}, u32[]{:S(2)}, u32[]{:S(2)}) collective-permute-start(f32[24,768]{1,0:T(8,128)S(1)} %pad_maximum_fusion.refs_13_), channel_id=1, source_target_pairs={{0,1},{1,0},{2,3},{3,2},{4,5},{5,4},{6,7},{7,6},{8,9},{9,8},{10,11... | collective-permute-start | bytes 221192 | tf_op jit(solution)/shard_map/ppermute | solution.py:749
  206.4 15.2 %collective-permute-start.18 = (bf16[4,48,768]{2,1,0:T(8,128)(2,1)S(1)}, bf16[4,48,768]{2,1,0:T(8,128)(2,1)S(1)}, u32[]{:S(2)}, u32[]{:S(2)}) collective-permute-start(bf16[4,48,768]{2,1,0:T(8,128)(2,1)S(1)} %get-tuple-element.201), channel_id=1, source_target_pairs={{0,4},{1,5},{2,6},{3,7},{4,0},{5,1},{6,2},{7,3},{8,12},{9,13},{10,... | collective-permute-start | bytes 884744 | tf_op jit(solution)/shard_map/ppermute | solution.py:749
  208.1 15.4 %collective-permute-start.19 = (bf16[4,24,1536]{2,1,0:T(8,128)(2,1)S(1)}, bf16[4,24,1536]{2,1,0:T(8,128)(2,1)S(1)}, u32[]{:S(2)}, u32[]{:S(2)}) collective-permute-start(bf16[4,24,1536]{2,1,0:T(8,128)(2,1)S(1)} %get-tuple-element.203), channel_id=1, source_target_pairs={{0,8},{8,0},{16,24},{24,16},{1,9},{9,1},{17,25},{25,17},{2,10},{10... | collective-permute-start | bytes 884744 | tf_op jit(solution)/shard_map/ppermute | solution.py:749
  224.8 15.4 %collective-permute-start.21 = (bf16[2,96,768]{2,1,0:T(8,128)(2,1)S(1)}, bf16[2,96,768]{2,1,0:T(8,128)(2,1)S(1)}, u32[]{:S(2)}, u32[]{:S(2)}) collective-permute-start(bf16[2,96,768]{2,1,0:T(8,128)(2,1)S(1)} %bitcast.67), channel_id=1, source_target_pairs={{0,8},{8,0},{16,24},{24,16},{1,9},{9,1},{17,25},{25,17},{2,10},{10... | collective-permute-start | bytes 884744 | tf_op jit(solution)/shard_map/ppermute | solution.py:749
  241.4 15.0 %collective-permute-start.26 = (bf16[4,96,768]{2,1,0:T(8,128)(2,1)S(1)}, bf16[4,96,768]{2,1,0:T(8,128)(2,1)S(1)}, u32[]{:S(2)}, u32[]{:S(2)}) collective-permute-start(bf16[4,96,768]{2,1,0:T(8,128)(2,1)S(1)} %bitcast.61), channel_id=1, source_target_pairs={{0,4},{1,5},{2,6},{3,7},{4,0},{5,1},{6,2},{7,3},{8,12},{9,13},{10,... | collective-permute-start | bytes 1769480 | tf_op jit(solution)/shard_map/ppermute | solution.py:749
  241.7 16.3 %collective-permute-start.27 = (bf16[4,24,3072]{2,1,0:T(8,128)(2,1)S(1)}, bf16[4,24,3072]{2,1,0:T(8,128)(2,1)S(1)}, u32[]{:S(2)}, u32[]{:S(2)}) collective-permute-start(bf16[4,24,3072]{2,1,0:T(8,128)(2,1)S(1)} %bitcast.63), channel_id=1, source_target_pairs={{0,8},{8,0},{16,24},{24,16},{1,9},{9,1},{17,25},{25,17},{2,10},{10... | collective-permute-start | bytes 1769480 | tf_op jit(solution)/shard_map/ppermute | solution.py:749
  258.8 25.6 %collective-permute-start.31 = (bf16[8,96,768]{2,1,0:T(8,128)(2,1)S(1)}, bf16[8,96,768]{2,1,0:T(8,128)(2,1)S(1)}, u32[]{:S(2)}, u32[]{:S(2)}) collective-permute-start(bf16[8,96,768]{2,1,0:T(8,128)(2,1)S(1)} %bitcast.53), channel_id=1, source_target_pairs={{0,2},{1,3},{2,0},{3,1},{4,6},{5,7},{6,4},{7,5},{8,10},{9,11},{10,... | collective-permute-start | bytes 3538952 | tf_op jit(solution)/shard_map/ppermute | solution.py:749
  259.2 25.3 %collective-permute-start.32 = (bf16[8,24,3072]{2,1,0:T(8,128)(2,1)S(1)}, bf16[8,24,3072]{2,1,0:T(8,128)(2,1)S(1)}, u32[]{:S(2)}, u32[]{:S(2)}) collective-permute-start(bf16[8,24,3072]{2,1,0:T(8,128)(2,1)S(1)} %bitcast.55), channel_id=1, source_target_pairs={{0,4},{1,5},{2,6},{3,7},{4,0},{5,1},{6,2},{7,3},{8,12},{9,13},{10,... | collective-permute-start | bytes 3538952 | tf_op jit(solution)/shard_map/ppermute | solution.py:749
  286.3 29.9 %collective-permute-start.44 = (bf16[16,24,3072]{2,1,0:T(8,128)(2,1)S(1)}, bf16[16,24,3072]{2,1,0:T(8,128)(2,1)}, u32[]{:S(2)}, u32[]{:S(2)}) collective-permute-start(bf16[16,24,3072]{2,1,0:T(8,128)(2,1)S(1)} %bitcast.51), channel_id=1, source_target_pairs={{0,1},{1,0},{2,3},{3,2},{4,5},{5,4},{6,7},{7,6},{8,9},{9,8},{10,11... | collective-permute-start | bytes 7077896 | tf_op jit(solution)/shard_map/ppermute | solution.py:749
  286.8 14.8 %collective-permute-start.36 = (bf16[2,48,768]{2,1,0:T(8,128)(2,1)S(1)}, bf16[2,48,768]{2,1,0:T(8,128)(2,1)S(1)}, u32[]{:S(2)}, u32[]{:S(2)}) collective-permute-start(bf16[2,48,768]{2,1,0:T(8,128)(2,1)S(1)} %bitcast.75), channel_id=1, source_target_pairs={{0,8},{8,0},{16,24},{24,16},{1,9},{9,1},{17,25},{25,17},{2,10},{10... | collective-permute-start | bytes 442376 | tf_op jit(solution)/shard_map/ppermute | solution.py:749
  314.2 14.3 %collective-permute-start.42 = (bf16[8,48,768]{2,1,0:T(8,128)(2,1)S(1)}, bf16[8,48,768]{2,1,0:T(8,128)(2,1)}, u32[]{:S(2)}, u32[]{:S(2)}) collective-permute-start(bf16[8,48,768]{2,1,0:T(8,128)(2,1)S(1)} %bitcast.65), channel_id=1, source_target_pairs={{0,2},{1,3},{2,0},{3,1},{4,6},{5,7},{6,4},{7,5},{8,10},{9,11},{10,... | collective-permute-start | bytes 1769480 | tf_op jit(solution)/shard_map/ppermute | solution.py:749
  315.9 14.3 %collective-permute-start.43 = (bf16[8,24,1536]{2,1,0:T(8,128)(2,1)}, bf16[8,24,1536]{2,1,0:T(8,128)(2,1)}, u32[]{:S(2)}, u32[]{:S(2)}) collective-permute-start(bf16[8,24,1536]{2,1,0:T(8,128)(2,1)} %bitcast.37.refs_3_), channel_id=1, source_target_pairs={{0,4},{1,5},{2,6},{3,7},{4,0},{5,1},{6,2},{7,3},{8,12},{9,13},{10,... | collective-permute-start | bytes 1769480 | tf_op jit(solution)/shard_map/ppermute | solution.py:749
  (32 other events, 348.7 us)

commit v2 on v1

v2 whole, which is shorter than its diff:
```python
import functools
import math

import jax
import jax.numpy as jnp
from jax import lax
from jax.experimental import pallas as pl
from jax.experimental.pallas import tpu as pltpu
from jax.sharding import PartitionSpec as P

WIN = 64
PICK = 8
LANES = 128
PACK = 4
DIGIT = 32
TOKEN = (8, 128)
epsilon = 1e-05
very_low = -1e30
bf16 = jnp.bfloat16
f32 = jnp.float32


def nt(left, right):
    return lax.dot_general(left, right, (((1,), (1,)), ((), ())), preferred_element_type=f32)


def tn(left, right):
    return lax.dot_general(left, right, (((0,), (0,)), ((), ())), preferred_element_type=f32)


def nn(left, right):
    return jnp.dot(left, right, preferred_element_type=f32)


def three_parts(value):
    high = value.astype(bf16)
    rest = value - high.astype(f32)
    middle = rest.astype(bf16)
    low = (rest - middle.astype(f32)).astype(bf16)
    return high, middle, low


def head_spread(group, head_size, width):
    row = lax.broadcasted_iota(jnp.int32, (LANES, width), 0)
    lane = lax.broadcasted_iota(jnp.int32, (LANES, width), 1)
    return jnp.where(row == group * PACK + lane // WIN, 1.0, 0.0).astype(bf16)


def stack_heads(tile, head_size, factor):
    width = tile.shape[1]
    lane = lax.broadcasted_iota(jnp.int32, tile.shape, 1) // head_size
    scaled = tile * jnp.asarray(factor, tile.dtype)
    zero = jnp.zeros_like(scaled)
    return jnp.concatenate([jnp.where(lane == h, scaled, zero) for h in range(PACK)], axis=0)


def pick_heads(full, head_size):
    lane = lax.broadcasted_iota(jnp.int32, (WIN, full.shape[1]), 1) // head_size
    out = full[0:WIN]
    for h in range(1, PACK):
        out = jnp.where(lane == h, full[h * WIN : (h + 1) * WIN], out)
    return out


def gates_into(gate_ref, group, place, score_ref, rim_score_ref, far_score_ref, head_size, rows, slots):
    width = PACK * WIN
    spread = head_spread(group, head_size, width)

    def expand(score):
        gate = jax.nn.log_sigmoid(score.astype(f32))
        return sum(nn(part, spread) for part in three_parts(gate))

    gate_ref[0:WIN, :] = jnp.where(place == 0, very_low, expand(rim_score_ref[...]))
    gate_ref[WIN : WIN + rows, :] = expand(score_ref[...])
    gate_ref[WIN + rows :, :] = expand(far_score_ref[...])


def near_bias(width):
    key = lax.broadcasted_iota(jnp.int32, (2 * WIN, width), 0)
    query = lax.broadcasted_iota(jnp.int32, (2 * WIN, width), 1) % WIN
    return (key <= query + WIN) & (key > query)


def tile_logits(i, keys_cat, query_stack, gate_ref, far_pos, place, rows, near_ok):
    width = PACK * WIN
    raw = nt(keys_cat, query_stack)
    gate_near = gate_ref[pl.ds(pl.multiple_of(i * WIN, WIN), 2 * WIN), :]
    gate_far = gate_ref[WIN + rows :, :]
    slots = gate_far.shape[0]
    near = jnp.where(near_ok, raw[: 2 * WIN] + gate_near, very_low)
    lane = lax.broadcasted_iota(jnp.int32, (slots, LANES), 1) % WIN
    far_ok = far_pos <= lane + (place * rows + i * WIN - WIN)
    far_raw = raw[2 * WIN :] + gate_far
    far = jnp.concatenate(
        [
            jnp.where(far_ok, far_raw[:, c * LANES : (c + 1) * LANES], very_low)
            for c in range(width // LANES)
        ],
        axis=1,
    )
    return jnp.concatenate([near, far], axis=0)


def launch(kernel, name, work, grid, in_specs, out_specs, out_shape, scratch, limit, operands, after=(), prefetch=(),
           free=(), aliases=None):
    count, extra = len(operands), len(after)

    def body(*refs):
        lead = len(prefetch)
        rest = refs[lead + count + extra :]
        rest[len(shapes)][...] = jnp.zeros(TOKEN, f32)
        kernel(*refs[: lead + count], *rest[: len(shapes)], *rest[len(shapes) + 1 :])

    def place(at, value, spec):
        if spec.memory_space == pltpu.SMEM or at in free:
            return value
        return pltpu.with_memory_space_constraint(value, pltpu.HBM)

    operands = [place(at, value, spec) for at, (value, spec) in enumerate(zip(operands, in_specs))]
    after = [pltpu.with_memory_space_constraint(value, pltpu.HBM) for value in after]
    shapes, kept = out_shape, len(free) > 0 and name == "advance"
    out = pl.pallas_call(
        body,
        grid_spec=pltpu.PrefetchScalarGridSpec(
            num_scalar_prefetch=len(prefetch),
            grid=grid,
            in_specs=list(in_specs) + [pl.BlockSpec(memory_space=pl.ANY)] * extra,
            out_specs=list(out_specs) + [same(*TOKEN)],
            scratch_shapes=scratch,
        ),
        out_shape=[shape if kept else pltpu.HBM(shape.shape, shape.dtype) for shape in shapes] + [pltpu.HBM(TOKEN, f32)],
        compiler_params=pltpu.CompilerParams(vmem_limit_bytes=limit * 2**20),
        cost_estimate=pl.CostEstimate(flops=int(work * 5e9), bytes_accessed=2**20, transcendentals=0),
        input_output_aliases=aliases or {},
        name=name,
    )(*prefetch, *operands, *after)
    return list(out)


def passed_along(value, axis, steps):
    count = lax.axis_size(axis)
    leading, last = (max(0, -steps), min(count, count - steps))
    return lax.ppermute(value, axis, [(source, source + steps) for source in range(leading, last)])


def normalise(values):
    average = jnp.mean(values, axis=-1, keepdims=True)
    centred = values - average
    variance = jnp.mean(centred * centred, axis=-1, keepdims=True)
    inverse = lax.rsqrt(variance + epsilon)
    return (centred * inverse, inverse)


def normalise_back(grad_out, unit, inverse, gain):
    grad_unit = grad_out * gain
    mean_grad = jnp.mean(grad_unit, axis=-1, keepdims=True)
    mean_cross = jnp.mean(grad_unit * unit, axis=-1, keepdims=True)
    return (grad_unit - mean_grad - unit * mean_cross) * inverse


def row(ref):
    return ref[...].reshape(1, -1)


def column_sums(values):
    return jnp.sum(values, axis=0, keepdims=True)


def accumulate(ref, update):
    step = pl.program_id(0)

    @pl.when(step == 0)
    def _():
        ref[...] = update

    @pl.when(step > 0)
    def _():
        ref[...] += update


def same(*shape):
    return pl.BlockSpec(shape, lambda *_: (0,) * len(shape))


class Moves:
    def __init__(self, sems):
        self.sems, self.made = sems, []

    def add(self, source, target):
        self.made.append((source, target, self.sems.at[len(self.made)]))
        return len(self.made) - 1

    def start(self, *which):
        for at in which:
            pltpu.make_async_copy(*self.made[at]).start()

    def wait(self, *which):
        for at in which:
            pltpu.make_async_copy(*self.made[at]).wait()


def rows_at(index, size):
    return pl.ds(pl.multiple_of(index * size, size), size)


def vmem():
    return pl.BlockSpec(memory_space=pltpu.VMEM)


def anywhere():
    return pl.BlockSpec(memory_space=pl.ANY)


def spread_slots(grid):
    blocks = grid.shape[0]
    slots = blocks * PICK
    wide = jnp.concatenate([jnp.broadcast_to(grid[s : s + 1, :], (PICK, grid.shape[1])) for s in range(blocks)], axis=0)
    lane = lax.broadcasted_iota(jnp.int32, wide.shape, 1)
    turn = lax.broadcasted_iota(jnp.int32, wide.shape, 0) % PICK
    return jnp.sum(jnp.where(lane == turn, wide, 0.0), axis=1, keepdims=True)


def project_kernel(
    steps, tokens_ref, picks_ref, quota_ref, gain_ref, shift_ref, joint_ref, query_bias_ref, value_bias_ref,
    score_weight_ref, normed_ref, q_ref, k_ref, v_ref, score_ref, rim_ref, sent_ref, gathered,
):
    step = pl.program_id(0)
    tile, width = tokens_ref.shape
    unit, _ = normalise(tokens_ref[...].astype(f32))
    normed = (unit * row(gain_ref) + row(shift_ref)).astype(bf16)
    normed_ref[...] = normed
    q_ref[...] = (nn(normed, joint_ref[:, :width]) + row(query_bias_ref)).astype(bf16)
    keys = nn(normed, joint_ref[:, width : 2 * width]).astype(bf16)
    values = (nn(normed, joint_ref[:, 2 * width :]) + row(value_bias_ref)).astype(bf16)
    score = nt(normed, score_weight_ref[...]).astype(bf16)
    heads = score.shape[1]
    k_ref[...] = keys
    v_ref[...] = values
    score_ref[...] = jnp.zeros_like(score_ref)
    score_ref[:, :heads] = score
    picks = spread_slots(picks_ref[...].astype(f32))
    slots = picks.shape[0]
    row_of = lax.broadcasted_iota(jnp.int32, (slots, tile), 1) + step * tile
    chosen = jnp.where(picks == row_of.astype(f32), 1.0, 0.0).astype(bf16)
    parts = ((0, keys), (width, values), (2 * width, normed), (3 * width, score_ref[...]))

    @pl.when(step == 0)
    def _():
        gathered[...] = jnp.zeros_like(gathered)

    for start, part in parts:
        gathered[:, start : start + part.shape[1]] += nn(chosen, part)

    @pl.when(step == steps - 1)
    def _():
        for start, part in parts:
            rim_ref[:, start : start + part.shape[1]] = part[tile - WIN :]
        sent_ref[...] = gathered[...].astype(bf16)
        lane = lax.broadcasted_iota(jnp.int32, (slots, LANES), 1)
        blocks = slots // PICK
        quota = jnp.broadcast_to(quota_ref[...].astype(f32), (slots, blocks))
        block_of = lax.broadcasted_iota(jnp.int32, (slots, blocks), 0) // PICK
        taken = jnp.where(lax.broadcasted_iota(jnp.int32, (slots, blocks), 1) == block_of, quota, 0.0)
        taken = jnp.sum(taken, axis=1, keepdims=True)
        turn = (lax.broadcasted_iota(jnp.int32, (slots, 1), 0) % PICK).astype(f32)
        live = jnp.where(turn < taken, 1.0, 0.0)
        high = jnp.floor(picks * (1.0 / DIGIT))
        coded = jnp.where(lane == heads, high, jnp.where(lane == heads + 1, picks - high * DIGIT, live))
        sent_ref[:, 3 * width :] = jnp.where(
            (lane >= heads) & (lane < heads + 3), coded, gathered[:, 3 * width :]
        ).astype(bf16)


def tiled(*shape):
    return pl.BlockSpec(shape, lambda r, *_: (r,) + (0,) * (len(shape) - 1))


def project(tokens, picks, quota, gain, shift, joint, query_bias, value_bias, score_weight, tile=256):
    rows, width = tokens.shape
    slots = picks.shape[0] * picks.shape[1]
    channels = 3 * width + LANES
    steps = rows // tile
    S = jax.ShapeDtypeStruct
    return launch(
        functools.partial(project_kernel, steps),
        "project", 10, (steps,),
        [
            tiled(tile, width), same(*picks.shape), same(*quota.shape), same(width), same(width), same(*joint.shape),
            same(width), same(width), same(*score_weight.shape),
        ],
        [tiled(tile, width)] * 4 + [tiled(tile, LANES), same(WIN, channels), same(slots, channels)],
        [S((rows, width), bf16)] * 4 + [S((rows, LANES), bf16), S((WIN, channels), bf16), S((slots, channels), bf16)],
        [pltpu.VMEM((slots, channels), f32)], 24,
        (tokens, picks, quota, gain, shift, joint, query_bias, value_bias, score_weight),
    )


def far_positions(far_score, heads, place_rows, blocks):
    wide = far_score.astype(f32)
    slot = lax.broadcasted_iota(jnp.int32, (far_score.shape[0], 1), 0)
    at = (wide[:, heads : heads + 1] * DIGIT + wide[:, heads + 1 : heads + 2]).astype(jnp.int32)
    return jnp.where(
        wide[:, heads + 2 : heads + 3] > 0.5, (slot // PICK) * place_rows + at, 2 * place_rows * blocks
    )


def load_block(group, place_ref, k_ref, v_ref, score_ref, rim_refs, far_refs, keys, values, gate_ref, head_size):
    rows, width = k_ref.shape
    rim_k_ref, rim_v_ref, rim_score_ref = rim_refs
    far_score_ref = far_refs[2]
    slots = far_score_ref.shape[0]
    keys[0:WIN, :] = rim_k_ref[...]
    keys[WIN:, :] = k_ref[...]
    values[0:WIN, :] = rim_v_ref[...]
    values[WIN:, :] = v_ref[...]
    gates_into(gate_ref, group, place_ref[0], score_ref, rim_score_ref, far_score_ref, head_size, rows, slots)


def attend_kernel(
    heads, head_size, unroll, place_ref, q_ref, k_ref, v_ref, score_ref,
    rim_k_ref, rim_v_ref, rim_score_ref, far_k_ref, far_v_ref, far_score_ref,
    mixed_ref, total_ref, keys, values, gate_ref,
):
    group = pl.program_id(0)
    place = place_ref[0]
    rows, width = q_ref.shape
    slots = far_k_ref.shape[0]
    load_block(
        group, place_ref, k_ref, v_ref, score_ref, (rim_k_ref, rim_v_ref, rim_score_ref),
        (far_k_ref, far_v_ref, far_score_ref), keys, values, gate_ref, head_size,
    )
    near_ok = near_bias(width)
    far_pos = jnp.broadcast_to(far_positions(far_score_ref[...], heads, rows, slots // PICK), (slots, LANES))

    @pl.loop(0, rows // WIN, unroll=unroll)
    def _(i):
        at = pl.ds(pl.multiple_of(i * WIN, WIN), WIN)
        span = pl.ds(pl.multiple_of(i * WIN, WIN), 2 * WIN)
        keys_cat = jnp.concatenate([keys[span, :], far_k_ref[...]], axis=0)
        values_cat = jnp.concatenate([values[span, :], far_v_ref[...]], axis=0)
        stack = stack_heads(q_ref[at, :], head_size, 1.0 / math.sqrt(head_size))
        logit = tile_logits(i, keys_cat, stack, gate_ref, far_pos, place, rows, near_ok)
        top = jnp.max(logit, axis=0, keepdims=True)
        power = jnp.exp(logit - top)
        total = jnp.sum(power, axis=0, keepdims=True)
        prob = (power * (1.0 / total)).astype(bf16)
        total_ref[0, pl.ds(i, 1), :] = top + jnp.log(total)
        mixed_ref[at, :] = pick_heads(tn(prob, values_cat), head_size).astype(bf16)


def far_specs(slots, width, groups):
    return [
        pl.BlockSpec((slots, width), lambda g: (0, g)),
        pl.BlockSpec((slots, width), lambda g: (0, groups + g)),
        pl.BlockSpec((slots, LANES), lambda g: (0, 3 * groups * width // LANES)),
    ]


def attend(place, q, k, v, score, rim, far, heads, unroll=8):
    rows, model = q.shape
    slots = far.shape[0]
    width = PACK * WIN
    groups = model // width
    cols = pl.BlockSpec((rows, width), lambda g: (0, g))
    return launch(
        functools.partial(attend_kernel, heads, WIN, unroll),
        "attend", 12, (groups,),
        [pl.BlockSpec(memory_space=pltpu.SMEM), cols, cols, cols, pl.BlockSpec((rows, LANES), lambda g: (0, 0))]
        + far_specs(WIN, width, groups) + far_specs(slots, width, groups),
        [cols, pl.BlockSpec((1, rows // WIN, width), lambda g: (g, 0, 0))],
        [
            jax.ShapeDtypeStruct((rows, model), bf16),
            jax.ShapeDtypeStruct((groups, rows // WIN, width), f32),
        ],
        [
            pltpu.VMEM((WIN + rows, width), bf16),
            pltpu.VMEM((WIN + rows, width), bf16),
            pltpu.VMEM((WIN + rows + slots, width), f32),
        ],
        32, (place, q, k, v, score, rim, rim, rim, far, far, far),
    )


def attend_back_kernel(
    heads, head_size, unroll, group, last, place_ref, q_h, k_h, v_h, grad_h, total_ref, score_h, rim_h, far_h, normed_h,
    *refs,
):
    refs = list(refs)
    earlier = [refs.pop(0) for _ in range(5)] if group else []
    beside_refs = [refs.pop(0) for _ in range(2)] if group else []
    dq_h, dk_h, dv_h, ds_ref, rim_out, far_out, rim_ds, far_ds, send, keep = refs[:10]
    q_ref, grad_ref, score_ref, dq_ref, keys, values, gate_ref, dkeys, dvalues, dscore, normed, loaded, stored = refs[10:]
    model = normed.shape[1]
    place = place_ref[0]
    rows, width = q_ref.shape
    slots = far_h.shape[0]
    cols, value_cols = pl.ds(group * width, width), pl.ds(model + group * width, width)
    scores, normed_cols = pl.ds(3 * model, LANES), pl.ds(2 * model, model)
    near, own, far = pl.ds(0, WIN), pl.ds(WIN, rows), pl.ds(WIN + rows, slots)
    loads = Moves(loaded)
    first = [
        loads.add(source, target)
        for source, target in (
            (score_h, score_ref.at[own, :]), (rim_h.at[:, scores], score_ref.at[near, :]),
            (far_h.at[:, scores], score_ref.at[far, :]),
        )
    ]
    second = [
        loads.add(source, target)
        for source, target in (
            (q_h.at[:, cols], q_ref), (grad_h.at[:, cols], grad_ref), (k_h.at[:, cols], keys.at[own, :]),
            (rim_h.at[:, cols], keys.at[near, :]), (far_h.at[:, cols], keys.at[far, :]),
            (v_h.at[:, cols], values.at[own, :]), (rim_h.at[:, value_cols], values.at[near, :]),
            (far_h.at[:, value_cols], values.at[far, :]),
        )
    ]
    third = [
        loads.add(source, target)
        for source, target in (
            (normed_h, normed.at[own, :]), (rim_h.at[:, normed_cols], normed.at[near, :]),
            (far_h.at[:, normed_cols], normed.at[far, :]),
        )
    ]
    loads.start(*first, *second, *third)
    for ref in (dkeys, dvalues, dscore):
        ref[...] = jnp.zeros_like(ref)
    loads.wait(*first)
    gather = head_spread(group, head_size, width)
    gate = jax.nn.log_sigmoid(score_ref[...].astype(f32))
    gate_ref[...] = sum(nn(part, gather) for part in three_parts(gate))
    gate_ref[0:WIN, :] = jnp.where(place == 0, very_low, gate_ref[0:WIN, :])
    near_ok = near_bias(width)
    far_pos = jnp.broadcast_to(far_positions(score_ref[far, :], heads, rows, slots // PICK), (slots, LANES))
    loads.wait(*second)

    @pl.loop(0, rows // WIN, unroll=unroll)
    def _(i):
        at = pl.ds(pl.multiple_of(i * WIN, WIN), WIN)
        after = pl.ds(pl.multiple_of(i * WIN + WIN, WIN), WIN)
        span = pl.ds(pl.multiple_of(i * WIN, WIN), 2 * WIN)
        keys_cat = jnp.concatenate([keys[span, :], keys[far, :]], axis=0)
        values_cat = jnp.concatenate([values[span, :], values[far, :]], axis=0)
        stack = stack_heads(q_ref[at, :], head_size, 1.0 / math.sqrt(head_size))
        grad_stack = stack_heads(grad_ref[at, :], head_size, 1.0)
        logit = tile_logits(i, keys_cat, stack, gate_ref, far_pos, place, rows, near_ok)
        prob = jnp.exp(logit - total_ref[group, pl.ds(i, 1), :])
        grad_prob = nt(values_cat, grad_stack)
        delta = jnp.sum(prob * grad_prob, axis=0, keepdims=True)
        grad_logit = prob * (grad_prob - delta)
        low = grad_logit.astype(bf16)
        dq_ref[at, :] = (pick_heads(tn(low, keys_cat), head_size) * (1.0 / math.sqrt(head_size))).astype(bf16)
        for ref, update in (
            (dkeys, nn(low, stack)),
            (dvalues, nn(prob.astype(bf16), grad_stack)),
            (dscore, grad_logit),
        ):
            ref[at, :] += update[:WIN]
            ref[after, :] = update[WIN : 2 * WIN]
            ref[far, :] += update[2 * WIN :]

    stores = Moves(stored)
    for source, target in ((dq_ref, dq_h), (dkeys.at[own, :], dk_h), (dvalues.at[own, :], dv_h)):
        stores.start(stores.add(source, target))
    loads.wait(*third)
    mine = place % 2
    half = model // 2
    joint = jnp.concatenate(
        [tn(normed[own, :], dq_ref[...])]
        + [tn(normed[...], ref[...].astype(bf16)) for ref in (dkeys, dvalues)],
        axis=1,
    ).astype(bf16)
    top, low = joint[:half], joint[half:]
    start = 0
    if group:
        start = beside_refs[0].shape[1]
        send[:, :start] = beside_refs[0][...]
        keep[:, :start] = beside_refs[1][...]
    send[:, start:] = jnp.where(mine == 0, low, top)
    keep[:, start:] = jnp.where(mine == 0, top, low)
    if group:
        for out, old in zip((rim_out, far_out), earlier[:2]):
            out[...] = old[...]
    for out, part in ((rim_out, near), (far_out, far)):
        for base, ref in ((0, dkeys), (model, dvalues)):
            out[:, base + group * width : base + (group + 1) * width] = ref[part, :].astype(bf16)
    for number, (out_ref, part) in enumerate(((rim_ds, near), (far_ds, far), (ds_ref, own))):
        sums = dscore[part, :]
        high = sums.astype(bf16)
        rest = (sums - high.astype(f32)).astype(bf16)
        update = (nt(high, gather) + nt(rest, gather)) * jax.nn.sigmoid(-score_ref[part, :].astype(f32))
        out_ref[...] = update + earlier[2 + number][...] if group else update
    if last:
        rim_out[:, 2 * model :] = rim_ds[...].astype(bf16)
        far_out[:, 2 * model :] = far_ds[...].astype(bf16)
    stores.wait(*range(len(stores.made)))


def attend_back(place, q, k, v, grad, total, score, rim, far, normed, heads, group, earlier, joined, after=(), unroll=4):
    rows, model = q.shape
    slots = far.shape[0]
    width = PACK * WIN
    groups = model // width
    channels = 2 * model + LANES
    S = jax.ShapeDtypeStruct
    half = (model // 2, 3 * width + (joined[0].shape[1] if joined else 0))
    ext = WIN + rows + slots
    V = pltpu.VMEM
    out = launch(
        functools.partial(attend_back_kernel, heads, WIN, unroll, group, group == groups - 1),
        "attend_back", 13, (),
        [pl.BlockSpec(memory_space=pltpu.SMEM)] + [anywhere()] * 4 + [vmem()] + [anywhere()] * 4
        + [vmem()] * (len(earlier) + len(joined)),
        [anywhere()] * 3 + [vmem()] * 7,
        [
            S((rows, width), bf16), S((rows, width), f32), S((rows, width), f32), S((rows, LANES), f32),
            S((WIN, channels), bf16), S((slots, channels), bf16), S((WIN, LANES), f32), S((slots, LANES), f32),
        ] + [S(half, bf16)] * 2,
        [
            V((rows, width), bf16), V((rows, width), bf16), V((ext, LANES), bf16), V((rows, width), bf16),
            V((ext, width), bf16), V((ext, width), bf16),
        ] + [V((ext, width), f32)] * 4
        + [V((ext, model), bf16), pltpu.SemaphoreType.DMA((14,)), pltpu.SemaphoreType.DMA((3,))],
        30, (place, q, k, v, grad, total, score, rim, far, normed, *earlier, *joined), after,
    )
    dq, dk, dv, ds, rim_out, far_out, rim_ds, far_ds, send, keep, token = out
    return (dq, dk, dv), (rim_out, far_out, rim_ds, far_ds, ds), (send, keep), token


cubic = 0.044715
root = 0.7978845608028654


def feed_kernel(
    tile, pieces, block, mine_ref, mixed_h, tokens_h, cot_h, out_weight_h, expand_h, reduce_h, out_bias_ref, gain_ref,
    shift_ref, expand_bias_ref,
    resid_h, hidden_h, grad_pre_h, sums_ref, send_one, keep_one, send_two, keep_two,
    mixed, tokens, cot, out_weight, expand, reduce, resids, normed, hidden, grad_pre, one, two, loaded, stored,
):
    rows, width = cot.shape
    inner = expand.shape[1]
    span = inner // pieces
    steps = rows // tile
    mine = mine_ref[0]
    loads = Moves(loaded)
    first = [loads.add(*pair) for pair in ((mixed_h, mixed), (out_weight_h, out_weight), (tokens_h, tokens))]
    second = loads.add(cot_h, cot)
    parts = []
    for piece in range(pieces):
        at = pl.ds(piece * span, span)
        parts.append(
            (loads.add(expand_h.at[:, at], expand.at[:, at]), loads.add(reduce_h.at[at, :], reduce.at[at, :]))
        )
    loads.start(*range(len(loads.made)))

    def store(number, source, target):
        return pltpu.make_async_copy(source, target, stored.at[number])

    def tile_stores(step):
        here = rows_at(step, tile)
        return [
            store(3 * step + at, source.at[here, :], target.at[here, :])
            for at, (source, target) in enumerate(((resids, resid_h), (hidden, hidden_h), (grad_pre, grad_pre_h)))
        ]

    def feed_tile(step, leading):
        here = rows_at(step, tile)
        if leading:
            loads.wait(*first)
        resid = tokens[here, :].astype(f32) + nn(mixed[here, :], out_weight[...]) + row(out_bias_ref)
        resids[here, :] = resid
        unit, _ = normalise(resid)
        low = (unit * row(gain_ref) + row(shift_ref)).astype(bf16)
        normed[here, :] = low
        if leading:
            loads.wait(second)
        sums = []
        for piece in range(pieces):
            at = slice(piece * span, (piece + 1) * span)
            if leading:
                loads.wait(*parts[piece])
            pre = nn(low, expand[:, at]) + row(expand_bias_ref)[:, at]
            back = nt(cot[here, :], reduce[at, :])
            squared = pre * pre
            half = 0.5 + 0.5 * jnp.tanh(pre * (root + root * cubic * squared))
            active = pre * half
            slope = half + (active - active * half) * (2.0 * root + 6.0 * root * cubic * squared)
            hidden[here, at] = active.astype(bf16)
            grad = (back * slope).astype(bf16)
            grad_pre[here, at] = grad
            sums.append(column_sums(grad.astype(f32)))
        total = jnp.concatenate(sums, axis=1)
        if leading:
            sums_ref[...] = total
        else:
            sums_ref[...] += total
        for copy in tile_stores(step):
            copy.start()

    feed_tile(0, True)

    @pl.loop(1, steps)
    def _(step):
        feed_tile(step, False)

    base = 3 * steps
    count = inner // 2 // block
    half = width // 2

    def one_store(turn, j):
        here = rows_at(j, block)
        target = (send_one, keep_one)[turn]
        return store(base + turn * count + j, one.at[turn, here, :], target.at[here, :])

    def two_store(turn):
        return store(base + 2 * count + turn, two.at[turn], (send_two, keep_two)[turn])

    for turn in range(2):
        side_of = (1 - mine) if turn == 0 else mine

        @pl.loop(0, count)
        def _(j):
            one[turn, rows_at(j, block), :] = tn(hidden[:, rows_at(side_of * count + j, block)], cot[...]).astype(bf16)
            one_store(turn, j).start()

    for turn in range(2):
        side_of = (1 - mine) if turn == 0 else mine
        two[turn] = tn(normed[:, rows_at(side_of, half)], grad_pre[...]).astype(bf16)
        two_store(turn).start()

    @pl.loop(0, steps)
    def _(step):
        for copy in tile_stores(step):
            copy.wait()

    for turn in range(2):
        @pl.loop(0, count)
        def _(j):
            one_store(turn, j).wait()

        two_store(turn).wait()


def feed(
    mine, mixed, tokens, cot, out_weight, out_bias, gain, shift, expand, expand_bias, reduce, tile=512, pieces=4, block=512,
):
    rows, width = tokens.shape
    inner = expand.shape[1]
    steps = rows // tile
    S = jax.ShapeDtypeStruct
    B = pltpu.VMEM
    return launch(
        functools.partial(feed_kernel, tile, pieces, block),
        "feed", 33, (),
        [anywhere()] * 6 + [vmem()] * 4,
        [anywhere()] * 3 + [vmem()] + [anywhere()] * 4,
        [
            S((rows, width), f32), S((rows, inner), bf16), S((rows, inner), bf16), S((1, inner), f32),
            S((inner // 2, width), bf16), S((inner // 2, width), bf16),
            S((width // 2, inner), bf16), S((width // 2, inner), bf16),
        ],
        [
            B((rows, width), bf16), B((rows, width), bf16), B((rows, width), bf16), B((width, width), bf16),
            B((width, inner), bf16), B((inner, width), bf16), B((rows, width), f32), B((rows, width), bf16),
            B((rows, inner), bf16), B((rows, inner), bf16), B((2, inner // 2, width), bf16), B((2, width // 2, inner), bf16),
            pltpu.SemaphoreType.DMA((4 + 2 * pieces,)),
            pltpu.SemaphoreType.DMA((3 * steps + inner // block + 2,)),
        ],
        60, (mixed, tokens, cot, out_weight, expand, reduce, out_bias, gain, shift, expand_bias), (), (mine,),
    )


def feed_back_kernel(
    tile, pieces, mine_ref, grad_pre_h, resid_h, cot_h, mixed_h, expand_h, out_weight_h, gain_ref,
    grad_resid_h, grad_mixed_h, sums_ref, send_h, keep_h,
    grad_pre, resid, cot, mixed, expand, out_weight, grad_attn, grad_mixed, three, loaded, stored,
):
    rows, width = cot.shape
    inner = expand.shape[1]
    span = inner // pieces
    steps = rows // tile
    half = width // 2
    mine = mine_ref[0]
    loads = Moves(loaded)

    def tile_load(step):
        return [
            loads.add(source.at[rows_at(step, tile), :], target.at[rows_at(step, tile), :])
            for source, target in ((grad_pre_h, grad_pre), (resid_h, resid), (cot_h, cot))
        ]

    tiles = [tile_load(0)]
    weights = [
        loads.add(expand_h.at[:, pl.ds(piece * span, span)], expand.at[:, pl.ds(piece * span, span)])
        for piece in range(pieces)
    ]
    late = loads.add(out_weight_h, out_weight)
    tiles += [tile_load(step) for step in range(1, steps)]
    last = loads.add(mixed_h, mixed)
    loads.start(*range(len(loads.made)))
    stores = Moves(stored)
    sums = []

    def first_part(step):
        here = rows_at(step, tile)
        grad_normed = jnp.zeros((tile, width), f32)
        for piece in range(pieces):
            at = slice(piece * span, (piece + 1) * span)
            if step == 0:
                loads.wait(weights[piece])
            grad_normed = grad_normed + nt(grad_pre[here, at], expand[:, at])
        return grad_normed

    def second_part(step, grad_normed):
        here = rows_at(step, tile)
        wide = cot[here, :].astype(f32)
        unit, inverse = normalise(resid[here, :])
        grad_resid = wide + normalise_back(grad_normed, unit, inverse, row(gain_ref))
        resid[here, :] = grad_resid
        low = grad_resid.astype(bf16)
        grad_attn[here, :] = low
        grad_mixed[here, :] = nt(low, out_weight[...]).astype(bf16)
        sums.append(
            jnp.concatenate(
                [
                    column_sums(low.astype(f32)),
                    column_sums(grad_normed * unit),
                    column_sums(grad_normed),
                    column_sums(wide),
                ],
                axis=0,
            )
        )

    loads.wait(*tiles[0])
    before = first_part(0)
    loads.wait(late, *tiles[1])
    ahead = first_part(1)
    second_part(0, before)
    loads.wait(last, *[at for tile_loads in tiles[2:] for at in tile_loads])
    for step in range(2, steps + 1):
        before, ahead = ahead, first_part(step) if step < steps else None
        second_part(step - 1, before)
    sums_ref[...] = sum(sums)
    for step in range(steps):
        here = rows_at(step, tile)
        stores.start(
            stores.add(resid.at[here, :], grad_resid_h.at[here, :]),
            stores.add(grad_mixed.at[here, :], grad_mixed_h.at[here, :]),
        )
    for turn in range(2):
        side_of = (1 - mine) if turn == 0 else mine
        three[turn] = tn(mixed[:, rows_at(side_of, half)], grad_attn[...]).astype(bf16)
        stores.start(stores.add(three.at[turn], (send_h, keep_h)[turn]))
    stores.wait(*range(len(stores.made)))


def feed_back(mine, grad_pre, resid, cot, mixed, expand, out_weight, gain, tile=256, pieces=4):
    rows, width = resid.shape
    inner = expand.shape[1]
    steps = rows // tile
    S = jax.ShapeDtypeStruct
    B = pltpu.VMEM
    return launch(
        functools.partial(feed_back_kernel, tile, pieces), "feed_back", 12, (),
        [anywhere()] * 6 + [vmem()],
        [anywhere()] * 2 + [vmem()] + [anywhere()] * 2,
        [
            S((rows, width), f32), S((rows, width), bf16), S((4, width), f32),
            S((width // 2, width), bf16), S((width // 2, width), bf16),
        ],
        [
            B((rows, inner), bf16), B((rows, width), f32), B((rows, width), bf16), B((rows, width), bf16),
            B((width, inner), bf16), B((width, width), bf16), B((rows, width), bf16), B((rows, width), bf16),
            B((2, width // 2, width), bf16),
            pltpu.SemaphoreType.DMA((3 * steps + pieces + 2,)),
            pltpu.SemaphoreType.DMA((2 * steps + 2,)),
        ],
        44, (grad_pre, resid, cot, mixed, expand, out_weight, gain), (), (mine,),
    )


def finish_kernel(resid_ref, hidden_ref, reduce_ref, bias_ref, out_ref):
    out_ref[...] = (resid_ref[...] + nn(hidden_ref[...], reduce_ref[...]) + row(bias_ref)).astype(bf16)


def finish(resid, hidden, reduce, bias, after=(), tile=256):
    rows, width = resid.shape
    inner = reduce.shape[0]
    return launch(
        finish_kernel, "finish", 7, (rows // tile,),
        [tiled(tile, width), tiled(tile, inner), same(inner, width), same(width)],
        [tiled(tile, width)], [jax.ShapeDtypeStruct((rows, width), bf16)],
        [], 26, (resid, hidden, reduce, bias), after,
    )


def beside(refs):
    return jnp.concatenate([ref[...] for ref in refs], axis=1)


def join_kernel(
    steps, groups, tokens_ref, resid_ref, ds_ref, rim_ref, far_ref, picks_ref, gain_ref, shift_ref,
    joint_ref, score_weight_ref, *refs,
):
    dq_refs, dk_refs, dv_refs = (refs[at * groups : (at + 1) * groups] for at in range(3))
    token_ref, sums_ref, score_grad_ref = refs[3 * groups :]
    step = pl.program_id(0)
    tile, width = tokens_ref.shape
    heads = score_weight_ref.shape[0]
    unit, inverse = normalise(tokens_ref[...].astype(f32))
    gain = row(gain_ref)
    normed = (unit * gain + row(shift_ref)).astype(bf16)
    picks = spread_slots(picks_ref[...].astype(f32))
    row_of = lax.broadcasted_iota(jnp.int32, (picks.shape[0], tile), 1) + step * tile
    chosen = jnp.where(picks == row_of.astype(f32), 1.0, 0.0).astype(bf16)
    at_end = jnp.where(step == steps - 1, 1.0, 0.0)

    def whole(own, start):
        span = own.shape[1]
        total = own + tn(chosen, far_ref[:, start : start + span])
        rim = rim_ref[:, start : start + span].astype(f32) * at_end
        return jnp.concatenate([total[: tile - WIN], total[tile - WIN :] + rim], axis=0).astype(bf16)

    dq = beside(dq_refs)
    dk = whole(beside(dk_refs), 0)
    dv = whole(beside(dv_refs), width)
    ds = whole(ds_ref[...], 2 * width)
    grad_normed = (
        nt(dq, joint_ref[:, :width])
        + nt(dk, joint_ref[:, width : 2 * width])
        + nt(dv, joint_ref[:, 2 * width :])
        + nn(ds[:, :heads], score_weight_ref[...])
    )
    token_ref[...] = resid_ref[...] + normalise_back(grad_normed, unit, inverse, gain)
    accumulate(
        sums_ref,
        jnp.concatenate(
            [
                column_sums(grad_normed * unit),
                column_sums(grad_normed),
                column_sums(dq.astype(f32)),
                column_sums(dv.astype(f32)),
            ],
            axis=0,
        ),
    )
    accumulate(score_grad_ref, tn(ds, normed)[: score_grad_ref.shape[0]])


def join(tokens, resid, dqs, dks, dvs, ds, rim, far, picks, gain, shift, joint, score_weight, after=(), tile=256):
    rows, width = tokens.shape
    heads = score_weight.shape[0]
    S = jax.ShapeDtypeStruct
    return launch(
        functools.partial(join_kernel, rows // tile, len(dqs)), "join", 14, (rows // tile,),
        [tiled(tile, width)] * 2 + [
            tiled(tile, LANES), same(*rim.shape), same(*far.shape), same(*picks.shape), same(width), same(width),
            same(*joint.shape), same(*score_weight.shape),
        ] + [tiled(tile, part.shape[1]) for part in (*dqs, *dks, *dvs)],
        [tiled(tile, width), same(4, width), same(heads, width)],
        [S((rows, width), f32), S((4, width), f32), S((heads, width), f32)],
        [], 28, (tokens, resid, ds, rim, far, picks, gain, shift, joint, score_weight, *dqs, *dks, *dvs), after,
    )


def swap(value, axis, bit):
    count = lax.axis_size(axis)
    return lax.ppermute(value, axis, [(i, i ^ bit) for i in range(count)])


def side(axis, bit):
    return (lax.axis_index(axis) // bit) % 2


def axis_bits(axis):
    count, bits, bit = lax.axis_size(axis), [], 1
    while bit < count:
        bits.append((axis, bit))
        bit *= 2
    return bits


def woven(*lists):
    result = []
    for step in range(max(map(len, lists))):
        for items in lists:
            result += items[step : step + 1]
    return result


def orders():
    near, far = axis_bits("seq"), axis_bits("dp")
    first, rest = near[:1], near[1:]
    return (
        first + rest + far,
        first + woven(rest[::-1], far),
        first + woven(far, rest),
    )


def cut(value, pieces):
    return value.reshape(pieces, value.shape[0] // pieces, value.shape[1])


class Chain:
    def __init__(self, send, keep, order):
        self.order, self.level, self.down = order, 0, True
        half = 2 ** (len(order) - 1)
        self.send, self.keep = cut(send, half), cut(keep, half)
        self.mine = [side(*where).astype(jnp.int32) for where in order]

    def got(self):
        return swap(self.send, *self.order[self.level])


def added(one, two):
    return (one[...].astype(f32) + two[...].astype(f32)).astype(bf16)


class Total:
    def __init__(self, value, order):
        self.send, self.order, self.level = value, order, 0

    def got(self):
        return swap(self.send, *self.order[self.level])


def advance_kernel(plan, bits_ref, *refs):
    refs = list(refs)
    outs = refs[sum(4 if kind == "split" else 2 for kind in plan) :]
    for kind in plan:
        if kind == "split":
            for _ in range(2):
                outs.pop(0)[...] = added(refs.pop(0), refs.pop(0))
        elif kind == "sum":
            outs.pop(0)[...] = refs.pop(0)[...] + refs.pop(0)[...]
        elif kind == "close":
            outs.pop(0)[...] = added(refs.pop(0), refs.pop(0))
        else:
            out = outs.pop(0)
            for which in range(2):
                out[which] = refs.pop(0)[...]


def advance(chains, after=()):
    plan, operands, in_specs, out_specs, shapes, bits, free = [], [], [], [], [], [], []
    depth = len(chains[0].order)
    for chain in chains:
        if isinstance(chain, Total):
            plan.append("sum")
            continue
        last = chain.down and chain.level == depth - 1
        plan.append("close" if last else "split" if chain.down else "stack")
    sizes = [chain.send.shape[0] // (2 if kind == "split" else 1) for chain, kind in zip(chains, plan)]
    steps = min([4] + [size for size, kind in zip(sizes, plan) if kind != "sum"])
    S = jax.ShapeDtypeStruct

    def half_of(which, other, block, tail):
        def index(g, bits_ref):
            mine = bits_ref[which]
            return ((1 - mine if other else mine) * steps + g, 0, 0)

        return pl.BlockSpec((block,) + tail, index)

    for chain, kind, size in zip(chains, plan, sizes):
        got, tail = chain.got(), chain.send.shape[1:]
        block = size // steps
        if kind == "sum":
            free += [len(operands), len(operands) + 1]
            operands += [chain.send, got]
            in_specs += [same(*chain.send.shape)] * 2
            out_specs += [same(*chain.send.shape)]
            shapes += [S(chain.send.shape, f32)]
        elif kind == "split":
            which = len(bits)
            bits.append(chain.mine[chain.level + 1])
            places = len(operands)
            free += [places + 1, places + 3] if chain.level == 0 else range(places, places + 4)
            for other in (True, False):
                operands += [chain.keep, got]
                in_specs += [half_of(which, other, block, tail)] * 2
            out_specs += [tiled(block, *tail)] * 2
            shapes += [S((size,) + tail, bf16)] * 2
        elif kind == "close":
            free += [len(operands), len(operands) + 1]
            operands += [chain.keep, got]
            in_specs += [tiled(block, *tail)] * 2
            out_specs += [tiled(block, *tail)]
            shapes += [S((size,) + tail, bf16)]
        else:
            free += [len(operands), len(operands) + 1]
            operands += [chain.send, got]
            in_specs += [tiled(block, *tail)] * 2
            out_specs += [pl.BlockSpec((2, block) + tail, lambda g, *_: (0, g, 0, 0))]
            shapes += [S((2, size) + tail, bf16)]
    bits = jnp.stack(bits) if bits else jnp.zeros((1,), jnp.int32)
    outs = launch(
        functools.partial(advance_kernel, plan), "advance", 2, (steps,), in_specs, out_specs, shapes, [], 20, operands,
        after, (bits,), free,
    )
    for chain, kind in zip(chains, plan):
        if kind == "split":
            chain.send, chain.keep = outs[:2]
            chain.level += 1
            outs = outs[2:]
        elif kind == "sum":
            chain.send = outs[0]
            chain.level += 1
            outs = outs[1:]
        else:
            chain.send = outs[0].reshape((-1,) + chain.send.shape[1:])
            outs = outs[1:]
            if kind == "close":
                chain.down = False
            else:
                chain.level -= 1
    return outs[0]


def finished(chain):
    if isinstance(chain, Total):
        return chain.level == len(chain.order)
    return not chain.down and chain.level == 0


def ends(chain):
    return chain.send, chain.got()


def own_place(order):
    place = 0
    for axis, bit in order:
        place = place * 2 + side(axis, bit)
    return place.astype(jnp.int32).reshape(1)


def widen_half(own, chain, half_of, into=(), after=()):
    value, other = half_of
    half, size, n = value.shape
    count, group = 2 * half, 4

    def side_of(own_ref):
        mine = own_ref[0] // half
        return 1 - mine if other else mine

    def kernel(own_ref, value_ref, *refs):
        out_ref = refs[-1]
        for i in range(group):
            out_ref[i] = value_ref[jnp.bitwise_xor(own_ref[0] % group, i)].astype(f32)

    out, token = launch(
        kernel, "widen", 4, (half // group,),
        [pl.BlockSpec((group, size, n), lambda s, own_ref: (jnp.bitwise_xor(own_ref[0] % half // group, s), 0, 0))]
        + [anywhere()] * len(into),
        [pl.BlockSpec((group, size, n), lambda s, own_ref: (side_of(own_ref) * (half // group) + s, 0, 0))],
        [jax.ShapeDtypeStruct((count, size, n), f32)],
        [], 24, (value, *into), after, (own,), (0,), {2: 0} if into else None,
    )
    return out, token


def widen_joint_half(owns, values, other, into=(), after=()):
    half, size, n = values[0].shape
    count, group, model, width = 2 * half, 4, n // 2, PACK * WIN

    def side_of(own_ref):
        mine = own_ref[0] // half
        return 1 - mine if other else mine

    def kernel(own_one_ref, own_two_ref, one_ref, two_ref, *refs):
        joint_ref, first_ref = refs[-2:]
        for i in range(group):
            one = one_ref[jnp.bitwise_xor(own_one_ref[0] % group, i)].astype(f32)
            two = two_ref[jnp.bitwise_xor(own_two_ref[0] % group, i)].astype(f32)
            first_ref[i] = two[:, :model]
            for piece, start, g in ((one, 0, 0), (one, 3 * width, 1), (two, model, 2)):
                for kind in range(3):
                    to = kind * model + g * width
                    joint_ref[i, :, to : to + width] = piece[:, start + kind * width : start + (kind + 1) * width]

    def read(which):
        def index(s, *own_refs):
            return (jnp.bitwise_xor(own_refs[which][0] % half // group, s), 0, 0)

        return pl.BlockSpec((group, size, n), index)

    def write(columns):
        return pl.BlockSpec((group, size, columns), lambda s, own_ref, _: (side_of(own_ref) * (half // group) + s, 0, 0))

    S = jax.ShapeDtypeStruct
    joint, first, token = launch(
        kernel, "widen_joint", 4, (half // group,),
        [read(0), read(1)] + [anywhere()] * len(into), [write(3 * model), write(model)],
        [S((count, size, 3 * model), f32), S((count, size, model), f32)],
        [], 24, (*values, *into), after, tuple(owns), (0, 1), {4: 0, 5: 1} if into else None,
    )
    return (joint, first), token


def per_device(
    tokens, cotangent, first_gain, first_shift, joint_weight, query_bias, value_bias, score_weight, out_weight, out_bias,
    second_gain, second_shift, expand_weight, expand_bias, reduce_weight, reduce_bias, picks, quota,
):
    rows, width = tokens.shape[1:]
    heads = score_weight.shape[1]
    inner = expand_weight.shape[1]
    blocks = lax.axis_size("seq")
    slots = blocks * PICK
    here = lax.axis_index("seq").astype(jnp.int32).reshape(1)
    first, second, _ = orders()
    mine = side(*first[0]).astype(jnp.int32).reshape(1)
    inputs, grad_out = tokens[0], cotangent[0]
    chosen, turned = picks[0, 0], score_weight.T
    normed, q, k, v, score, rim_sent, sent, _ = project(
        inputs, chosen, quota[0], first_gain, first_shift, joint_weight, query_bias, value_bias, turned
    )
    rim = passed_along(rim_sent, "seq", 1)
    far = lax.all_to_all(
        sent.reshape(blocks, PICK, -1), "seq", split_axis=0, concat_axis=0, tiled=True
    ).reshape(slots, -1)
    mixed, total, _ = attend(here, q, k, v, score, rim, far, heads)
    resid, hidden, grad_pre, expand_sums, *halves, _ = feed(
        mine, mixed, inputs, grad_out, out_weight, out_bias, second_gain, second_shift, expand_weight, expand_bias,
        reduce_weight,
    )
    reduced, expanded = Chain(*halves[:2], first), Chain(*halves[2:], second)
    grad_resid, grad_mixed, sums_two, *out_halves, stage = feed_back(
        mine, grad_pre, resid, grad_out, mixed, expand_weight, out_weight, second_gain
    )
    big = [reduced, expanded]
    back = functools.partial(attend_back, here, q, k, v, grad_mixed, total, score, rim, far, normed, heads)
    stage = advance(big, (stage,))
    grads_zero, carried, joined, stage = back(0, (), (), (stage,))
    grads_one, carried, joined, stage = back(1, carried, joined, (stage,))
    one = Chain(*joined, first)
    stage = advance(big, (stage,))
    grads_two, carried, joined, stage = back(2, carried, tuple(out_halves), (stage,))
    two = Chain(*joined, second)
    rim_grad, far_grad, _, _, ds = carried
    rim_back = passed_along(rim_grad, "seq", -1)
    far_back = lax.all_to_all(
        far_grad.reshape(blocks, PICK, -1), "seq", split_axis=0, concat_axis=0, tiled=True
    ).reshape(slots, -1)
    dqs, dks, dvs = zip(grads_zero, grads_one, grads_two)
    stage = advance(big + [one], (stage,))
    stage = advance(big + [two], (stage,))
    token_grad, sums_one, score_grad, stage = join(
        inputs, grad_resid, dqs, dks, dvs, ds, rim_back, far_back, chosen, first_gain, first_shift, joint_weight, turned,
        (stage,),
    )
    small = Total(
        jnp.concatenate([sums_one, sums_two, expand_sums.reshape(inner // width, width), score_grad], axis=0), first
    )
    late = [one, two]
    stage = advance(big + late, (stage,))
    layer_out, stage = finish(resid, hidden, reduce_weight, reduce_bias, (stage,))
    for chains in (
        big + late + [small], late, big + late + [small], late + [small], big + late + [small],
    ):
        stage = advance([chain for chain in chains if not finished(chain)], (stage,))
    while not finished(reduced):
        stage = advance([chain for chain in big + late if not finished(chain)], (stage,))
    own_first, own_second = own_place(first), own_place(second)
    halves_one, halves_two = ends(reduced), ends(expanded)
    reduce_weight_grad, stage = widen_half(own_first, reduced, (halves_one[0], False), (), (stage,))
    expand_weight_grad, stage = widen_half(own_second, expanded, (halves_two[0], False), (), (stage,))
    reduce_weight_grad, stage = widen_half(own_first, reduced, (halves_one[1], True), (reduce_weight_grad,), (stage,))
    expand_weight_grad, stage = widen_half(own_second, expanded, (halves_two[1], True), (expand_weight_grad,), (stage,))
    while not (finished(one) and finished(two)):
        stage = advance([chain for chain in late if not finished(chain)], (stage,))
    while not finished(small):
        stage = advance([small], (stage,))
    halves_one, halves_two = ends(one), ends(two)
    owns = (own_first, own_second)
    both, stage = widen_joint_half(owns, (halves_one[0], halves_two[0]), False, (), (stage,))
    both, stage = widen_joint_half(owns, (halves_one[1], halves_two[1]), True, both, (stage,))
    reduce_weight_grad = reduce_weight_grad.reshape(inner, width)
    expand_weight_grad = expand_weight_grad.reshape(width, inner)
    joint_weight_grad, out_weight_grad = both[0].reshape(width, 3 * width), both[1].reshape(width, width)
    small = small.send
    gain_one, shift_one, query_sum, value_sum, out_sum, gain_two, shift_two, reduce_sum = (small[i] for i in range(8))
    past = 8 + inner // width
    return (
        layer_out[None],
        token_grad[None],
        gain_one,
        shift_one,
        joint_weight_grad,
        query_sum,
        value_sum,
        small[past : past + heads].T,
        out_weight_grad,
        out_sum,
        gain_two,
        shift_two,
        expand_weight_grad,
        small[8:past].reshape(inner),
        reduce_weight_grad,
        reduce_sum,
    )


def solution(mesh):
    placed = (
        P("dp", "seq", None),
        P("dp", "seq", None),
        P(),
        P(),
        P(),
        P(),
        P(),
        P(),
        P(),
        P(),
        P(),
        P(),
        P(),
        P(),
        P(),
        P(),
        P("dp", "seq", None, None),
        P("dp", "seq", None),
    )
    return jax.shard_map(
        per_device,
        mesh=mesh,
        in_specs=placed,
        out_specs=(
            P("dp", "seq", None),
            P("dp", "seq", None),
            P(),
            P(),
            P(),
            P(),
            P(),
            P(),
            P(),
            P(),
            P(),
            P(),
            P(),
            P(),
            P(),
            P(),
        ),
        check_vma=False,
    )
```

time: 344 us -> 314 us (0.913); the launches traced: 343 us -> 309 us
  waiting for transfers between devices: 80.2 us -> 62.3 us
  Pallas kernels: 188 us -> 177 us
  starting transfers between devices: 59.9 us -> 55 us
    ppermute x45, waiting for transfers between devices: 73.8 us -> 55 us  [swap(): return lax.ppermute(value, axis, [(i, i ^ bit) for i in range(count)])]
    pallas_call x24 -> x28, Pallas kernels: 188 us -> 177 us  [launch(): pl.pallas_call(body, grid_spec=pltpu.PrefetchScalarGridSpec(num_scalar_pr...]
    unnamed x15 -> x40, local copies, waits for them, and re-layouts: 3.63 us -> 7.8 us
    ppermute x45, starting transfers between devices: 46.5 us -> 42.4 us  [swap(): return lax.ppermute(value, axis, [(i, i ^ bit) for i in range(count)])]
  transfers between devices with their start and end apart: 49 -> 49, of which waited for: 23 -> 17; matrix products, arithmetic and copies ran while one was open for 2% -> 1% of each run, Pallas kernels for 31% -> 35%
where the time goes in v2:
time: 314 us; the launch traced here: 309 us
  Pallas kernels  177 us (56%)
  waiting for transfers between devices  62.3 us (20%)
  starting transfers between devices  55 us (18%)
  local copies, waits for them, and re-layouts  10.8 us (3%)
    pallas_call x28, Pallas kernels, launch(): pl.pallas_call(body, grid_spec=pltpu.PrefetchScalarGridSpec(num_scalar_pr...  177 us
    ppermute x45, waiting for transfers between devices, swap(): return lax.ppermute(value, axis, [(i, i ^ bit) for i in range(count)])  55 us
    ppermute x45, starting transfers between devices, swap(): return lax.ppermute(value, axis, [(i, i ^ bit) for i in range(count)])  42.4 us
    unnamed x40, local copies, waits for them, and re-layouts  7.8 us
    all_to_all x1, waiting for transfers between devices, per_device(): lax.all_to_all(sent.reshape(blocks, PICK, -1), 'seq', split_axis=0, conca...  7.23 us
  transfers between devices with their start and end apart: 49, of which 17 were waited for; matrix products, arithmetic and copies ran while one was open for 1% of the time, Pallas kernels for 35%

profile of v2, /device:TPU:0, one launch (start us, length us, event | category | flops | bytes accessed | tf_op | source)
XLA Modules:
  0.0 309.5 jit_solution(14694963865524875118)
XLA Ops:
  0.6 11.3 %project.1 = (bf16[1024,768]{1,0:T(8,128)(2,1)}, bf16[1024,768]{1,0:T(8,128)(2,1)}, bf16[1024,768]{1,0:T(8,128)(2,1)}, bf16[1024,768]{1,0:T(8,128)(2,1)}, bf16[1...) custom-call(bf16[1024,768]{1,0:T(8,128)(2,1)} %bitcast.89, ...), custom_call_target="tpu_custom_call" | custom-call | flops 49999998976 | bytes 1048576 | tf_op jit(solution)/shard_map/project/pallas_call | solution.py:122
  14.3 5.0 %all-to-all-start = ((bf16[8,8,2432]{2,1,0:T(8,128)(2,1)}), bf16[8,8,2432]{2,1,0:T(8,128)(2,1)S(1)}, u32[]{:S(2)}, u32[]{:S(2)}) async-start(bf16[8,8,2432]{2,1,0:T(8,128)(2,1)} %bitcast.83), calls=%async_computation | async-start | bytes 622592 | tf_op jit(solution)/shard_map/all_to_all | solution.py:1118
  19.5 7.2 %all-to-all-done = bf16[8,8,2432]{2,1,0:T(8,128)(2,1)S(1)} async-done(((bf16[8,8,2432]{2,1,0:T(8,128)(2,1)}), bf16[8,8,2432]{2,1,0:T(8,128)(2,1)S(1)}, u32[]{:S(2)}, u32[]{:S(2)}) %all-to-all-start) | async-done | bytes 311328 | tf_op jit(solution)/shard_map/all_to_all | solution.py:1118
  27.6 13.8 %attend.1 = (bf16[1024,768]{1,0:T(8,128)(2,1)}, f32[3,16,256]{2,1,0:T(8,128)}, f32[8,128]{1,0:T(8,128)}) custom-call(s32[1]{0:T(128)} %bitcast.1.refs_0_, bf16[1024,768]{1,0:T(8,128)(2,1)} %get-tuple-element.159.refs_1_, bf16[1024,768]{1,0:T(8,128)(2,1)} %get-tuple-element.160.refs_2_, bf16[1024,768]{1,0:T(8,128)(2,1)} %get-tuple-element.161.refs_3_, ...), custom_call_target="tpu_custom_call" | custom-call | flops 60000002048 | bytes 1048576 | tf_op jit(solution)/shard_map/attend/pallas_call | solution.py:122
  41.4 32.4 %feed.1 = (f32[1024,768]{1,0:T(8,128)}, bf16[1024,3072]{1,0:T(8,128)(2,1)}, bf16[1024,3072]{1,0:T(8,128)(2,1)}, f32[1,3072]{1,0:T(1,128)}, bf16[1536,768]{1,0:T(...) custom-call(s32[1]{0:T(128)} %bitcast.refs_0_, ...), custom_call_target="tpu_custom_call" | custom-call | flops 165000003584 | bytes 1048576 | tf_op jit(solution)/shard_map/feed/pallas_call | solution.py:122
  74.4 15.9 %feed_back.1 = (f32[1024,768]{1,0:T(8,128)}, bf16[1024,768]{1,0:T(8,128)(2,1)}, f32[4,768]{1,0:T(4,128)}, bf16[384,768]{1,0:T(8,128)(2,1)}, bf16[384,768]{1,0:T(8,128)(2,1)}, /*index=5*/f32[8,128]{1,0:T(8,128)}) custom-call(s32[1]{0:T(128)} %bitcast.refs_0_, bf16[1024,3072]{1,0:T(8,128)(2,1)} %get-tuple-element.172.refs_1_, ...), custom_call_target="tpu_custom_call" | custom-call | flops 60000002048 | bytes 1048576 | tf_op jit(solution)/shard_map/feed_back/pallas_call | solution.py:122
  90.3 4.5 %advance.13 = (bf16[8,96,768]{2,1,0:T(8,128)(2,1)S(1)}, bf16[8,96,768]{2,1,0:T(8,128)(2,1)S(1)}, bf16[8,24,3072]{2,1,0:T(8,128)(2,1)S(1)}, bf16[8,24,3072]{2,1,0:T(8,128)(2,1)S(1)}, f32[8,128]{1,0:T(8,128)}) custom-call(s32[2]{0:T(128)S(1)} %pad_add_fusion.3.refs_0_, bf16[16,96,768]{2,1,0:T(8,128)(2,1)} %bitcast.103, ...), custom_call_target="tpu_custom_call" | custom-call | flops 10000000000 | bytes 1048576 | tf_op jit(solution)/shard_map/advance/pallas_call | solution.py:122
  96.3 12.8 %attend_back.3 = (bf16[1024,256]{1,0:T(8,128)(2,1)}, f32[1024,256]{1,0:T(8,128)}, f32[1024,256]{1,0:T(8,128)}, f32[1024,128]{1,0:T(8,128)}, bf16[64,1664]{1,0:T(...) custom-call(s32[1]{0:T(128)} %bitcast.1.refs_0_, ...), custom_call_target="tpu_custom_call" | custom-call | flops 65000001536 | bytes 1048576 | tf_op jit(solution)/shard_map/attend_back/pallas_call | solution.py:122
  109.1 13.9 %attend_back.4 = (bf16[1024,256]{1,0:T(8,128)(2,1)}, f32[1024,256]{1,0:T(8,128)}, f32[1024,256]{1,0:T(8,128)}, f32[1024,128]{1,0:T(8,128)}, bf16[64,1664]{1,0:T(...) custom-call(s32[1]{0:T(128)} %bitcast.1.refs_0_, ...), custom_call_target="tpu_custom_call" | custom-call | flops 65000001536 | bytes 1048576 | tf_op jit(solution)/shard_map/attend_back/pallas_call | solution.py:122
  127.5 14.1 %attend_back.5 = (bf16[1024,256]{1,0:T(8,128)(2,1)}, f32[1024,256]{1,0:T(8,128)}, f32[1024,256]{1,0:T(8,128)}, f32[1024,128]{1,0:T(8,128)}, bf16[64,1664]{1,0:T(...) custom-call(s32[1]{0:T(128)} %bitcast.1.refs_0_, ...), custom_call_target="tpu_custom_call" | custom-call | flops 65000001536 | bytes 1048576 | tf_op jit(solution)/shard_map/attend_back/pallas_call | solution.py:122
  141.8 2.7 advance.15
  153.3 4.0 %all-to-all-start.1 = ((bf16[8,8,1664]{2,1,0:T(8,128)(2,1)}), bf16[8,8,1664]{2,1,0:T(8,128)(2,1)}, u32[]{:S(2)}, u32[]{:S(2)}) async-start(bf16[8,8,1664]{2,1,0:T(8,128)(2,1)} %bitcast.84), calls=%async_computation.1 | async-start | bytes 425984 | tf_op jit(solution)/shard_map/all_to_all | solution.py:1141
  161.2 2.6 advance.16
  167.4 2.6 collective-permute-start.11
  170.4 13.6 %join.1 = (f32[1024,768]{1,0:T(8,128)}, f32[4,768]{1,0:T(4,128)}, f32[12,768]{1,0:T(8,128)}, f32[8,128]{1,0:T(8,128)}) custom-call(bf16[1024,768]{1,0:T(8,128)(2,1)} %bitcast.91, f32[1024,768]{1,0:T(8,128)} %get-tuple-element.221.refs_1_, f32[1024,128]{1,0:T(8,128)} %get-tuple-element.222.refs_2_, bf16[64,1664]{1,0:T(8,128)(2,1)} %collective-permute-done.15.refs_3_, ...), custom_call_target="tpu_custom_call" | custom-call | flops 70000001024 | bytes 1048576 | tf_op jit(solution)/shard_map/join/pallas_call | solution.py:122
  188.0 2.6 collective-permute-start.16
  191.0 9.9 %finish.1 = (bf16[1024,768]{1,0:T(8,128)(2,1)}, f32[8,128]{1,0:T(8,128)}) custom-call(f32[1024,768]{1,0:T(8,128)} %get-tuple-element.166.refs_2_.refs_0_, bf16[1024,3072]{1,0:T(8,128)(2,1)} %get-tuple-element.167.refs_1_, bf16[3072,768]{1,0:T(8,128)(2,1)} %refs_2_.1, f32[768]{0:T(1024)} %refs_3_.3, f32[8,128]{1,0:T(8,128)} %get-tuple-element.236.refs_4_), custom_call_target="tpu_custom_call" | custom-call | flops 35000000512 | bytes 1048576 | tf_op jit(solution)/shard_map/finish/pallas_call | solution.py:122
  203.5 2.6 collective-permute-start.23
  214.1 2.7 collective-permute-start.25
  223.6 2.7 collective-permute-start.31
  234.3 10.6 %collective-permute-done.35.refs_10_ = f32[24,768]{1,0:T(8,128)S(1)} collective-permute-done((f32[24,768]{1,0:T(8,128)S(1)}, f32[24,768]{1,0:T(8,128)S(1)}, u32[]{:S(2)}, u32[]{:S(2)}) %collective-permute-start.35) | collective-permute-done | bytes 73760 | tf_op jit(solution)/shard_map/ppermute | solution.py:868
  251.3 25.6 %collective-permute-done.39.refs_6_ = bf16[4,24,1536]{2,1,0:T(8,128)(2,1)} collective-permute-done((bf16[4,24,1536]{2,1,0:T(8,128)(2,1)}, bf16[4,24,1536]{2,1,0:T(8,128)(2,1)}, u32[]{:S(2)}, u32[]{:S(2)}) %collective-permute-start.39) | collective-permute-done | bytes 294944 | tf_op jit(solution)/shard_map/ppermute | solution.py:868
  276.9 3.5 %advance.23 = (bf16[2,8,96,768]{3,2,1,0:T(8,128)(2,1)S(1)}, bf16[2,8,24,3072]{3,2,1,0:T(8,128)(2,1)S(1)}, bf16[2,4,24,1536]{3,2,1,0:T(8,128)(2,1)S(1)}, bf16[2,4,24,1536]{3,2,1,0:T(8,128)(2,1)S(1)}, f32[8,128]{1,0:T(8,128)}) custom-call(s32[1]{0:T(128)} %constant.170.clone.1.refs_0_, bf16[8,96,768]{2,1,0:T(8,128)(2,1)S(1)} %bitcast.54, ...), custom_call_target="tpu_custom_call" | custom-call | flops 10000000000 | bytes 1048576 | tf_op jit(solution)/shard_map/advance/pallas_call | solution.py:122
  305.1 4.1 %widen_joint.3 = (f32[32,24,2304]{2,1,0:T(8,128)}, f32[32,24,768]{2,1,0:T(8,128)}, f32[8,128]{1,0:T(8,128)}) custom-call(s32[1]{0:T(128)} %bitcast.39.refs_0_, s32[1]{0:T(128)} %bitcast.37.refs_0_.refs_1_, bf16[16,24,1536]{2,1,0:T(8,128)(2,1)S(1)} %collective-permute-done.45.refs_2_, ...), custom_call_target="tpu_custom_call", output_to_operand_aliasing={{0}: (4, {}), {1}: (5, {})} | custom-call | flops 20000000000 | bytes 1048576 | tf_op jit(solution)/shard_map/widen_joint/pallas_call | solution.py:122
  (156 shorter events, 87.4 us)
Async XLA Ops:
  73.8 16.5 %collective-permute-start.1 = (bf16[16,96,768]{2,1,0:T(8,128)(2,1)}, bf16[16,96,768]{2,1,0:T(8,128)(2,1)S(1)}, u32[]{:S(2)}, u32[]{:S(2)}) collective-permute-start(bf16[16,96,768]{2,1,0:T(8,128)(2,1)} %bitcast.86), channel_id=1, source_target_pairs={{0,1},{1,0},{2,3},{3,2},{4,5},{5,4},{6,7},{7,6},{8,9},{9,8},{10,11... | collective-permute-start | bytes 7077896 | tf_op jit(solution)/shard_map/ppermute | solution.py:868
  73.9 16.5 %collective-permute-start.2 = (bf16[16,24,3072]{2,1,0:T(8,128)(2,1)}, bf16[16,24,3072]{2,1,0:T(8,128)(2,1)S(1)}, u32[]{:S(2)}, u32[]{:S(2)}) collective-permute-start(bf16[16,24,3072]{2,1,0:T(8,128)(2,1)} %bitcast.85), channel_id=1, source_target_pairs={{0,1},{1,0},{2,3},{3,2},{4,5},{5,4},{6,7},{7,6},{8,9},{9,8},{10,11... | collective-permute-start | bytes 7077896 | tf_op jit(solution)/shard_map/ppermute | solution.py:868
  94.9 28.2 %collective-permute-start.3 = (bf16[8,96,768]{2,1,0:T(8,128)(2,1)S(1)}, bf16[8,96,768]{2,1,0:T(8,128)(2,1)S(1)}, u32[]{:S(2)}, u32[]{:S(2)}) collective-permute-start(bf16[8,96,768]{2,1,0:T(8,128)(2,1)S(1)} %get-tuple-element.175), channel_id=1, source_target_pairs={{0,2},{1,3},{2,0},{3,1},{4,6},{5,7},{6,4},{7,5},{8,10},{9,11},{10,... | collective-permute-start | bytes 3538952 | tf_op jit(solution)/shard_map/ppermute | solution.py:868
  95.4 27.7 %collective-permute-start.4 = (bf16[8,24,3072]{2,1,0:T(8,128)(2,1)S(1)}, bf16[8,24,3072]{2,1,0:T(8,128)(2,1)S(1)}, u32[]{:S(2)}, u32[]{:S(2)}) collective-permute-start(bf16[8,24,3072]{2,1,0:T(8,128)(2,1)S(1)} %get-tuple-element.177), channel_id=1, source_target_pairs={{0,4},{1,5},{2,6},{3,7},{4,0},{5,1},{6,2},{7,3},{8,12},{9,13},{10,... | collective-permute-start | bytes 3538952 | tf_op jit(solution)/shard_map/ppermute | solution.py:868
  123.0 18.7 %collective-permute-start.7 = (bf16[16,24,1536]{2,1,0:T(8,128)(2,1)}, bf16[16,24,1536]{2,1,0:T(8,128)(2,1)S(1)}, u32[]{:S(2)}, u32[]{:S(2)}) collective-permute-start(bf16[16,24,1536]{2,1,0:T(8,128)(2,1)} %bitcast.93), channel_id=1, source_target_pairs={{0,1},{1,0},{2,3},{3,2},{4,5},{5,4},{6,7},{7,6},{8,9},{9,8},{10,11... | collective-permute-start | bytes 3538952 | tf_op jit(solution)/shard_map/ppermute | solution.py:868
  124.8 17.0 %collective-permute-start.5 = (bf16[4,96,768]{2,1,0:T(8,128)(2,1)S(1)}, bf16[4,96,768]{2,1,0:T(8,128)(2,1)S(1)}, u32[]{:S(2)}, u32[]{:S(2)}) collective-permute-start(bf16[4,96,768]{2,1,0:T(8,128)(2,1)S(1)} %get-tuple-element.192), channel_id=1, source_target_pairs={{0,4},{1,5},{2,6},{3,7},{4,0},{5,1},{6,2},{7,3},{8,12},{9,13},{10,... | collective-permute-start | bytes 1769480 | tf_op jit(solution)/shard_map/ppermute | solution.py:868
  126.0 15.8 %collective-permute-start.6 = (bf16[4,24,3072]{2,1,0:T(8,128)(2,1)S(1)}, bf16[4,24,3072]{2,1,0:T(8,128)(2,1)S(1)}, u32[]{:S(2)}, u32[]{:S(2)}) collective-permute-start(bf16[4,24,3072]{2,1,0:T(8,128)(2,1)S(1)} %get-tuple-element.194), channel_id=1, source_target_pairs={{0,8},{8,0},{16,24},{24,16},{1,9},{9,1},{17,25},{25,17},{2,10},{10... | collective-permute-start | bytes 1769480 | tf_op jit(solution)/shard_map/ppermute | solution.py:868
  141.7 17.6 %collective-permute-start.10 = (bf16[16,24,1536]{2,1,0:T(8,128)(2,1)}, bf16[16,24,1536]{2,1,0:T(8,128)(2,1)S(1)}, u32[]{:S(2)}, u32[]{:S(2)}) collective-permute-start(bf16[16,24,1536]{2,1,0:T(8,128)(2,1)} %bitcast.92), channel_id=1, source_target_pairs={{0,1},{1,0},{2,3},{3,2},{4,5},{5,4},{6,7},{7,6},{8,9},{9,8},{10,11... | collective-permute-start | bytes 3538952 | tf_op jit(solution)/shard_map/ppermute | solution.py:868
  152.0 18.3 %collective-permute-start.15 = (bf16[64,1664]{1,0:T(8,128)(2,1)}, bf16[64,1664]{1,0:T(8,128)(2,1)}, u32[]{:S(2)}, u32[]{:S(2)}) collective-permute-start(bf16[64,1664]{1,0:T(8,128)(2,1)} %get-tuple-element.223), channel_id=1, source_target_pairs={{1,0},{2,1},{3,2},{4,3},{5,4},{6,5},{7,6},{9,8},{10,9},{11,10},{12... | collective-permute-start | bytes 638984 | tf_op jit(solution)/shard_map/ppermute | solution.py:143
  153.3 17.0 %all-to-all-start.1 = ((bf16[8,8,1664]{2,1,0:T(8,128)(2,1)}), bf16[8,8,1664]{2,1,0:T(8,128)(2,1)}, u32[]{:S(2)}, u32[]{:S(2)}) async-start(bf16[8,8,1664]{2,1,0:T(8,128)(2,1)} %bitcast.84), calls=%async_computation.1 | async-start | bytes 425984 | tf_op jit(solution)/shard_map/all_to_all | solution.py:1141
  157.4 27.6 %collective-permute-start.13 = (bf16[8,24,1536]{2,1,0:T(8,128)(2,1)S(1)}, bf16[8,24,1536]{2,1,0:T(8,128)(2,1)S(1)}, u32[]{:S(2)}, u32[]{:S(2)}) collective-permute-start(bf16[8,24,1536]{2,1,0:T(8,128)(2,1)S(1)} %get-tuple-element.218), channel_id=1, source_target_pairs={{0,2},{1,3},{2,0},{3,1},{4,6},{5,7},{6,4},{7,5},{8,10},{9,11},{10,... | collective-permute-start | bytes 1769480 | tf_op jit(solution)/shard_map/ppermute | solution.py:868
  165.9 19.0 %collective-permute-start.14 = (bf16[8,24,1536]{2,1,0:T(8,128)(2,1)S(1)}, bf16[8,24,1536]{2,1,0:T(8,128)(2,1)S(1)}, u32[]{:S(2)}, u32[]{:S(2)}) collective-permute-start(bf16[8,24,1536]{2,1,0:T(8,128)(2,1)S(1)} %get-tuple-element.220), channel_id=1, source_target_pairs={{0,4},{1,5},{2,6},{3,7},{4,0},{5,1},{6,2},{7,3},{8,12},{9,13},{10,... | collective-permute-start | bytes 1769480 | tf_op jit(solution)/shard_map/ppermute | solution.py:868
  167.4 17.5 %collective-permute-start.11 = (bf16[1,96,768]{2,1,0:T(8,128)(2,1)}, bf16[1,96,768]{2,1,0:T(8,128)(2,1)S(1)}, u32[]{:S(2)}, u32[]{:S(2)}) collective-permute-start(bf16[1,96,768]{2,1,0:T(8,128)(2,1)} %get-tuple-element.214), channel_id=1, source_target_pairs={{0,16},{8,24},{16,0},{24,8},{1,17},{9,25},{17,1},{25,9},{2,18},{10... | collective-permute-start | bytes 442376 | tf_op jit(solution)/shard_map/ppermute | solution.py:868
  184.8 16.1 %collective-permute-start.20 = (f32[24,768]{1,0:T(8,128)S(1)}, f32[24,768]{1,0:T(8,128)S(1)}, u32[]{:S(2)}, u32[]{:S(2)}) collective-permute-start(f32[24,768]{1,0:T(8,128)S(1)} %pad_maximum_fusion.refs_13_), channel_id=1, source_target_pairs={{0,1},{1,0},{2,3},{3,2},{4,5},{5,4},{6,7},{7,6},{8,9},{9,8},{10,11... | collective-permute-start | bytes 221192 | tf_op jit(solution)/shard_map/ppermute | solution.py:868
  186.9 15.4 %collective-permute-start.19 = (bf16[4,24,1536]{2,1,0:T(8,128)(2,1)S(1)}, bf16[4,24,1536]{2,1,0:T(8,128)(2,1)S(1)}, u32[]{:S(2)}, u32[]{:S(2)}) collective-permute-start(bf16[4,24,1536]{2,1,0:T(8,128)(2,1)S(1)} %get-tuple-element.244), channel_id=1, source_target_pairs={{0,8},{8,0},{16,24},{24,16},{1,9},{9,1},{17,25},{25,17},{2,10},{10... | collective-permute-start | bytes 884744 | tf_op jit(solution)/shard_map/ppermute | solution.py:868
  206.5 16.1 %collective-permute-start.21 = (bf16[2,96,768]{2,1,0:T(8,128)(2,1)S(1)}, bf16[2,96,768]{2,1,0:T(8,128)(2,1)S(1)}, u32[]{:S(2)}, u32[]{:S(2)}) collective-permute-start(bf16[2,96,768]{2,1,0:T(8,128)(2,1)S(1)} %bitcast.69), channel_id=1, source_target_pairs={{0,8},{8,0},{16,24},{24,16},{1,9},{9,1},{17,25},{25,17},{2,10},{10... | collective-permute-start | bytes 884744 | tf_op jit(solution)/shard_map/ppermute | solution.py:868
  206.5 16.1 %collective-permute-start.22 = (bf16[2,24,3072]{2,1,0:T(8,128)(2,1)S(1)}, bf16[2,24,3072]{2,1,0:T(8,128)(2,1)S(1)}, u32[]{:S(2)}, u32[]{:S(2)}) collective-permute-start(bf16[2,24,3072]{2,1,0:T(8,128)(2,1)S(1)} %bitcast.71), channel_id=1, source_target_pairs={{0,2},{1,3},{2,0},{3,1},{4,6},{5,7},{6,4},{7,5},{8,10},{9,11},{10,... | collective-permute-start | bytes 884744 | tf_op jit(solution)/shard_map/ppermute | solution.py:868
  227.8 17.2 %collective-permute-start.28 = (bf16[4,96,768]{2,1,0:T(8,128)(2,1)S(1)}, bf16[4,96,768]{2,1,0:T(8,128)(2,1)S(1)}, u32[]{:S(2)}, u32[]{:S(2)}) collective-permute-start(bf16[4,96,768]{2,1,0:T(8,128)(2,1)S(1)} %bitcast.61), channel_id=1, source_target_pairs={{0,4},{1,5},{2,6},{3,7},{4,0},{5,1},{6,2},{7,3},{8,12},{9,13},{10,... | collective-permute-start | bytes 1769480 | tf_op jit(solution)/shard_map/ppermute | solution.py:868
  228.3 16.7 %collective-permute-start.29 = (bf16[4,24,3072]{2,1,0:T(8,128)(2,1)S(1)}, bf16[4,24,3072]{2,1,0:T(8,128)(2,1)S(1)}, u32[]{:S(2)}, u32[]{:S(2)}) collective-permute-start(bf16[4,24,3072]{2,1,0:T(8,128)(2,1)S(1)} %bitcast.63), channel_id=1, source_target_pairs={{0,8},{8,0},{16,24},{24,16},{1,9},{9,1},{17,25},{25,17},{2,10},{10... | collective-permute-start | bytes 1769480 | tf_op jit(solution)/shard_map/ppermute | solution.py:868
  246.8 30.1 %collective-permute-start.37 = (bf16[8,96,768]{2,1,0:T(8,128)(2,1)S(1)}, bf16[8,96,768]{2,1,0:T(8,128)(2,1)S(1)}, u32[]{:S(2)}, u32[]{:S(2)}) collective-permute-start(bf16[8,96,768]{2,1,0:T(8,128)(2,1)S(1)} %bitcast.53), channel_id=1, source_target_pairs={{0,2},{1,3},{2,0},{3,1},{4,6},{5,7},{6,4},{7,5},{8,10},{9,11},{10,... | collective-permute-start | bytes 3538952 | tf_op jit(solution)/shard_map/ppermute | solution.py:868
  246.8 30.1 %collective-permute-start.38 = (bf16[8,24,3072]{2,1,0:T(8,128)(2,1)S(1)}, bf16[8,24,3072]{2,1,0:T(8,128)(2,1)}, u32[]{:S(2)}, u32[]{:S(2)}) collective-permute-start(bf16[8,24,3072]{2,1,0:T(8,128)(2,1)S(1)} %bitcast.55), channel_id=1, source_target_pairs={{0,4},{1,5},{2,6},{3,7},{4,0},{5,1},{6,2},{7,3},{8,12},{9,13},{10,... | collective-permute-start | bytes 3538952 | tf_op jit(solution)/shard_map/ppermute | solution.py:868
  248.3 28.5 %collective-permute-start.39 = (bf16[4,24,1536]{2,1,0:T(8,128)(2,1)}, bf16[4,24,1536]{2,1,0:T(8,128)(2,1)}, u32[]{:S(2)}, u32[]{:S(2)}) collective-permute-start(bf16[4,24,1536]{2,1,0:T(8,128)(2,1)} %bitcast.33.refs_5_), channel_id=1, source_target_pairs={{0,4},{1,5},{2,6},{3,7},{4,0},{5,1},{6,2},{7,3},{8,12},{9,13},{10,... | collective-permute-start | bytes 884744 | tf_op jit(solution)/shard_map/ppermute | solution.py:868
  248.8 28.1 %collective-permute-start.40 = (bf16[4,24,1536]{2,1,0:T(8,128)(2,1)}, bf16[4,24,1536]{2,1,0:T(8,128)(2,1)}, u32[]{:S(2)}, u32[]{:S(2)}) collective-permute-start(bf16[4,24,1536]{2,1,0:T(8,128)(2,1)} %bitcast.34.refs_7_), channel_id=1, source_target_pairs={{0,8},{8,0},{16,24},{24,16},{1,9},{9,1},{17,25},{25,17},{2,10},{10... | collective-permute-start | bytes 884744 | tf_op jit(solution)/shard_map/ppermute | solution.py:868
  250.0 48.6 %collective-permute-start.36 = (f32[24,768]{1,0:T(8,128)}, f32[24,768]{1,0:T(8,128)S(1)}, u32[]{:S(2)}, u32[]{:S(2)}) collective-permute-start(f32[24,768]{1,0:T(8,128)} %copy-done), channel_id=1, source_target_pairs={{0,16},{8,24},{16,0},{24,8},{1,17},{9,25},{17,1},{25,9},{2,18},{10... | collective-permute-start | bytes 221192 | tf_op jit(solution)/shard_map/ppermute | solution.py:868
  (45 other events, 469.9 us)

commit v3 on v2

--- a/solution.py
+++ b/solution.py
@@ -102,7 +102,7 @@
 
 
 def launch(kernel, name, work, grid, in_specs, out_specs, out_shape, scratch, limit, operands, after=(), prefetch=(),
-           free=(), aliases=None):
+           free=(), aliases=None, held=()):
     count, extra = len(operands), len(after)
 
     def body(*refs):
@@ -128,7 +128,9 @@
             out_specs=list(out_specs) + [same(*TOKEN)],
             scratch_shapes=scratch,
         ),
-        out_shape=[shape if kept else pltpu.HBM(shape.shape, shape.dtype) for shape in shapes] + [pltpu.HBM(TOKEN, f32)],
+        out_shape=[
+            shape if kept and at not in held else pltpu.HBM(shape.shape, shape.dtype) for at, shape in enumerate(shapes)
+        ] + [pltpu.HBM(TOKEN, f32)],
         compiler_params=pltpu.CompilerParams(vmem_limit_bytes=limit * 2**20),
         cost_estimate=pl.CostEstimate(flops=int(work * 5e9), bytes_accessed=2**20, transcendentals=0),
         input_output_aliases=aliases or {},
@@ -381,39 +383,64 @@
     )
 
 
+class Block:
+    def __init__(self, groups, loaded, k_h, v_h, score_h, rim_h, far_h, score_ref, keys, values, model, rows):
+        self.loads = loads = Moves(loaded)
+        slots, width = far_h.shape[0], keys.shape[2]
+        self.near, self.own, self.far = pl.ds(0, WIN), pl.ds(WIN, rows), pl.ds(WIN + rows, slots)
+        scores = pl.ds(3 * model, LANES)
+        self.first = [
+            loads.add(source, target)
+            for source, target in (
+                (score_h, score_ref.at[self.own, :]), (rim_h.at[:, scores], score_ref.at[self.near, :]),
+                (far_h.at[:, scores], score_ref.at[self.far, :]),
+            )
+        ]
+        self.second = []
+        for at, group in enumerate(groups):
+            cols, value_cols = pl.ds(group * width, width), pl.ds(model + group * width, width)
+            self.second.append(
+                [
+                    loads.add(source, target)
+                    for source, target in (
+                        (k_h.at[:, cols], keys.at[at, self.own, :]), (rim_h.at[:, cols], keys.at[at, self.near, :]),
+                        (far_h.at[:, cols], keys.at[at, self.far, :]), (v_h.at[:, cols], values.at[at, self.own, :]),
+                        (rim_h.at[:, value_cols], values.at[at, self.near, :]),
+                        (far_h.at[:, value_cols], values.at[at, self.far, :]),
+                    )
+                ]
+            )
+
+    def add(self, at, source, target):
+        self.second[at].append(self.loads.add(source, target))
+
+
+def gates_of(gate, spread, place, gate_ref):
+    gate_ref[...] = sum(nn(part, spread) for part in three_parts(gate))
+    gate_ref[0:WIN, :] = jnp.where(place == 0, very_low, gate_ref[0:WIN, :])
+
+
 def attend_back_kernel(
-    heads, head_size, unroll, group, last, place_ref, q_h, k_h, v_h, grad_h, total_ref, score_h, rim_h, far_h, normed_h,
+    heads, head_size, unroll, groups, last, place_ref, q_h, k_h, v_h, grad_h, total_ref, score_h, rim_h, far_h, normed_h,
     *refs,
 ):
     refs = list(refs)
-    earlier = [refs.pop(0) for _ in range(5)] if group else []
-    beside_refs = [refs.pop(0) for _ in range(2)] if group else []
+    earlier = [refs.pop(0) for _ in range(5)] if groups[0] else []
+    beside_refs = [refs.pop(0) for _ in range(2)] if groups[0] else []
     dq_h, dk_h, dv_h, ds_ref, rim_out, far_out, rim_ds, far_ds, send, keep = refs[:10]
-    q_ref, grad_ref, score_ref, dq_ref, keys, values, gate_ref, dkeys, dvalues, dscore, normed, loaded, stored = refs[10:]
+    q_ref, grad_ref, score_ref, dq_ref, keys, values, gate_refs, all_dkeys, all_dvalues, all_dscore, normed = refs[10:21]
+    loaded, stored = refs[21:]
     model = normed.shape[1]
     place = place_ref[0]
-    rows, width = q_ref.shape
+    _, rows, width = q_ref.shape
     slots = far_h.shape[0]
-    cols, value_cols = pl.ds(group * width, width), pl.ds(model + group * width, width)
-    scores, normed_cols = pl.ds(3 * model, LANES), pl.ds(2 * model, model)
-    near, own, far = pl.ds(0, WIN), pl.ds(WIN, rows), pl.ds(WIN + rows, slots)
-    loads = Moves(loaded)
-    first = [
-        loads.add(source, target)
-        for source, target in (
-            (score_h, score_ref.at[own, :]), (rim_h.at[:, scores], score_ref.at[near, :]),
-            (far_h.at[:, scores], score_ref.at[far, :]),
-        )
-    ]
-    second = [
-        loads.add(source, target)
-        for source, target in (
-            (q_h.at[:, cols], q_ref), (grad_h.at[:, cols], grad_ref), (k_h.at[:, cols], keys.at[own, :]),
-            (rim_h.at[:, cols], keys.at[near, :]), (far_h.at[:, cols], keys.at[far, :]),
-            (v_h.at[:, cols], values.at[own, :]), (rim_h.at[:, value_cols], values.at[near, :]),
-            (far_h.at[:, value_cols], values.at[far, :]),
-        )
-    ]
+    block = Block(groups, loaded, k_h, v_h, score_h, rim_h, far_h, score_ref, keys, values, model, rows)
+    near, own, far, loads = block.near, block.own, block.far, block.loads
+    for g, group in enumerate(groups):
+        cols = pl.ds(group * width, width)
+        block.add(g, q_h.at[:, cols], q_ref.at[g])
+        block.add(g, grad_h.at[:, cols], grad_ref.at[g])
+    normed_cols = pl.ds(2 * model, model)
     third = [
         loads.add(source, target)
         for source, target in (
@@ -421,106 +448,117 @@
             (far_h.at[:, normed_cols], normed.at[far, :]),
         )
     ]
-    loads.start(*first, *second, *third)
-    for ref in (dkeys, dvalues, dscore):
+    loads.start(*range(len(loads.made)))
+    for ref in (all_dkeys, all_dvalues, all_dscore):
         ref[...] = jnp.zeros_like(ref)
-    loads.wait(*first)
-    gather = head_spread(group, head_size, width)
+    loads.wait(*block.first)
     gate = jax.nn.log_sigmoid(score_ref[...].astype(f32))
-    gate_ref[...] = sum(nn(part, gather) for part in three_parts(gate))
-    gate_ref[0:WIN, :] = jnp.where(place == 0, very_low, gate_ref[0:WIN, :])
     near_ok = near_bias(width)
     far_pos = jnp.broadcast_to(far_positions(score_ref[far, :], heads, rows, slots // PICK), (slots, LANES))
-    loads.wait(*second)
-
-    @pl.loop(0, rows // WIN, unroll=unroll)
-    def _(i):
-        at = pl.ds(pl.multiple_of(i * WIN, WIN), WIN)
-        after = pl.ds(pl.multiple_of(i * WIN + WIN, WIN), WIN)
-        span = pl.ds(pl.multiple_of(i * WIN, WIN), 2 * WIN)
-        keys_cat = jnp.concatenate([keys[span, :], keys[far, :]], axis=0)
-        values_cat = jnp.concatenate([values[span, :], values[far, :]], axis=0)
-        stack = stack_heads(q_ref[at, :], head_size, 1.0 / math.sqrt(head_size))
-        grad_stack = stack_heads(grad_ref[at, :], head_size, 1.0)
-        logit = tile_logits(i, keys_cat, stack, gate_ref, far_pos, place, rows, near_ok)
-        prob = jnp.exp(logit - total_ref[group, pl.ds(i, 1), :])
-        grad_prob = nt(values_cat, grad_stack)
-        delta = jnp.sum(prob * grad_prob, axis=0, keepdims=True)
-        grad_logit = prob * (grad_prob - delta)
-        low = grad_logit.astype(bf16)
-        dq_ref[at, :] = (pick_heads(tn(low, keys_cat), head_size) * (1.0 / math.sqrt(head_size))).astype(bf16)
-        for ref, update in (
-            (dkeys, nn(low, stack)),
-            (dvalues, nn(prob.astype(bf16), grad_stack)),
-            (dscore, grad_logit),
-        ):
-            ref[at, :] += update[:WIN]
-            ref[after, :] = update[WIN : 2 * WIN]
-            ref[far, :] += update[2 * WIN :]
-
     stores = Moves(stored)
-    for source, target in ((dq_ref, dq_h), (dkeys.at[own, :], dk_h), (dvalues.at[own, :], dv_h)):
-        stores.start(stores.add(source, target))
-    loads.wait(*third)
     mine = place % 2
     half = model // 2
-    joint = jnp.concatenate(
-        [tn(normed[own, :], dq_ref[...])]
-        + [tn(normed[...], ref[...].astype(bf16)) for ref in (dkeys, dvalues)],
-        axis=1,
-    ).astype(bf16)
-    top, low = joint[:half], joint[half:]
     start = 0
-    if group:
+    if beside_refs:
         start = beside_refs[0].shape[1]
         send[:, :start] = beside_refs[0][...]
         keep[:, :start] = beside_refs[1][...]
-    send[:, start:] = jnp.where(mine == 0, low, top)
-    keep[:, start:] = jnp.where(mine == 0, top, low)
-    if group:
         for out, old in zip((rim_out, far_out), earlier[:2]):
             out[...] = old[...]
-    for out, part in ((rim_out, near), (far_out, far)):
-        for base, ref in ((0, dkeys), (model, dvalues)):
-            out[:, base + group * width : base + (group + 1) * width] = ref[part, :].astype(bf16)
-    for number, (out_ref, part) in enumerate(((rim_ds, near), (far_ds, far), (ds_ref, own))):
-        sums = dscore[part, :]
-        high = sums.astype(bf16)
-        rest = (sums - high.astype(f32)).astype(bf16)
-        update = (nt(high, gather) + nt(rest, gather)) * jax.nn.sigmoid(-score_ref[part, :].astype(f32))
-        out_ref[...] = update + earlier[2 + number][...] if group else update
+    for g, group in enumerate(groups):
+        gate_ref, dkeys, dvalues, dscore = (ref.at[g] for ref in (gate_refs, all_dkeys, all_dvalues, all_dscore))
+        gather = head_spread(group, head_size, width)
+        gates_of(gate, gather, place, gate_ref)
+        loads.wait(*block.second[g])
+
+        @pl.loop(0, rows // WIN, unroll=unroll)
+        def _(i):
+            at = pl.ds(pl.multiple_of(i * WIN, WIN), WIN)
+            after = pl.ds(pl.multiple_of(i * WIN + WIN, WIN), WIN)
+            span = pl.ds(pl.multiple_of(i * WIN, WIN), 2 * WIN)
+            keys_cat = jnp.concatenate([keys[g, span, :], keys[g, far, :]], axis=0)
+            values_cat = jnp.concatenate([values[g, span, :], values[g, far, :]], axis=0)
+            stack = stack_heads(q_ref[g, at, :], head_size, 1.0 / math.sqrt(head_size))
+            grad_stack = stack_heads(grad_ref[g, at, :], head_size, 1.0)
+            logit = tile_logits(i, keys_cat, stack, gate_ref, far_pos, place, rows, near_ok)
+            prob = jnp.exp(logit - total_ref[group, pl.ds(i, 1), :])
+            grad_prob = nt(values_cat, grad_stack)
+            delta = jnp.sum(prob * grad_prob, axis=0, keepdims=True)
+            grad_logit = prob * (grad_prob - delta)
+            low = grad_logit.astype(bf16)
+            dq = pick_heads(tn(low, keys_cat), head_size) * (1.0 / math.sqrt(head_size))
+            dq_ref[g, at, :] = dq.astype(bf16)
+            for ref, update in (
+                (dkeys, nn(low, stack)),
+                (dvalues, nn(prob.astype(bf16), grad_stack)),
+                (dscore, grad_logit),
+            ):
+                ref[at, :] += update[:WIN]
+                ref[after, :] = update[WIN : 2 * WIN]
+                ref[far, :] += update[2 * WIN :]
+
+        to = pl.ds(g * width, width)
+        for source, target in ((dq_ref.at[g], dq_h), (dkeys.at[own, :], dk_h), (dvalues.at[own, :], dv_h)):
+            stores.start(stores.add(source, target.at[:, to]))
+        if g == 0:
+            loads.wait(*third)
+        joint = jnp.concatenate(
+            [tn(normed[own, :], dq_ref[g])]
+            + [tn(normed[...], ref[...].astype(bf16)) for ref in (dkeys, dvalues)],
+            axis=1,
+        ).astype(bf16)
+        top, low = joint[:half], joint[half:]
+        span = slice(start + 3 * width * g, start + 3 * width * (g + 1))
+        send[:, span] = jnp.where(mine == 0, low, top)
+        keep[:, span] = jnp.where(mine == 0, top, low)
+        for out, part in ((rim_out, near), (far_out, far)):
+            for base, ref in ((0, dkeys), (model, dvalues)):
+                out[:, base + group * width : base + (group + 1) * width] = ref[part, :].astype(bf16)
+        for number, (out_ref, part) in enumerate(((rim_ds, near), (far_ds, far), (ds_ref, own))):
+            sums = dscore[part, :]
+            high = sums.astype(bf16)
+            rest = (sums - high.astype(f32)).astype(bf16)
+            update = (nt(high, gather) + nt(rest, gather)) * jax.nn.sigmoid(-score_ref[part, :].astype(f32))
+            if g:
+                out_ref[...] += update
+            else:
+                out_ref[...] = update + earlier[2 + number][...] if earlier else update
     if last:
         rim_out[:, 2 * model :] = rim_ds[...].astype(bf16)
         far_out[:, 2 * model :] = far_ds[...].astype(bf16)
     stores.wait(*range(len(stores.made)))
 
 
-def attend_back(place, q, k, v, grad, total, score, rim, far, normed, heads, group, earlier, joined, after=(), unroll=4):
+def attend_back(place, q, k, v, grad, total, score, rim, far, normed, heads, groups, earlier, joined, after=(), unroll=4):
     rows, model = q.shape
     slots = far.shape[0]
     width = PACK * WIN
-    groups = model // width
+    count = len(groups)
     channels = 2 * model + LANES
     S = jax.ShapeDtypeStruct
-    half = (model // 2, 3 * width + (joined[0].shape[1] if joined else 0))
+    half = (model // 2, 3 * width * count + (joined[0].shape[1] if joined else 0))
     ext = WIN + rows + slots
     V = pltpu.VMEM
     out = launch(
-        functools.partial(attend_back_kernel, heads, WIN, unroll, group, group == groups - 1),
-        "attend_back", 13, (),
+        functools.partial(attend_back_kernel, heads, WIN, unroll, groups, groups[-1] == model // width - 1),
+        "attend_back", 13 * count, (),
         [pl.BlockSpec(memory_space=pltpu.SMEM)] + [anywhere()] * 4 + [vmem()] + [anywhere()] * 4
         + [vmem()] * (len(earlier) + len(joined)),
         [anywhere()] * 3 + [vmem()] * 7,
         [
-            S((rows, width), bf16), S((rows, width), f32), S((rows, width), f32), S((rows, LANES), f32),
-            S((WIN, channels), bf16), S((slots, channels), bf16), S((WIN, LANES), f32), S((slots, LANES), f32),
+            S((rows, count * width), bf16), S((rows, count * width), f32), S((rows, count * width), f32),
+            S((rows, LANES), f32), S((WIN, channels), bf16), S((slots, channels), bf16), S((WIN, LANES), f32),
+            S((slots, LANES), f32),
         ] + [S(half, bf16)] * 2,
         [
-            V((rows, width), bf16), V((rows, width), bf16), V((ext, LANES), bf16), V((rows, width), bf16),
-            V((ext, width), bf16), V((ext, width), bf16),
-        ] + [V((ext, width), f32)] * 4
-        + [V((ext, model), bf16), pltpu.SemaphoreType.DMA((14,)), pltpu.SemaphoreType.DMA((3,))],
-        30, (place, q, k, v, grad, total, score, rim, far, normed, *earlier, *joined), after,
+            V((count, rows, width), bf16), V((count, rows, width), bf16), V((ext, LANES), bf16),
+            V((count, rows, width), bf16), V((count, ext, width), bf16), V((count, ext, width), bf16),
+        ] + [V((count, ext, width), f32)] * 4
+        + [
+            V((ext, model), bf16), pltpu.SemaphoreType.DMA((6 + 8 * count,)), pltpu.SemaphoreType.DMA((3 * count,)),
+        ],
+        32 if count == 1 else 44,
+        (place, q, k, v, grad, total, score, rim, far, normed, *earlier, *joined), after,
     )
     dq, dk, dv, ds, rim_out, far_out, rim_ds, far_ds, send, keep, token = out
     return (dq, dk, dv), (rim_out, far_out, rim_ds, far_ds, ds), (send, keep), token
@@ -588,7 +626,7 @@
             grad = (back * slope).astype(bf16)
             grad_pre[here, at] = grad
             sums.append(column_sums(grad.astype(f32)))
-        total = jnp.concatenate(sums, axis=1)
+        total = jnp.concatenate(sums, axis=0)
         if leading:
             sums_ref[...] = total
         else:
@@ -641,11 +679,11 @@
 
 
 def feed(
-    mine, mixed, tokens, cot, out_weight, out_bias, gain, shift, expand, expand_bias, reduce, tile=512, pieces=4, block=512,
+    mine, mixed, tokens, cot, out_weight, out_bias, gain, shift, expand, expand_bias, reduce, tile=512, block=512,
 ):
     rows, width = tokens.shape
     inner = expand.shape[1]
-    steps = rows // tile
+    steps, pieces = rows // tile, inner // width
     S = jax.ShapeDtypeStruct
     B = pltpu.VMEM
     return launch(
@@ -654,7 +692,7 @@
         [anywhere()] * 6 + [vmem()] * 4,
         [anywhere()] * 3 + [vmem()] + [anywhere()] * 4,
         [
-            S((rows, width), f32), S((rows, inner), bf16), S((rows, inner), bf16), S((1, inner), f32),
+            S((rows, width), f32), S((rows, inner), bf16), S((rows, inner), bf16), S((pieces, inner // pieces), f32),
             S((inner // 2, width), bf16), S((inner // 2, width), bf16),
             S((width // 2, inner), bf16), S((width // 2, inner), bf16),
         ],
@@ -800,10 +838,10 @@
 
 def join_kernel(
     steps, groups, tokens_ref, resid_ref, ds_ref, rim_ref, far_ref, picks_ref, gain_ref, shift_ref,
-    joint_ref, score_weight_ref, *refs,
+    joint_ref, score_weight_ref, sums_two_ref, expand_sums_ref, *refs,
 ):
     dq_refs, dk_refs, dv_refs = (refs[at * groups : (at + 1) * groups] for at in range(3))
-    token_ref, sums_ref, score_grad_ref = refs[3 * groups :]
+    token_ref, small_ref = refs[3 * groups :]
     step = pl.program_id(0)
     tile, width = tokens_ref.shape
     heads = score_weight_ref.shape[0]
@@ -832,34 +870,48 @@
         + nn(ds[:, :heads], score_weight_ref[...])
     )
     token_ref[...] = resid_ref[...] + normalise_back(grad_normed, unit, inverse, gain)
-    accumulate(
-        sums_ref,
-        jnp.concatenate(
-            [
-                column_sums(grad_normed * unit),
-                column_sums(grad_normed),
-                column_sums(dq.astype(f32)),
-                column_sums(dv.astype(f32)),
-            ],
-            axis=0,
-        ),
-    )
-    accumulate(score_grad_ref, tn(ds, normed)[: score_grad_ref.shape[0]])
-
-
-def join(tokens, resid, dqs, dks, dvs, ds, rim, far, picks, gain, shift, joint, score_weight, after=(), tile=256):
+    sums = jnp.concatenate(
+        [
+            column_sums(grad_normed * unit),
+            column_sums(grad_normed),
+            column_sums(dq.astype(f32)),
+            column_sums(dv.astype(f32)),
+        ],
+        axis=0,
+    )
+    score_grad = tn(ds, normed)[:heads]
+    past = 8 + expand_sums_ref.shape[0]
+
+    @pl.when(step == 0)
+    def _():
+        small_ref[0:4, :] = sums
+        small_ref[4:8, :] = sums_two_ref[...]
+        small_ref[8:past, :] = expand_sums_ref[...]
+        small_ref[past : past + heads, :] = score_grad
+
+    @pl.when(step > 0)
+    def _():
+        small_ref[0:4, :] += sums
+        small_ref[past : past + heads, :] += score_grad
+
+
+def join(
+    tokens, resid, dqs, dks, dvs, ds, rim, far, picks, gain, shift, joint, score_weight, sums_two, expand_sums, after=(),
+    tile=256,
+):
     rows, width = tokens.shape
     heads = score_weight.shape[0]
+    count = 8 + expand_sums.shape[0] + heads
     S = jax.ShapeDtypeStruct
     return launch(
         functools.partial(join_kernel, rows // tile, len(dqs)), "join", 14, (rows // tile,),
         [tiled(tile, width)] * 2 + [
             tiled(tile, LANES), same(*rim.shape), same(*far.shape), same(*picks.shape), same(width), same(width),
-            same(*joint.shape), same(*score_weight.shape),
+            same(*joint.shape), same(*score_weight.shape), same(*sums_two.shape), same(*expand_sums.shape),
         ] + [tiled(tile, part.shape[1]) for part in (*dqs, *dks, *dvs)],
-        [tiled(tile, width), same(4, width), same(heads, width)],
-        [S((rows, width), f32), S((4, width), f32), S((heads, width), f32)],
-        [], 28, (tokens, resid, ds, rim, far, picks, gain, shift, joint, score_weight, *dqs, *dks, *dvs), after,
+        [tiled(tile, width), same(count, width)],
+        [S((rows, width), f32), S((count, width), f32)],
+        [], 28, (tokens, resid, ds, rim, far, picks, gain, shift, joint, score_weight, sums_two, expand_sums, *dqs, *dks, *dvs), after,
     )
 
 
@@ -904,7 +956,7 @@
 
 class Chain:
     def __init__(self, send, keep, order):
-        self.order, self.level, self.down = order, 0, True
+        self.order, self.level, self.down, self.held = order, 0, True, True
         half = 2 ** (len(order) - 1)
         self.send, self.keep = cut(send, half), cut(keep, half)
         self.mine = [side(*where).astype(jnp.int32) for where in order]
@@ -942,7 +994,8 @@
                 out[which] = refs.pop(0)[...]
 
 
-def advance(chains, after=()):
+def advance(chains, after=(), hold=False):
+    held = []
     plan, operands, in_specs, out_specs, shapes, bits, free = [], [], [], [], [], [], []
     depth = len(chains[0].order)
     for chain in chains:
@@ -975,14 +1028,16 @@
             which = len(bits)
             bits.append(chain.mine[chain.level + 1])
             places = len(operands)
-            free += [places + 1, places + 3] if chain.level == 0 else range(places, places + 4)
+            free += [places + 1, places + 3] if chain.held else range(places, places + 4)
+            chain.held = hold
+            held += [len(shapes) + 1] if hold else []
             for other in (True, False):
                 operands += [chain.keep, got]
                 in_specs += [half_of(which, other, block, tail)] * 2
             out_specs += [tiled(block, *tail)] * 2
             shapes += [S((size,) + tail, bf16)] * 2
         elif kind == "close":
-            free += [len(operands), len(operands) + 1]
+            free += [len(operands) + 1] if chain.held else [len(operands), len(operands) + 1]
             operands += [chain.keep, got]
             in_specs += [tiled(block, *tail)] * 2
             out_specs += [tiled(block, *tail)]
@@ -996,7 +1051,7 @@
     bits = jnp.stack(bits) if bits else jnp.zeros((1,), jnp.int32)
     outs = launch(
         functools.partial(advance_kernel, plan), "advance", 2, (steps,), in_specs, out_specs, shapes, [], 20, operands,
-        after, (bits,), free,
+        after, (bits,), free, None, held,
     )
     for chain, kind in zip(chains, plan):
         if kind == "split":
@@ -1130,32 +1185,29 @@
     big = [reduced, expanded]
     back = functools.partial(attend_back, here, q, k, v, grad_mixed, total, score, rim, far, normed, heads)
     stage = advance(big, (stage,))
-    grads_zero, carried, joined, stage = back(0, (), (), (stage,))
-    grads_one, carried, joined, stage = back(1, carried, joined, (stage,))
+    grads_one, carried, joined, stage = back((0, 1), (), (), (stage,))
     one = Chain(*joined, first)
-    stage = advance(big, (stage,))
-    grads_two, carried, joined, stage = back(2, carried, tuple(out_halves), (stage,))
+    stage = advance(big, (stage,), True)
+    grads_two, carried, joined, stage = back((2,), carried, tuple(out_halves), (stage,))
     two = Chain(*joined, second)
     rim_grad, far_grad, _, _, ds = carried
     rim_back = passed_along(rim_grad, "seq", -1)
     far_back = lax.all_to_all(
         far_grad.reshape(blocks, PICK, -1), "seq", split_axis=0, concat_axis=0, tiled=True
     ).reshape(slots, -1)
-    dqs, dks, dvs = zip(grads_zero, grads_one, grads_two)
-    stage = advance(big + [one], (stage,))
-    stage = advance(big + [two], (stage,))
-    token_grad, sums_one, score_grad, stage = join(
+    dqs, dks, dvs = zip(grads_one, grads_two)
+    stage = advance(big + [one], (stage,), True)
+    stage = advance(big + [two], (stage,), True)
+    token_grad, small, stage = join(
         inputs, grad_resid, dqs, dks, dvs, ds, rim_back, far_back, chosen, first_gain, first_shift, joint_weight, turned,
-        (stage,),
-    )
-    small = Total(
-        jnp.concatenate([sums_one, sums_two, expand_sums.reshape(inner // width, width), score_grad], axis=0), first
-    )
+        sums_two, expand_sums, (stage,),
+    )
+    small = Total(small, first)
     late = [one, two]
     stage = advance(big + late, (stage,))
     layer_out, stage = finish(resid, hidden, reduce_weight, reduce_bias, (stage,))
     for chains in (
-        big + late + [small], late, big + late + [small], late + [small], big + late + [small],
+        big + late + [small], big + late + [small], big + late + [small], late + [small], late + [small],
     ):
         stage = advance([chain for chain in chains if not finished(chain)], (stage,))
     while not finished(reduced):

time: 314 us -> 305 us (0.971)
  local copies, waits for them, and re-layouts: 10.8 us -> 5.82 us
  Pallas kernels: 177 us -> 173 us
    pallas_call x28 -> x26, Pallas kernels: 177 us -> 173 us  [launch(): pl.pallas_call(body, grid_spec=pltpu.PrefetchScalarGridSpec(num_scalar_pr...]
    unnamed x40 -> x18, local copies, waits for them, and re-layouts: 7.8 us -> 3.92 us
  transfers between devices with their start and end apart: 49 -> 49, of which waited for: 17 -> 16; matrix products, arithmetic and copies ran while one was open for 1% -> 1% of each run, Pallas kernels for 35% -> 33%
where the time goes in v3:
time: 305 us; the launch traced here: 301 us
  Pallas kernels  173 us (57%)
  waiting for transfers between devices  64 us (21%)
  starting transfers between devices  56.3 us (18%)
  local copies, waits for them, and re-layouts  5.82 us (2%)
    pallas_call x26, Pallas kernels, launch(): pl.pallas_call(body, grid_spec=pltpu.PrefetchScalarGridSpec(num_scalar_pr...  173 us
    ppermute x45, waiting for transfers between devices, swap(): return lax.ppermute(value, axis, [(i, i ^ bit) for i in range(count)])  56.8 us
    ppermute x45, starting transfers between devices, swap(): return lax.ppermute(value, axis, [(i, i ^ bit) for i in range(count)])  43.6 us
    all_to_all x1, waiting for transfers between devices, per_device(): lax.all_to_all(sent.reshape(blocks, PICK, -1), 'seq', split_axis=0, conca...  7.23 us
  transfers between devices with their start and end apart: 49, of which 16 were waited for; matrix products, arithmetic and copies ran while one was open for 1% of the time, Pallas kernels for 33%

profile of v3, /device:TPU:0, one launch (start us, length us, event | category | flops | bytes accessed | tf_op | source)
XLA Modules:
  0.0 301.2 jit_solution(7999886974993280733)
XLA Ops:
  0.6 11.3 %project.1 = (bf16[1024,768]{1,0:T(8,128)(2,1)}, bf16[1024,768]{1,0:T(8,128)(2,1)}, bf16[1024,768]{1,0:T(8,128)(2,1)}, bf16[1024,768]{1,0:T(8,128)(2,1)}, bf16[1...) custom-call(bf16[1024,768]{1,0:T(8,128)(2,1)} %bitcast.91, ...), custom_call_target="tpu_custom_call" | custom-call | flops 49999998976 | bytes 1048576 | tf_op jit(solution)/shard_map/project/pallas_call | solution.py:122
  14.3 5.0 %all-to-all-start = ((bf16[8,8,2432]{2,1,0:T(8,128)(2,1)}), bf16[8,8,2432]{2,1,0:T(8,128)(2,1)S(1)}, u32[]{:S(2)}, u32[]{:S(2)}) async-start(bf16[8,8,2432]{2,1,0:T(8,128)(2,1)} %bitcast.86), calls=%async_computation | async-start | bytes 622592 | tf_op jit(solution)/shard_map/all_to_all | solution.py:1173
  19.5 7.2 %all-to-all-done = bf16[8,8,2432]{2,1,0:T(8,128)(2,1)S(1)} async-done(((bf16[8,8,2432]{2,1,0:T(8,128)(2,1)}), bf16[8,8,2432]{2,1,0:T(8,128)(2,1)S(1)}, u32[]{:S(2)}, u32[]{:S(2)}) %all-to-all-start) | async-done | bytes 311328 | tf_op jit(solution)/shard_map/all_to_all | solution.py:1173
  27.6 13.7 %attend.1 = (bf16[1024,768]{1,0:T(8,128)(2,1)}, f32[3,16,256]{2,1,0:T(8,128)}, f32[8,128]{1,0:T(8,128)}) custom-call(s32[1]{0:T(128)} %bitcast.1.refs_0_, bf16[1024,768]{1,0:T(8,128)(2,1)} %get-tuple-element.146.refs_1_, bf16[1024,768]{1,0:T(8,128)(2,1)} %get-tuple-element.147.refs_2_, bf16[1024,768]{1,0:T(8,128)(2,1)} %get-tuple-element.148.refs_3_, ...), custom_call_target="tpu_custom_call" | custom-call | flops 60000002048 | bytes 1048576 | tf_op jit(solution)/shard_map/attend/pallas_call | solution.py:122
  41.3 32.4 %feed.1 = (f32[1024,768]{1,0:T(8,128)}, bf16[1024,3072]{1,0:T(8,128)(2,1)}, bf16[1024,3072]{1,0:T(8,128)(2,1)}, f32[4,768]{1,0:T(4,128)}, bf16[1536,768]{1,0:T(8...) custom-call(s32[1]{0:T(128)} %bitcast.refs_0_, ...), custom_call_target="tpu_custom_call" | custom-call | flops 165000003584 | bytes 1048576 | tf_op jit(solution)/shard_map/feed/pallas_call | solution.py:122
  74.3 16.0 %feed_back.1 = (f32[1024,768]{1,0:T(8,128)}, bf16[1024,768]{1,0:T(8,128)(2,1)}, f32[4,768]{1,0:T(4,128)}, bf16[384,768]{1,0:T(8,128)(2,1)}, bf16[384,768]{1,0:T(8,128)(2,1)}, /*index=5*/f32[8,128]{1,0:T(8,128)}) custom-call(s32[1]{0:T(128)} %bitcast.refs_0_, bf16[1024,3072]{1,0:T(8,128)(2,1)} %get-tuple-element.159.refs_1_, ...), custom_call_target="tpu_custom_call" | custom-call | flops 60000002048 | bytes 1048576 | tf_op jit(solution)/shard_map/feed_back/pallas_call | solution.py:122
  90.3 4.7 %advance.12 = (bf16[8,96,768]{2,1,0:T(8,128)(2,1)S(1)}, bf16[8,96,768]{2,1,0:T(8,128)(2,1)S(1)}, bf16[8,24,3072]{2,1,0:T(8,128)(2,1)S(1)}, bf16[8,24,3072]{2,1,0:T(8,128)(2,1)S(1)}, f32[8,128]{1,0:T(8,128)}) custom-call(s32[2]{0:T(128)S(1)} %pad_add_fusion.3.refs_0_, bf16[16,96,768]{2,1,0:T(8,128)(2,1)} %bitcast.105, ...), custom_call_target="tpu_custom_call" | custom-call | flops 10000000000 | bytes 1048576 | tf_op jit(solution)/shard_map/advance/pallas_call | solution.py:122
  96.4 22.6 %attend_back.2 = (bf16[1024,512]{1,0:T(8,128)(2,1)}, f32[1024,512]{1,0:T(8,128)}, f32[1024,512]{1,0:T(8,128)}, f32[1024,128]{1,0:T(8,128)}, bf16[64,1664]{1,0:T(...) custom-call(s32[1]{0:T(128)} %bitcast.1.refs_0_, ...), custom_call_target="tpu_custom_call" | custom-call | flops 130000003072 | bytes 1048576 | tf_op jit(solution)/shard_map/attend_back/pallas_call | solution.py:122
  119.1 3.8 %collective-permute-done.3.refs_2_.refs_4_ = bf16[8,96,768]{2,1,0:T(8,128)(2,1)S(1)} collective-permute-done((bf16[8,96,768]{2,1,0:T(8,128)(2,1)S(1)}, bf16[8,96,768]{2,1,0:T(8,128)(2,1)S(1)}, u32[]{:S(2)}, u32[]{:S(2)}) %collective-permute-start.3) | collective-permute-done | bytes 1179680 | tf_op jit(solution)/shard_map/ppermute | solution.py:920
  128.0 13.9 %attend_back.3 = (bf16[1024,256]{1,0:T(8,128)(2,1)}, f32[1024,256]{1,0:T(8,128)}, f32[1024,256]{1,0:T(8,128)}, f32[1024,128]{1,0:T(8,128)}, bf16[64,1664]{1,0:T(...) custom-call(s32[1]{0:T(128)} %bitcast.1.refs_0_, ...), custom_call_target="tpu_custom_call" | custom-call | flops 65000001536 | bytes 1048576 | tf_op jit(solution)/shard_map/attend_back/pallas_call | solution.py:122
  142.0 3.5 %advance.14 = (bf16[2,96,768]{2,1,0:T(8,128)(2,1)S(1)}, bf16[2,96,768]{2,1,0:T(8,128)(2,1)}, bf16[2,24,3072]{2,1,0:T(8,128)(2,1)S(1)}, bf16[2,24,3072]{2,1,0:T(8...) custom-call(s32[3]{0:T(128)S(1)} %pad_add_fusion.2.refs_0_, ...), custom_call_target="tpu_custom_call" | custom-call | flops 10000000000 | bytes 1048576 | tf_op jit(solution)/shard_map/advance/pallas_call | solution.py:122
  148.9 4.1 %all-to-all-start.1 = ((bf16[8,8,1664]{2,1,0:T(8,128)(2,1)}), bf16[8,8,1664]{2,1,0:T(8,128)(2,1)}, u32[]{:S(2)}, u32[]{:S(2)}) async-start(bf16[8,8,1664]{2,1,0:T(8,128)(2,1)} %bitcast.21), calls=%async_computation.1 | async-start | bytes 425984 | tf_op jit(solution)/shard_map/all_to_all | solution.py:1195
  155.2 3.2 %advance.15 = (bf16[1,96,768]{2,1,0:T(8,128)(2,1)}, bf16[1,96,768]{2,1,0:T(8,128)(2,1)}, bf16[1,24,3072]{2,1,0:T(8,128)(2,1)}, bf16[1,24,3072]{2,1,0:T(8,128)(2,...) custom-call(s32[3]{0:T(128)S(1)} %pad_add_fusion.1.refs_0_, ...), custom_call_target="tpu_custom_call" | custom-call | flops 10000000000 | bytes 1048576 | tf_op jit(solution)/shard_map/advance/pallas_call | solution.py:122
  162.6 12.7 %join.1 = (f32[1024,768]{1,0:T(8,128)}, f32[24,768]{1,0:T(8,128)}, f32[8,128]{1,0:T(8,128)}) custom-call(bf16[1024,768]{1,0:T(8,128)(2,1)} %bitcast.93, f32[1024,768]{1,0:T(8,128)} %get-tuple-element.200.refs_1_, f32[1024,128]{1,0:T(8,128)} %get-tuple-element.201.refs_2_, bf16[64,1664]{1,0:T(8,128)(2,1)} %collective-permute-done.15.refs_3_, ...), custom_call_target="tpu_custom_call" | custom-call | flops 70000001024 | bytes 1048576 | tf_op jit(solution)/shard_map/join/pallas_call | solution.py:122
  175.6 2.7 advance.16
  183.4 10.0 %finish.1 = (bf16[1024,768]{1,0:T(8,128)(2,1)}, f32[8,128]{1,0:T(8,128)}) custom-call(f32[1024,768]{1,0:T(8,128)} %get-tuple-element.153.refs_2_.refs_0_, bf16[1024,3072]{1,0:T(8,128)(2,1)} %get-tuple-element.154.refs_1_, bf16[3072,768]{1,0:T(8,128)(2,1)} %refs_2_.1, f32[768]{0:T(1024)} %refs_3_.3, f32[8,128]{1,0:T(8,128)} %get-tuple-element.214.refs_4_), custom_call_target="tpu_custom_call" | custom-call | flops 35000000512 | bytes 1048576 | tf_op jit(solution)/shard_map/finish/pallas_call | solution.py:122
  193.4 3.2 %collective-permute-done.17.refs_4_ = bf16[1,24,3072]{2,1,0:T(8,128)(2,1)S(1)} collective-permute-done((bf16[1,24,3072]{2,1,0:T(8,128)(2,1)S(1)}, bf16[1,24,3072]{2,1,0:T(8,128)(2,1)S(1)}, u32[]{:S(2)}, u32[]{:S(2)}) %collective-permute-start.17) | collective-permute-done | bytes 147488 | tf_op jit(solution)/shard_map/ppermute | solution.py:920
  203.4 7.6 %collective-permute-done.25.refs_14_ = f32[24,768]{1,0:T(8,128)S(1)} collective-permute-done((f32[24,768]{1,0:T(8,128)S(1)}, f32[24,768]{1,0:T(8,128)S(1)}, u32[]{:S(2)}, u32[]{:S(2)}) %collective-permute-start.25) | collective-permute-done | bytes 73760 | tf_op jit(solution)/shard_map/ppermute | solution.py:920
  217.5 9.3 %collective-permute-done.28.refs_6_ = bf16[1,24,1536]{2,1,0:T(8,128)(2,1)S(1)} collective-permute-done((bf16[1,24,1536]{2,1,0:T(8,128)(2,1)S(1)}, bf16[1,24,1536]{2,1,0:T(8,128)(2,1)S(1)}, u32[]{:S(2)}, u32[]{:S(2)}) %collective-permute-start.28) | collective-permute-done | bytes 73760 | tf_op jit(solution)/shard_map/ppermute | solution.py:920
  235.8 2.9 collective-permute-done.32.refs_4_
  245.2 3.1 %collective-permute-done.36.refs_6_ = f32[24,768]{1,0:T(8,128)S(1)} collective-permute-done((f32[24,768]{1,0:T(8,128)S(1)}, f32[24,768]{1,0:T(8,128)S(1)}, u32[]{:S(2)}, u32[]{:S(2)}) %collective-permute-start.36) | collective-permute-done | bytes 73760 | tf_op jit(solution)/shard_map/ppermute | solution.py:920
  254.8 17.9 %collective-permute-done.39.refs_6_ = bf16[4,24,1536]{2,1,0:T(8,128)(2,1)S(1)} collective-permute-done((bf16[4,24,1536]{2,1,0:T(8,128)(2,1)S(1)}, bf16[4,24,1536]{2,1,0:T(8,128)(2,1)S(1)}, u32[]{:S(2)}, u32[]{:S(2)}) %collective-permute-start.39) | collective-permute-done | bytes 294944 | tf_op jit(solution)/shard_map/ppermute | solution.py:920
  272.7 3.4 %advance.22 = (bf16[2,8,96,768]{3,2,1,0:T(8,128)(2,1)S(1)}, bf16[2,8,24,3072]{3,2,1,0:T(8,128)(2,1)S(1)}, bf16[2,4,24,1536]{3,2,1,0:T(8,128)(2,1)S(1)}, bf16[2,4,24,1536]{3,2,1,0:T(8,128)(2,1)S(1)}, f32[8,128]{1,0:T(8,128)}) custom-call(s32[1]{0:T(128)} %constant.170.clone.1.refs_0_, bf16[8,96,768]{2,1,0:T(8,128)(2,1)S(1)} %bitcast.54, ...), custom_call_target="tpu_custom_call" | custom-call | flops 10000000000 | bytes 1048576 | tf_op jit(solution)/shard_map/advance/pallas_call | solution.py:122
  289.1 2.8 collective-permute-done.41.refs_2_
  (128 shorter events, 82.9 us)
Async XLA Ops:
  11.9 14.8 %collective-permute-start = (bf16[64,2432]{1,0:T(8,128)(2,1)}, bf16[64,2432]{1,0:T(8,128)(2,1)S(1)}, u32[]{:S(2)}, u32[]{:S(2)}) collective-permute-start(bf16[64,2432]{1,0:T(8,128)(2,1)} %get-tuple-element.150), channel_id=1, source_target_pairs={{0,1},{1,2},{2,3},{3,4},{4,5},{5,6},{6,7},{8,9},{9,10},{10,11},{11... | collective-permute-start | bytes 933896 | tf_op jit(solution)/shard_map/ppermute | solution.py:145
  73.7 16.6 %collective-permute-start.1 = (bf16[16,96,768]{2,1,0:T(8,128)(2,1)}, bf16[16,96,768]{2,1,0:T(8,128)(2,1)S(1)}, u32[]{:S(2)}, u32[]{:S(2)}) collective-permute-start(bf16[16,96,768]{2,1,0:T(8,128)(2,1)} %bitcast.88), channel_id=1, source_target_pairs={{0,1},{1,0},{2,3},{3,2},{4,5},{5,4},{6,7},{7,6},{8,9},{9,8},{10,11... | collective-permute-start | bytes 7077896 | tf_op jit(solution)/shard_map/ppermute | solution.py:920
  73.8 16.5 %collective-permute-start.2 = (bf16[16,24,3072]{2,1,0:T(8,128)(2,1)}, bf16[16,24,3072]{2,1,0:T(8,128)(2,1)S(1)}, u32[]{:S(2)}, u32[]{:S(2)}) collective-permute-start(bf16[16,24,3072]{2,1,0:T(8,128)(2,1)} %bitcast.87), channel_id=1, source_target_pairs={{0,1},{1,0},{2,3},{3,2},{4,5},{5,4},{6,7},{7,6},{8,9},{9,8},{10,11... | collective-permute-start | bytes 7077896 | tf_op jit(solution)/shard_map/ppermute | solution.py:920
  95.0 27.9 %collective-permute-start.3 = (bf16[8,96,768]{2,1,0:T(8,128)(2,1)S(1)}, bf16[8,96,768]{2,1,0:T(8,128)(2,1)S(1)}, u32[]{:S(2)}, u32[]{:S(2)}) collective-permute-start(bf16[8,96,768]{2,1,0:T(8,128)(2,1)S(1)} %get-tuple-element.162), channel_id=1, source_target_pairs={{0,2},{1,3},{2,0},{3,1},{4,6},{5,7},{6,4},{7,5},{8,10},{9,11},{10,... | collective-permute-start | bytes 3538952 | tf_op jit(solution)/shard_map/ppermute | solution.py:920
  95.6 27.6 %collective-permute-start.4 = (bf16[8,24,3072]{2,1,0:T(8,128)(2,1)S(1)}, bf16[8,24,3072]{2,1,0:T(8,128)(2,1)S(1)}, u32[]{:S(2)}, u32[]{:S(2)}) collective-permute-start(bf16[8,24,3072]{2,1,0:T(8,128)(2,1)S(1)} %get-tuple-element.164), channel_id=1, source_target_pairs={{0,4},{1,5},{2,6},{3,7},{4,0},{5,1},{6,2},{7,3},{8,12},{9,13},{10,... | collective-permute-start | bytes 3538952 | tf_op jit(solution)/shard_map/ppermute | solution.py:920
  119.1 22.9 %collective-permute-start.7 = (bf16[16,24,1536]{2,1,0:T(8,128)(2,1)}, bf16[16,24,1536]{2,1,0:T(8,128)(2,1)S(1)}, u32[]{:S(2)}, u32[]{:S(2)}) collective-permute-start(bf16[16,24,1536]{2,1,0:T(8,128)(2,1)} %bitcast.95), channel_id=1, source_target_pairs={{0,1},{1,0},{2,3},{3,2},{4,5},{5,4},{6,7},{7,6},{8,9},{9,8},{10,11... | collective-permute-start | bytes 3538952 | tf_op jit(solution)/shard_map/ppermute | solution.py:920
  125.5 16.5 %collective-permute-start.5 = (bf16[4,96,768]{2,1,0:T(8,128)(2,1)S(1)}, bf16[4,96,768]{2,1,0:T(8,128)(2,1)S(1)}, u32[]{:S(2)}, u32[]{:S(2)}) collective-permute-start(bf16[4,96,768]{2,1,0:T(8,128)(2,1)S(1)} %get-tuple-element.171), channel_id=1, source_target_pairs={{0,4},{1,5},{2,6},{3,7},{4,0},{5,1},{6,2},{7,3},{8,12},{9,13},{10,... | collective-permute-start | bytes 1769480 | tf_op jit(solution)/shard_map/ppermute | solution.py:920
  126.4 15.6 %collective-permute-start.6 = (bf16[4,24,3072]{2,1,0:T(8,128)(2,1)S(1)}, bf16[4,24,3072]{2,1,0:T(8,128)(2,1)S(1)}, u32[]{:S(2)}, u32[]{:S(2)}) collective-permute-start(bf16[4,24,3072]{2,1,0:T(8,128)(2,1)S(1)} %get-tuple-element.173), channel_id=1, source_target_pairs={{0,8},{8,0},{16,24},{24,16},{1,9},{9,1},{17,25},{25,17},{2,10},{10... | collective-permute-start | bytes 1769480 | tf_op jit(solution)/shard_map/ppermute | solution.py:920
  147.6 15.0 %collective-permute-start.15 = (bf16[64,1664]{1,0:T(8,128)(2,1)}, bf16[64,1664]{1,0:T(8,128)(2,1)}, u32[]{:S(2)}, u32[]{:S(2)}) collective-permute-start(bf16[64,1664]{1,0:T(8,128)(2,1)} %get-tuple-element.202), channel_id=1, source_target_pairs={{1,0},{2,1},{3,2},{4,3},{5,4},{6,5},{7,6},{9,8},{10,9},{11,10},{12... | collective-permute-start | bytes 638984 | tf_op jit(solution)/shard_map/ppermute | solution.py:145
  148.9 13.7 %all-to-all-start.1 = ((bf16[8,8,1664]{2,1,0:T(8,128)(2,1)}), bf16[8,8,1664]{2,1,0:T(8,128)(2,1)}, u32[]{:S(2)}, u32[]{:S(2)}) async-start(bf16[8,8,1664]{2,1,0:T(8,128)(2,1)} %bitcast.21), calls=%async_computation.1 | async-start | bytes 425984 | tf_op jit(solution)/shard_map/all_to_all | solution.py:1195
  153.0 22.5 %collective-permute-start.13 = (bf16[8,24,1536]{2,1,0:T(8,128)(2,1)S(1)}, bf16[8,24,1536]{2,1,0:T(8,128)(2,1)S(1)}, u32[]{:S(2)}, u32[]{:S(2)}) collective-permute-start(bf16[8,24,1536]{2,1,0:T(8,128)(2,1)S(1)} %get-tuple-element.197), channel_id=1, source_target_pairs={{0,2},{1,3},{2,0},{3,1},{4,6},{5,7},{6,4},{7,5},{8,10},{9,11},{10,... | collective-permute-start | bytes 1769480 | tf_op jit(solution)/shard_map/ppermute | solution.py:920
  158.4 17.3 %collective-permute-start.14 = (bf16[8,24,1536]{2,1,0:T(8,128)(2,1)S(1)}, bf16[8,24,1536]{2,1,0:T(8,128)(2,1)S(1)}, u32[]{:S(2)}, u32[]{:S(2)}) collective-permute-start(bf16[8,24,1536]{2,1,0:T(8,128)(2,1)S(1)} %get-tuple-element.199), channel_id=1, source_target_pairs={{0,4},{1,5},{2,6},{3,7},{4,0},{5,1},{6,2},{7,3},{8,12},{9,13},{10,... | collective-permute-start | bytes 1769480 | tf_op jit(solution)/shard_map/ppermute | solution.py:920
  159.7 15.7 %collective-permute-start.11 = (bf16[1,96,768]{2,1,0:T(8,128)(2,1)}, bf16[1,96,768]{2,1,0:T(8,128)(2,1)S(1)}, u32[]{:S(2)}, u32[]{:S(2)}) collective-permute-start(bf16[1,96,768]{2,1,0:T(8,128)(2,1)} %get-tuple-element.193), channel_id=1, source_target_pairs={{0,16},{8,24},{16,0},{24,8},{1,17},{9,25},{17,1},{25,9},{2,18},{10... | collective-permute-start | bytes 442376 | tf_op jit(solution)/shard_map/ppermute | solution.py:920
  175.4 18.0 %collective-permute-start.20 = (f32[24,768]{1,0:T(8,128)}, f32[24,768]{1,0:T(8,128)S(1)}, u32[]{:S(2)}, u32[]{:S(2)}) collective-permute-start(f32[24,768]{1,0:T(8,128)} %get-tuple-element.223.refs_13_), channel_id=1, source_target_pairs={{0,1},{1,0},{2,3},{3,2},{4,5},{5,4},{6,7},{7,6},{8,9},{9,8},{10,11... | collective-permute-start | bytes 221192 | tf_op jit(solution)/shard_map/ppermute | solution.py:920
  178.4 18.2 %collective-permute-start.18 = (bf16[4,24,1536]{2,1,0:T(8,128)(2,1)S(1)}, bf16[4,24,1536]{2,1,0:T(8,128)(2,1)S(1)}, u32[]{:S(2)}, u32[]{:S(2)}) collective-permute-start(bf16[4,24,1536]{2,1,0:T(8,128)(2,1)S(1)} %get-tuple-element.220), channel_id=1, source_target_pairs={{0,4},{1,5},{2,6},{3,7},{4,0},{5,1},{6,2},{7,3},{8,12},{9,13},{10,... | collective-permute-start | bytes 884744 | tf_op jit(solution)/shard_map/ppermute | solution.py:920
  178.9 17.7 %collective-permute-start.19 = (bf16[4,24,1536]{2,1,0:T(8,128)(2,1)S(1)}, bf16[4,24,1536]{2,1,0:T(8,128)(2,1)S(1)}, u32[]{:S(2)}, u32[]{:S(2)}) collective-permute-start(bf16[4,24,1536]{2,1,0:T(8,128)(2,1)S(1)} %get-tuple-element.222), channel_id=1, source_target_pairs={{0,8},{8,0},{16,24},{24,16},{1,9},{9,1},{17,25},{25,17},{2,10},{10... | collective-permute-start | bytes 884744 | tf_op jit(solution)/shard_map/ppermute | solution.py:920
  212.3 15.4 %collective-permute-start.26 = (bf16[4,96,768]{2,1,0:T(8,128)(2,1)S(1)}, bf16[4,96,768]{2,1,0:T(8,128)(2,1)S(1)}, u32[]{:S(2)}, u32[]{:S(2)}) collective-permute-start(bf16[4,96,768]{2,1,0:T(8,128)(2,1)S(1)} %bitcast.65), channel_id=1, source_target_pairs={{0,4},{1,5},{2,6},{3,7},{4,0},{5,1},{6,2},{7,3},{8,12},{9,13},{10,... | collective-permute-start | bytes 1769480 | tf_op jit(solution)/shard_map/ppermute | solution.py:920
  213.6 16.2 %collective-permute-start.27 = (bf16[4,24,3072]{2,1,0:T(8,128)(2,1)S(1)}, bf16[4,24,3072]{2,1,0:T(8,128)(2,1)S(1)}, u32[]{:S(2)}, u32[]{:S(2)}) collective-permute-start(bf16[4,24,3072]{2,1,0:T(8,128)(2,1)S(1)} %bitcast.67), channel_id=1, source_target_pairs={{0,8},{8,0},{16,24},{24,16},{1,9},{9,1},{17,25},{25,17},{2,10},{10... | collective-permute-start | bytes 1769480 | tf_op jit(solution)/shard_map/ppermute | solution.py:920
  243.7 29.0 %collective-permute-start.37 = (bf16[8,96,768]{2,1,0:T(8,128)(2,1)S(1)}, bf16[8,96,768]{2,1,0:T(8,128)(2,1)}, u32[]{:S(2)}, u32[]{:S(2)}) collective-permute-start(bf16[8,96,768]{2,1,0:T(8,128)(2,1)S(1)} %bitcast.53), channel_id=1, source_target_pairs={{0,2},{1,3},{2,0},{3,1},{4,6},{5,7},{6,4},{7,5},{8,10},{9,11},{10,... | collective-permute-start | bytes 3538952 | tf_op jit(solution)/shard_map/ppermute | solution.py:920
  244.5 28.2 %collective-permute-start.38 = (bf16[8,24,3072]{2,1,0:T(8,128)(2,1)S(1)}, bf16[8,24,3072]{2,1,0:T(8,128)(2,1)}, u32[]{:S(2)}, u32[]{:S(2)}) collective-permute-start(bf16[8,24,3072]{2,1,0:T(8,128)(2,1)S(1)} %bitcast.55), channel_id=1, source_target_pairs={{0,4},{1,5},{2,6},{3,7},{4,0},{5,1},{6,2},{7,3},{8,12},{9,13},{10,... | collective-permute-start | bytes 3538952 | tf_op jit(solution)/shard_map/ppermute | solution.py:920
  252.1 20.6 %collective-permute-start.39 = (bf16[4,24,1536]{2,1,0:T(8,128)(2,1)S(1)}, bf16[4,24,1536]{2,1,0:T(8,128)(2,1)S(1)}, u32[]{:S(2)}, u32[]{:S(2)}) collective-permute-start(bf16[4,24,1536]{2,1,0:T(8,128)(2,1)S(1)} %bitcast.73), channel_id=1, source_target_pairs={{0,4},{1,5},{2,6},{3,7},{4,0},{5,1},{6,2},{7,3},{8,12},{9,13},{10,... | collective-permute-start | bytes 884744 | tf_op jit(solution)/shard_map/ppermute | solution.py:920
  252.9 19.8 %collective-permute-start.40 = (bf16[4,24,1536]{2,1,0:T(8,128)(2,1)S(1)}, bf16[4,24,1536]{2,1,0:T(8,128)(2,1)}, u32[]{:S(2)}, u32[]{:S(2)}) collective-permute-start(bf16[4,24,1536]{2,1,0:T(8,128)(2,1)S(1)} %bitcast.75), channel_id=1, source_target_pairs={{0,8},{8,0},{16,24},{24,16},{1,9},{9,1},{17,25},{25,17},{2,10},{10... | collective-permute-start | bytes 884744 | tf_op jit(solution)/shard_map/ppermute | solution.py:920
  276.7 15.2 %collective-permute-start.41 = (bf16[8,24,1536]{2,1,0:T(8,128)(2,1)S(1)}, bf16[8,24,1536]{2,1,0:T(8,128)(2,1)S(1)}, u32[]{:S(2)}, u32[]{:S(2)}) collective-permute-start(bf16[8,24,1536]{2,1,0:T(8,128)(2,1)S(1)} %bitcast.61), channel_id=1, source_target_pairs={{0,2},{1,3},{2,0},{3,1},{4,6},{5,7},{6,4},{7,5},{8,10},{9,11},{10,... | collective-permute-start | bytes 1769480 | tf_op jit(solution)/shard_map/ppermute | solution.py:920
  277.9 15.0 %collective-permute-start.42 = (bf16[8,24,1536]{2,1,0:T(8,128)(2,1)S(1)}, bf16[8,24,1536]{2,1,0:T(8,128)(2,1)S(1)}, u32[]{:S(2)}, u32[]{:S(2)}) collective-permute-start(bf16[8,24,1536]{2,1,0:T(8,128)(2,1)S(1)} %bitcast.63), channel_id=1, source_target_pairs={{0,4},{1,5},{2,6},{3,7},{4,0},{5,1},{6,2},{7,3},{8,12},{9,13},{10,... | collective-permute-start | bytes 1769480 | tf_op jit(solution)/shard_map/ppermute | solution.py:920
  (34 other events, 375.8 us)

commit v4 on v3

--- a/solution.py
+++ b/solution.py
@@ -529,7 +529,7 @@
     stores.wait(*range(len(stores.made)))
 
 
-def attend_back(place, q, k, v, grad, total, score, rim, far, normed, heads, groups, earlier, joined, after=(), unroll=4):
+def attend_back(place, q, k, v, grad, total, score, rim, far, normed, heads, groups, earlier, joined, after=(), unroll=8):
     rows, model = q.shape
     slots = far.shape[0]
     width = PACK * WIN
@@ -679,7 +679,7 @@
 
 
 def feed(
-    mine, mixed, tokens, cot, out_weight, out_bias, gain, shift, expand, expand_bias, reduce, tile=512, block=512,
+    mine, mixed, tokens, cot, out_weight, out_bias, gain, shift, expand, expand_bias, reduce, tile=1024, block=768,
 ):
     rows, width = tokens.shape
     inner = expand.shape[1]

time: 305 us -> 304 us (level)
  no operation moved by 1% of the time
where the time goes in v4:
time: 304 us; the launch traced here: 299 us
  Pallas kernels  171 us (56%)
  waiting for transfers between devices  64.5 us (21%)
  starting transfers between devices  56.3 us (19%)
  local copies, waits for them, and re-layouts  5.82 us (2%)
    pallas_call x26, Pallas kernels, launch(): pl.pallas_call(body, grid_spec=pltpu.PrefetchScalarGridSpec(num_scalar_pr...  171 us
    ppermute x45, waiting for transfers between devices, swap(): return lax.ppermute(value, axis, [(i, i ^ bit) for i in range(count)])  57.3 us
    ppermute x45, starting transfers between devices, swap(): return lax.ppermute(value, axis, [(i, i ^ bit) for i in range(count)])  43.6 us
    all_to_all x1, waiting for transfers between devices, per_device(): lax.all_to_all(sent.reshape(blocks, PICK, -1), 'seq', split_axis=0, conca...  7.23 us
  transfers between devices with their start and end apart: 49, of which 16 were waited for; matrix products, arithmetic and copies ran while one was open for 1% of the time, Pallas kernels for 33%

profile of v4, /device:TPU:0, one launch (start us, length us, event | category | flops | bytes accessed | tf_op | source)
XLA Modules:
  0.0 299.3 jit_solution(16164050783246692585)
XLA Ops:
  0.6 11.3 %project.1 = (bf16[1024,768]{1,0:T(8,128)(2,1)}, bf16[1024,768]{1,0:T(8,128)(2,1)}, bf16[1024,768]{1,0:T(8,128)(2,1)}, bf16[1024,768]{1,0:T(8,128)(2,1)}, bf16[1...) custom-call(bf16[1024,768]{1,0:T(8,128)(2,1)} %bitcast.91, ...), custom_call_target="tpu_custom_call" | custom-call | flops 49999998976 | bytes 1048576 | tf_op jit(solution)/shard_map/project/pallas_call | solution.py:122
  14.3 5.0 %all-to-all-start = ((bf16[8,8,2432]{2,1,0:T(8,128)(2,1)}), bf16[8,8,2432]{2,1,0:T(8,128)(2,1)S(1)}, u32[]{:S(2)}, u32[]{:S(2)}) async-start(bf16[8,8,2432]{2,1,0:T(8,128)(2,1)} %bitcast.86), calls=%async_computation | async-start | bytes 622592 | tf_op jit(solution)/shard_map/all_to_all | solution.py:1173
  19.5 7.2 %all-to-all-done = bf16[8,8,2432]{2,1,0:T(8,128)(2,1)S(1)} async-done(((bf16[8,8,2432]{2,1,0:T(8,128)(2,1)}), bf16[8,8,2432]{2,1,0:T(8,128)(2,1)S(1)}, u32[]{:S(2)}, u32[]{:S(2)}) %all-to-all-start) | async-done | bytes 311328 | tf_op jit(solution)/shard_map/all_to_all | solution.py:1173
  27.6 13.7 %attend.1 = (bf16[1024,768]{1,0:T(8,128)(2,1)}, f32[3,16,256]{2,1,0:T(8,128)}, f32[8,128]{1,0:T(8,128)}) custom-call(s32[1]{0:T(128)} %bitcast.1.refs_0_, bf16[1024,768]{1,0:T(8,128)(2,1)} %get-tuple-element.146.refs_1_, bf16[1024,768]{1,0:T(8,128)(2,1)} %get-tuple-element.147.refs_2_, bf16[1024,768]{1,0:T(8,128)(2,1)} %get-tuple-element.148.refs_3_, ...), custom_call_target="tpu_custom_call" | custom-call | flops 60000002048 | bytes 1048576 | tf_op jit(solution)/shard_map/attend/pallas_call | solution.py:122
  41.3 30.8 %feed.1 = (f32[1024,768]{1,0:T(8,128)}, bf16[1024,3072]{1,0:T(8,128)(2,1)}, bf16[1024,3072]{1,0:T(8,128)(2,1)}, f32[4,768]{1,0:T(4,128)}, bf16[1536,768]{1,0:T(8...) custom-call(s32[1]{0:T(128)} %bitcast.refs_0_, ...), custom_call_target="tpu_custom_call" | custom-call | flops 165000003584 | bytes 1048576 | tf_op jit(solution)/shard_map/feed/pallas_call | solution.py:122
  72.7 16.0 %feed_back.1 = (f32[1024,768]{1,0:T(8,128)}, bf16[1024,768]{1,0:T(8,128)(2,1)}, f32[4,768]{1,0:T(4,128)}, bf16[384,768]{1,0:T(8,128)(2,1)}, bf16[384,768]{1,0:T(8,128)(2,1)}, /*index=5*/f32[8,128]{1,0:T(8,128)}) custom-call(s32[1]{0:T(128)} %bitcast.refs_0_, bf16[1024,3072]{1,0:T(8,128)(2,1)} %get-tuple-element.159.refs_1_, ...), custom_call_target="tpu_custom_call" | custom-call | flops 60000002048 | bytes 1048576 | tf_op jit(solution)/shard_map/feed_back/pallas_call | solution.py:122
  88.7 4.7 %advance.12 = (bf16[8,96,768]{2,1,0:T(8,128)(2,1)S(1)}, bf16[8,96,768]{2,1,0:T(8,128)(2,1)S(1)}, bf16[8,24,3072]{2,1,0:T(8,128)(2,1)S(1)}, bf16[8,24,3072]{2,1,0:T(8,128)(2,1)S(1)}, f32[8,128]{1,0:T(8,128)}) custom-call(s32[2]{0:T(128)S(1)} %pad_add_fusion.3.refs_0_, bf16[16,96,768]{2,1,0:T(8,128)(2,1)} %bitcast.105, ...), custom_call_target="tpu_custom_call" | custom-call | flops 10000000000 | bytes 1048576 | tf_op jit(solution)/shard_map/advance/pallas_call | solution.py:122
  94.8 22.1 %attend_back.2 = (bf16[1024,512]{1,0:T(8,128)(2,1)}, f32[1024,512]{1,0:T(8,128)}, f32[1024,512]{1,0:T(8,128)}, f32[1024,128]{1,0:T(8,128)}, bf16[64,1664]{1,0:T(...) custom-call(s32[1]{0:T(128)} %bitcast.1.refs_0_, ...), custom_call_target="tpu_custom_call" | custom-call | flops 130000003072 | bytes 1048576 | tf_op jit(solution)/shard_map/attend_back/pallas_call | solution.py:122
  117.0 4.3 %collective-permute-done.3.refs_2_.refs_4_ = bf16[8,96,768]{2,1,0:T(8,128)(2,1)S(1)} collective-permute-done((bf16[8,96,768]{2,1,0:T(8,128)(2,1)S(1)}, bf16[8,96,768]{2,1,0:T(8,128)(2,1)S(1)}, u32[]{:S(2)}, u32[]{:S(2)}) %collective-permute-start.3) | collective-permute-done | bytes 1179680 | tf_op jit(solution)/shard_map/ppermute | solution.py:920
  126.4 13.9 %attend_back.3 = (bf16[1024,256]{1,0:T(8,128)(2,1)}, f32[1024,256]{1,0:T(8,128)}, f32[1024,256]{1,0:T(8,128)}, f32[1024,128]{1,0:T(8,128)}, bf16[64,1664]{1,0:T(...) custom-call(s32[1]{0:T(128)} %bitcast.1.refs_0_, ...), custom_call_target="tpu_custom_call" | custom-call | flops 65000001536 | bytes 1048576 | tf_op jit(solution)/shard_map/attend_back/pallas_call | solution.py:122
  140.3 3.3 %advance.14 = (bf16[2,96,768]{2,1,0:T(8,128)(2,1)S(1)}, bf16[2,96,768]{2,1,0:T(8,128)(2,1)}, bf16[2,24,3072]{2,1,0:T(8,128)(2,1)S(1)}, bf16[2,24,3072]{2,1,0:T(8...) custom-call(s32[3]{0:T(128)S(1)} %pad_add_fusion.2.refs_0_, ...), custom_call_target="tpu_custom_call" | custom-call | flops 10000000000 | bytes 1048576 | tf_op jit(solution)/shard_map/advance/pallas_call | solution.py:122
  147.1 4.1 %all-to-all-start.1 = ((bf16[8,8,1664]{2,1,0:T(8,128)(2,1)}), bf16[8,8,1664]{2,1,0:T(8,128)(2,1)}, u32[]{:S(2)}, u32[]{:S(2)}) async-start(bf16[8,8,1664]{2,1,0:T(8,128)(2,1)} %bitcast.21), calls=%async_computation.1 | async-start | bytes 425984 | tf_op jit(solution)/shard_map/all_to_all | solution.py:1195
  153.3 3.2 %advance.15 = (bf16[1,96,768]{2,1,0:T(8,128)(2,1)}, bf16[1,96,768]{2,1,0:T(8,128)(2,1)}, bf16[1,24,3072]{2,1,0:T(8,128)(2,1)}, bf16[1,24,3072]{2,1,0:T(8,128)(2,...) custom-call(s32[3]{0:T(128)S(1)} %pad_add_fusion.1.refs_0_, ...), custom_call_target="tpu_custom_call" | custom-call | flops 10000000000 | bytes 1048576 | tf_op jit(solution)/shard_map/advance/pallas_call | solution.py:122
  160.8 12.7 %join.1 = (f32[1024,768]{1,0:T(8,128)}, f32[24,768]{1,0:T(8,128)}, f32[8,128]{1,0:T(8,128)}) custom-call(bf16[1024,768]{1,0:T(8,128)(2,1)} %bitcast.93, f32[1024,768]{1,0:T(8,128)} %get-tuple-element.200.refs_1_, f32[1024,128]{1,0:T(8,128)} %get-tuple-element.201.refs_2_, bf16[64,1664]{1,0:T(8,128)(2,1)} %collective-permute-done.15.refs_3_, ...), custom_call_target="tpu_custom_call" | custom-call | flops 70000001024 | bytes 1048576 | tf_op jit(solution)/shard_map/join/pallas_call | solution.py:122
  173.8 2.7 advance.16
  181.6 10.0 %finish.1 = (bf16[1024,768]{1,0:T(8,128)(2,1)}, f32[8,128]{1,0:T(8,128)}) custom-call(f32[1024,768]{1,0:T(8,128)} %get-tuple-element.153.refs_2_.refs_0_, bf16[1024,3072]{1,0:T(8,128)(2,1)} %get-tuple-element.154.refs_1_, bf16[3072,768]{1,0:T(8,128)(2,1)} %refs_2_.1, f32[768]{0:T(1024)} %refs_3_.3, f32[8,128]{1,0:T(8,128)} %get-tuple-element.214.refs_4_), custom_call_target="tpu_custom_call" | custom-call | flops 35000000512 | bytes 1048576 | tf_op jit(solution)/shard_map/finish/pallas_call | solution.py:122
  191.5 3.2 %collective-permute-done.17.refs_4_ = bf16[1,24,3072]{2,1,0:T(8,128)(2,1)S(1)} collective-permute-done((bf16[1,24,3072]{2,1,0:T(8,128)(2,1)S(1)}, bf16[1,24,3072]{2,1,0:T(8,128)(2,1)S(1)}, u32[]{:S(2)}, u32[]{:S(2)}) %collective-permute-start.17) | collective-permute-done | bytes 147488 | tf_op jit(solution)/shard_map/ppermute | solution.py:920
  201.5 7.6 %collective-permute-done.25.refs_14_ = f32[24,768]{1,0:T(8,128)S(1)} collective-permute-done((f32[24,768]{1,0:T(8,128)S(1)}, f32[24,768]{1,0:T(8,128)S(1)}, u32[]{:S(2)}, u32[]{:S(2)}) %collective-permute-start.25) | collective-permute-done | bytes 73760 | tf_op jit(solution)/shard_map/ppermute | solution.py:920
  215.6 9.3 %collective-permute-done.28.refs_6_ = bf16[1,24,1536]{2,1,0:T(8,128)(2,1)S(1)} collective-permute-done((bf16[1,24,1536]{2,1,0:T(8,128)(2,1)S(1)}, bf16[1,24,1536]{2,1,0:T(8,128)(2,1)S(1)}, u32[]{:S(2)}, u32[]{:S(2)}) %collective-permute-start.28) | collective-permute-done | bytes 73760 | tf_op jit(solution)/shard_map/ppermute | solution.py:920
  234.0 2.9 collective-permute-done.32.refs_4_
  243.3 3.1 %collective-permute-done.36.refs_6_ = f32[24,768]{1,0:T(8,128)S(1)} collective-permute-done((f32[24,768]{1,0:T(8,128)S(1)}, f32[24,768]{1,0:T(8,128)S(1)}, u32[]{:S(2)}, u32[]{:S(2)}) %collective-permute-start.36) | collective-permute-done | bytes 73760 | tf_op jit(solution)/shard_map/ppermute | solution.py:920
  252.9 17.9 %collective-permute-done.39.refs_6_ = bf16[4,24,1536]{2,1,0:T(8,128)(2,1)S(1)} collective-permute-done((bf16[4,24,1536]{2,1,0:T(8,128)(2,1)S(1)}, bf16[4,24,1536]{2,1,0:T(8,128)(2,1)S(1)}, u32[]{:S(2)}, u32[]{:S(2)}) %collective-permute-start.39) | collective-permute-done | bytes 294944 | tf_op jit(solution)/shard_map/ppermute | solution.py:920
  270.8 3.4 %advance.22 = (bf16[2,8,96,768]{3,2,1,0:T(8,128)(2,1)S(1)}, bf16[2,8,24,3072]{3,2,1,0:T(8,128)(2,1)S(1)}, bf16[2,4,24,1536]{3,2,1,0:T(8,128)(2,1)S(1)}, bf16[2,4,24,1536]{3,2,1,0:T(8,128)(2,1)S(1)}, f32[8,128]{1,0:T(8,128)}) custom-call(s32[1]{0:T(128)} %constant.170.clone.1.refs_0_, bf16[8,96,768]{2,1,0:T(8,128)(2,1)S(1)} %bitcast.54, ...), custom_call_target="tpu_custom_call" | custom-call | flops 10000000000 | bytes 1048576 | tf_op jit(solution)/shard_map/advance/pallas_call | solution.py:122
  287.2 2.8 collective-permute-done.41.refs_2_
  (128 shorter events, 82.9 us)
Async XLA Ops:
  11.9 14.8 %collective-permute-start = (bf16[64,2432]{1,0:T(8,128)(2,1)}, bf16[64,2432]{1,0:T(8,128)(2,1)S(1)}, u32[]{:S(2)}, u32[]{:S(2)}) collective-permute-start(bf16[64,2432]{1,0:T(8,128)(2,1)} %get-tuple-element.150), channel_id=1, source_target_pairs={{0,1},{1,2},{2,3},{3,4},{4,5},{5,6},{6,7},{8,9},{9,10},{10,11},{11... | collective-permute-start | bytes 933896 | tf_op jit(solution)/shard_map/ppermute | solution.py:145
  72.1 16.6 %collective-permute-start.1 = (bf16[16,96,768]{2,1,0:T(8,128)(2,1)}, bf16[16,96,768]{2,1,0:T(8,128)(2,1)S(1)}, u32[]{:S(2)}, u32[]{:S(2)}) collective-permute-start(bf16[16,96,768]{2,1,0:T(8,128)(2,1)} %bitcast.88), channel_id=1, source_target_pairs={{0,1},{1,0},{2,3},{3,2},{4,5},{5,4},{6,7},{7,6},{8,9},{9,8},{10,11... | collective-permute-start | bytes 7077896 | tf_op jit(solution)/shard_map/ppermute | solution.py:920
  72.2 16.5 %collective-permute-start.2 = (bf16[16,24,3072]{2,1,0:T(8,128)(2,1)}, bf16[16,24,3072]{2,1,0:T(8,128)(2,1)S(1)}, u32[]{:S(2)}, u32[]{:S(2)}) collective-permute-start(bf16[16,24,3072]{2,1,0:T(8,128)(2,1)} %bitcast.87), channel_id=1, source_target_pairs={{0,1},{1,0},{2,3},{3,2},{4,5},{5,4},{6,7},{7,6},{8,9},{9,8},{10,11... | collective-permute-start | bytes 7077896 | tf_op jit(solution)/shard_map/ppermute | solution.py:920
  93.4 27.9 %collective-permute-start.3 = (bf16[8,96,768]{2,1,0:T(8,128)(2,1)S(1)}, bf16[8,96,768]{2,1,0:T(8,128)(2,1)S(1)}, u32[]{:S(2)}, u32[]{:S(2)}) collective-permute-start(bf16[8,96,768]{2,1,0:T(8,128)(2,1)S(1)} %get-tuple-element.162), channel_id=1, source_target_pairs={{0,2},{1,3},{2,0},{3,1},{4,6},{5,7},{6,4},{7,5},{8,10},{9,11},{10,... | collective-permute-start | bytes 3538952 | tf_op jit(solution)/shard_map/ppermute | solution.py:920
  94.0 27.6 %collective-permute-start.4 = (bf16[8,24,3072]{2,1,0:T(8,128)(2,1)S(1)}, bf16[8,24,3072]{2,1,0:T(8,128)(2,1)S(1)}, u32[]{:S(2)}, u32[]{:S(2)}) collective-permute-start(bf16[8,24,3072]{2,1,0:T(8,128)(2,1)S(1)} %get-tuple-element.164), channel_id=1, source_target_pairs={{0,4},{1,5},{2,6},{3,7},{4,0},{5,1},{6,2},{7,3},{8,12},{9,13},{10,... | collective-permute-start | bytes 3538952 | tf_op jit(solution)/shard_map/ppermute | solution.py:920
  117.0 23.3 %collective-permute-start.7 = (bf16[16,24,1536]{2,1,0:T(8,128)(2,1)}, bf16[16,24,1536]{2,1,0:T(8,128)(2,1)S(1)}, u32[]{:S(2)}, u32[]{:S(2)}) collective-permute-start(bf16[16,24,1536]{2,1,0:T(8,128)(2,1)} %bitcast.95), channel_id=1, source_target_pairs={{0,1},{1,0},{2,3},{3,2},{4,5},{5,4},{6,7},{7,6},{8,9},{9,8},{10,11... | collective-permute-start | bytes 3538952 | tf_op jit(solution)/shard_map/ppermute | solution.py:920
  123.9 16.4 %collective-permute-start.5 = (bf16[4,96,768]{2,1,0:T(8,128)(2,1)S(1)}, bf16[4,96,768]{2,1,0:T(8,128)(2,1)S(1)}, u32[]{:S(2)}, u32[]{:S(2)}) collective-permute-start(bf16[4,96,768]{2,1,0:T(8,128)(2,1)S(1)} %get-tuple-element.171), channel_id=1, source_target_pairs={{0,4},{1,5},{2,6},{3,7},{4,0},{5,1},{6,2},{7,3},{8,12},{9,13},{10,... | collective-permute-start | bytes 1769480 | tf_op jit(solution)/shard_map/ppermute | solution.py:920
  124.8 15.5 %collective-permute-start.6 = (bf16[4,24,3072]{2,1,0:T(8,128)(2,1)S(1)}, bf16[4,24,3072]{2,1,0:T(8,128)(2,1)S(1)}, u32[]{:S(2)}, u32[]{:S(2)}) collective-permute-start(bf16[4,24,3072]{2,1,0:T(8,128)(2,1)S(1)} %get-tuple-element.173), channel_id=1, source_target_pairs={{0,8},{8,0},{16,24},{24,16},{1,9},{9,1},{17,25},{25,17},{2,10},{10... | collective-permute-start | bytes 1769480 | tf_op jit(solution)/shard_map/ppermute | solution.py:920
  145.8 15.0 %collective-permute-start.15 = (bf16[64,1664]{1,0:T(8,128)(2,1)}, bf16[64,1664]{1,0:T(8,128)(2,1)}, u32[]{:S(2)}, u32[]{:S(2)}) collective-permute-start(bf16[64,1664]{1,0:T(8,128)(2,1)} %get-tuple-element.202), channel_id=1, source_target_pairs={{1,0},{2,1},{3,2},{4,3},{5,4},{6,5},{7,6},{9,8},{10,9},{11,10},{12... | collective-permute-start | bytes 638984 | tf_op jit(solution)/shard_map/ppermute | solution.py:145
  147.1 13.7 %all-to-all-start.1 = ((bf16[8,8,1664]{2,1,0:T(8,128)(2,1)}), bf16[8,8,1664]{2,1,0:T(8,128)(2,1)}, u32[]{:S(2)}, u32[]{:S(2)}) async-start(bf16[8,8,1664]{2,1,0:T(8,128)(2,1)} %bitcast.21), calls=%async_computation.1 | async-start | bytes 425984 | tf_op jit(solution)/shard_map/all_to_all | solution.py:1195
  151.1 22.5 %collective-permute-start.13 = (bf16[8,24,1536]{2,1,0:T(8,128)(2,1)S(1)}, bf16[8,24,1536]{2,1,0:T(8,128)(2,1)S(1)}, u32[]{:S(2)}, u32[]{:S(2)}) collective-permute-start(bf16[8,24,1536]{2,1,0:T(8,128)(2,1)S(1)} %get-tuple-element.197), channel_id=1, source_target_pairs={{0,2},{1,3},{2,0},{3,1},{4,6},{5,7},{6,4},{7,5},{8,10},{9,11},{10,... | collective-permute-start | bytes 1769480 | tf_op jit(solution)/shard_map/ppermute | solution.py:920
  156.5 17.3 %collective-permute-start.14 = (bf16[8,24,1536]{2,1,0:T(8,128)(2,1)S(1)}, bf16[8,24,1536]{2,1,0:T(8,128)(2,1)S(1)}, u32[]{:S(2)}, u32[]{:S(2)}) collective-permute-start(bf16[8,24,1536]{2,1,0:T(8,128)(2,1)S(1)} %get-tuple-element.199), channel_id=1, source_target_pairs={{0,4},{1,5},{2,6},{3,7},{4,0},{5,1},{6,2},{7,3},{8,12},{9,13},{10,... | collective-permute-start | bytes 1769480 | tf_op jit(solution)/shard_map/ppermute | solution.py:920
  157.8 15.7 %collective-permute-start.11 = (bf16[1,96,768]{2,1,0:T(8,128)(2,1)}, bf16[1,96,768]{2,1,0:T(8,128)(2,1)S(1)}, u32[]{:S(2)}, u32[]{:S(2)}) collective-permute-start(bf16[1,96,768]{2,1,0:T(8,128)(2,1)} %get-tuple-element.193), channel_id=1, source_target_pairs={{0,16},{8,24},{16,0},{24,8},{1,17},{9,25},{17,1},{25,9},{2,18},{10... | collective-permute-start | bytes 442376 | tf_op jit(solution)/shard_map/ppermute | solution.py:920
  173.5 18.0 %collective-permute-start.20 = (f32[24,768]{1,0:T(8,128)}, f32[24,768]{1,0:T(8,128)S(1)}, u32[]{:S(2)}, u32[]{:S(2)}) collective-permute-start(f32[24,768]{1,0:T(8,128)} %get-tuple-element.223.refs_13_), channel_id=1, source_target_pairs={{0,1},{1,0},{2,3},{3,2},{4,5},{5,4},{6,7},{7,6},{8,9},{9,8},{10,11... | collective-permute-start | bytes 221192 | tf_op jit(solution)/shard_map/ppermute | solution.py:920
  176.5 18.2 %collective-permute-start.18 = (bf16[4,24,1536]{2,1,0:T(8,128)(2,1)S(1)}, bf16[4,24,1536]{2,1,0:T(8,128)(2,1)S(1)}, u32[]{:S(2)}, u32[]{:S(2)}) collective-permute-start(bf16[4,24,1536]{2,1,0:T(8,128)(2,1)S(1)} %get-tuple-element.220), channel_id=1, source_target_pairs={{0,4},{1,5},{2,6},{3,7},{4,0},{5,1},{6,2},{7,3},{8,12},{9,13},{10,... | collective-permute-start | bytes 884744 | tf_op jit(solution)/shard_map/ppermute | solution.py:920
  177.1 17.7 %collective-permute-start.19 = (bf16[4,24,1536]{2,1,0:T(8,128)(2,1)S(1)}, bf16[4,24,1536]{2,1,0:T(8,128)(2,1)S(1)}, u32[]{:S(2)}, u32[]{:S(2)}) collective-permute-start(bf16[4,24,1536]{2,1,0:T(8,128)(2,1)S(1)} %get-tuple-element.222), channel_id=1, source_target_pairs={{0,8},{8,0},{16,24},{24,16},{1,9},{9,1},{17,25},{25,17},{2,10},{10... | collective-permute-start | bytes 884744 | tf_op jit(solution)/shard_map/ppermute | solution.py:920
  210.4 15.4 %collective-permute-start.26 = (bf16[4,96,768]{2,1,0:T(8,128)(2,1)S(1)}, bf16[4,96,768]{2,1,0:T(8,128)(2,1)S(1)}, u32[]{:S(2)}, u32[]{:S(2)}) collective-permute-start(bf16[4,96,768]{2,1,0:T(8,128)(2,1)S(1)} %bitcast.65), channel_id=1, source_target_pairs={{0,4},{1,5},{2,6},{3,7},{4,0},{5,1},{6,2},{7,3},{8,12},{9,13},{10,... | collective-permute-start | bytes 1769480 | tf_op jit(solution)/shard_map/ppermute | solution.py:920
  211.7 16.2 %collective-permute-start.27 = (bf16[4,24,3072]{2,1,0:T(8,128)(2,1)S(1)}, bf16[4,24,3072]{2,1,0:T(8,128)(2,1)S(1)}, u32[]{:S(2)}, u32[]{:S(2)}) collective-permute-start(bf16[4,24,3072]{2,1,0:T(8,128)(2,1)S(1)} %bitcast.67), channel_id=1, source_target_pairs={{0,8},{8,0},{16,24},{24,16},{1,9},{9,1},{17,25},{25,17},{2,10},{10... | collective-permute-start | bytes 1769480 | tf_op jit(solution)/shard_map/ppermute | solution.py:920
  241.9 28.9 %collective-permute-start.37 = (bf16[8,96,768]{2,1,0:T(8,128)(2,1)S(1)}, bf16[8,96,768]{2,1,0:T(8,128)(2,1)}, u32[]{:S(2)}, u32[]{:S(2)}) collective-permute-start(bf16[8,96,768]{2,1,0:T(8,128)(2,1)S(1)} %bitcast.53), channel_id=1, source_target_pairs={{0,2},{1,3},{2,0},{3,1},{4,6},{5,7},{6,4},{7,5},{8,10},{9,11},{10,... | collective-permute-start | bytes 3538952 | tf_op jit(solution)/shard_map/ppermute | solution.py:920
  242.6 28.2 %collective-permute-start.38 = (bf16[8,24,3072]{2,1,0:T(8,128)(2,1)S(1)}, bf16[8,24,3072]{2,1,0:T(8,128)(2,1)}, u32[]{:S(2)}, u32[]{:S(2)}) collective-permute-start(bf16[8,24,3072]{2,1,0:T(8,128)(2,1)S(1)} %bitcast.55), channel_id=1, source_target_pairs={{0,4},{1,5},{2,6},{3,7},{4,0},{5,1},{6,2},{7,3},{8,12},{9,13},{10,... | collective-permute-start | bytes 3538952 | tf_op jit(solution)/shard_map/ppermute | solution.py:920
  250.2 20.6 %collective-permute-start.39 = (bf16[4,24,1536]{2,1,0:T(8,128)(2,1)S(1)}, bf16[4,24,1536]{2,1,0:T(8,128)(2,1)S(1)}, u32[]{:S(2)}, u32[]{:S(2)}) collective-permute-start(bf16[4,24,1536]{2,1,0:T(8,128)(2,1)S(1)} %bitcast.73), channel_id=1, source_target_pairs={{0,4},{1,5},{2,6},{3,7},{4,0},{5,1},{6,2},{7,3},{8,12},{9,13},{10,... | collective-permute-start | bytes 884744 | tf_op jit(solution)/shard_map/ppermute | solution.py:920
  251.0 19.8 %collective-permute-start.40 = (bf16[4,24,1536]{2,1,0:T(8,128)(2,1)S(1)}, bf16[4,24,1536]{2,1,0:T(8,128)(2,1)}, u32[]{:S(2)}, u32[]{:S(2)}) collective-permute-start(bf16[4,24,1536]{2,1,0:T(8,128)(2,1)S(1)} %bitcast.75), channel_id=1, source_target_pairs={{0,8},{8,0},{16,24},{24,16},{1,9},{9,1},{17,25},{25,17},{2,10},{10... | collective-permute-start | bytes 884744 | tf_op jit(solution)/shard_map/ppermute | solution.py:920
  274.8 15.2 %collective-permute-start.41 = (bf16[8,24,1536]{2,1,0:T(8,128)(2,1)S(1)}, bf16[8,24,1536]{2,1,0:T(8,128)(2,1)S(1)}, u32[]{:S(2)}, u32[]{:S(2)}) collective-permute-start(bf16[8,24,1536]{2,1,0:T(8,128)(2,1)S(1)} %bitcast.61), channel_id=1, source_target_pairs={{0,2},{1,3},{2,0},{3,1},{4,6},{5,7},{6,4},{7,5},{8,10},{9,11},{10,... | collective-permute-start | bytes 1769480 | tf_op jit(solution)/shard_map/ppermute | solution.py:920
  276.1 15.0 %collective-permute-start.42 = (bf16[8,24,1536]{2,1,0:T(8,128)(2,1)S(1)}, bf16[8,24,1536]{2,1,0:T(8,128)(2,1)S(1)}, u32[]{:S(2)}, u32[]{:S(2)}) collective-permute-start(bf16[8,24,1536]{2,1,0:T(8,128)(2,1)S(1)} %bitcast.63), channel_id=1, source_target_pairs={{0,4},{1,5},{2,6},{3,7},{4,0},{5,1},{6,2},{7,3},{8,12},{9,13},{10,... | collective-permute-start | bytes 1769480 | tf_op jit(solution)/shard_map/ppermute | solution.py:920
  (34 other events, 374.0 us)

commit v5 on v4

--- a/solution.py
+++ b/solution.py
@@ -1206,12 +1206,10 @@
     late = [one, two]
     stage = advance(big + late, (stage,))
     layer_out, stage = finish(resid, hidden, reduce_weight, reduce_bias, (stage,))
-    for chains in (
-        big + late + [small], big + late + [small], big + late + [small], late + [small], late + [small],
-    ):
+    for chains in (big + late, big + late, big + late + [small], late + [small], late + [small]):
         stage = advance([chain for chain in chains if not finished(chain)], (stage,))
     while not finished(reduced):
-        stage = advance([chain for chain in big + late if not finished(chain)], (stage,))
+        stage = advance([chain for chain in big + late + [small] if not finished(chain)], (stage,))
     own_first, own_second = own_place(first), own_place(second)
     halves_one, halves_two = ends(reduced), ends(expanded)
     reduce_weight_grad, stage = widen_half(own_first, reduced, (halves_one[0], False), (), (stage,))
@@ -1219,7 +1217,7 @@
     reduce_weight_grad, stage = widen_half(own_first, reduced, (halves_one[1], True), (reduce_weight_grad,), (stage,))
     expand_weight_grad, stage = widen_half(own_second, expanded, (halves_two[1], True), (expand_weight_grad,), (stage,))
     while not (finished(one) and finished(two)):
-        stage = advance([chain for chain in late if not finished(chain)], (stage,))
+        stage = advance([chain for chain in late + [small] if not finished(chain)], (stage,))
     while not finished(small):
         stage = advance([small], (stage,))
     halves_one, halves_two = ends(one), ends(two)

time: 304 us -> 302 us (level)
  local copies, waits for them, and re-layouts: 5.82 us -> 2.74 us
    unnamed x18 -> x10, local copies, waits for them, and re-layouts: 3.92 us -> 0.85 us
  transfers between devices with their start and end apart: 49 -> 49, of which waited for: 16 -> 20; matrix products, arithmetic and copies ran while one was open for 1% -> 0% of each run, Pallas kernels for 33% -> 33%
where the time goes in v5:
time: 302 us; the launch traced here: 298 us
  Pallas kernels  173 us (57%)
  waiting for transfers between devices  64.5 us (21%)
  starting transfers between devices  56.2 us (19%)
    pallas_call x26, Pallas kernels, launch(): pl.pallas_call(body, grid_spec=pltpu.PrefetchScalarGridSpec(num_scalar_pr...  173 us
    ppermute x45, waiting for transfers between devices, swap(): return lax.ppermute(value, axis, [(i, i ^ bit) for i in range(count)])  57.2 us
    ppermute x45, starting transfers between devices, swap(): return lax.ppermute(value, axis, [(i, i ^ bit) for i in range(count)])  43.4 us
    all_to_all x1, waiting for transfers between devices, per_device(): lax.all_to_all(sent.reshape(blocks, PICK, -1), 'seq', split_axis=0, conca...  7.23 us
  transfers between devices with their start and end apart: 49, of which 20 were waited for; matrix products, arithmetic and copies ran while one was open for 0% of the time, Pallas kernels for 33%

profile of v5, /device:TPU:0, one launch (start us, length us, event | category | flops | bytes accessed | tf_op | source)
XLA Modules:
  0.0 297.8 jit_solution(8988471749897842222)
XLA Ops:
  0.6 11.3 %project.1 = (bf16[1024,768]{1,0:T(8,128)(2,1)}, bf16[1024,768]{1,0:T(8,128)(2,1)}, bf16[1024,768]{1,0:T(8,128)(2,1)}, bf16[1024,768]{1,0:T(8,128)(2,1)}, bf16[1...) custom-call(bf16[1024,768]{1,0:T(8,128)(2,1)} %bitcast.87, ...), custom_call_target="tpu_custom_call" | custom-call | flops 49999998976 | bytes 1048576 | tf_op jit(solution)/shard_map/project/pallas_call | solution.py:122
  14.3 5.0 %all-to-all-start = ((bf16[8,8,2432]{2,1,0:T(8,128)(2,1)}), bf16[8,8,2432]{2,1,0:T(8,128)(2,1)S(1)}, u32[]{:S(2)}, u32[]{:S(2)}) async-start(bf16[8,8,2432]{2,1,0:T(8,128)(2,1)} %bitcast.82), calls=%async_computation | async-start | bytes 622592 | tf_op jit(solution)/shard_map/all_to_all | solution.py:1173
  19.5 7.2 %all-to-all-done = bf16[8,8,2432]{2,1,0:T(8,128)(2,1)S(1)} async-done(((bf16[8,8,2432]{2,1,0:T(8,128)(2,1)}), bf16[8,8,2432]{2,1,0:T(8,128)(2,1)S(1)}, u32[]{:S(2)}, u32[]{:S(2)}) %all-to-all-start) | async-done | bytes 311328 | tf_op jit(solution)/shard_map/all_to_all | solution.py:1173
  27.6 13.8 %attend.1 = (bf16[1024,768]{1,0:T(8,128)(2,1)}, f32[3,16,256]{2,1,0:T(8,128)}, f32[8,128]{1,0:T(8,128)}) custom-call(s32[1]{0:T(128)} %bitcast.1.refs_0_, bf16[1024,768]{1,0:T(8,128)(2,1)} %get-tuple-element.146.refs_1_, bf16[1024,768]{1,0:T(8,128)(2,1)} %get-tuple-element.147.refs_2_, bf16[1024,768]{1,0:T(8,128)(2,1)} %get-tuple-element.148.refs_3_, ...), custom_call_target="tpu_custom_call" | custom-call | flops 60000002048 | bytes 1048576 | tf_op jit(solution)/shard_map/attend/pallas_call | solution.py:122
  41.4 30.8 %feed.1 = (f32[1024,768]{1,0:T(8,128)}, bf16[1024,3072]{1,0:T(8,128)(2,1)}, bf16[1024,3072]{1,0:T(8,128)(2,1)}, f32[4,768]{1,0:T(4,128)}, bf16[1536,768]{1,0:T(8...) custom-call(s32[1]{0:T(128)} %bitcast.refs_0_, ...), custom_call_target="tpu_custom_call" | custom-call | flops 165000003584 | bytes 1048576 | tf_op jit(solution)/shard_map/feed/pallas_call | solution.py:122
  72.7 16.0 %feed_back.1 = (f32[1024,768]{1,0:T(8,128)}, bf16[1024,768]{1,0:T(8,128)(2,1)}, f32[4,768]{1,0:T(4,128)}, bf16[384,768]{1,0:T(8,128)(2,1)}, bf16[384,768]{1,0:T(8,128)(2,1)}, /*index=5*/f32[8,128]{1,0:T(8,128)}) custom-call(s32[1]{0:T(128)} %bitcast.refs_0_, bf16[1024,3072]{1,0:T(8,128)(2,1)} %get-tuple-element.159.refs_1_, ...), custom_call_target="tpu_custom_call" | custom-call | flops 60000002048 | bytes 1048576 | tf_op jit(solution)/shard_map/feed_back/pallas_call | solution.py:122
  88.8 4.7 %advance.12 = (bf16[8,96,768]{2,1,0:T(8,128)(2,1)S(1)}, bf16[8,96,768]{2,1,0:T(8,128)(2,1)S(1)}, bf16[8,24,3072]{2,1,0:T(8,128)(2,1)S(1)}, bf16[8,24,3072]{2,1,0:T(8,128)(2,1)S(1)}, f32[8,128]{1,0:T(8,128)}) custom-call(s32[2]{0:T(128)S(1)} %pad_add_fusion.3.refs_0_, bf16[16,96,768]{2,1,0:T(8,128)(2,1)} %bitcast.101, ...), custom_call_target="tpu_custom_call" | custom-call | flops 10000000000 | bytes 1048576 | tf_op jit(solution)/shard_map/advance/pallas_call | solution.py:122
  94.9 22.1 %attend_back.2 = (bf16[1024,512]{1,0:T(8,128)(2,1)}, f32[1024,512]{1,0:T(8,128)}, f32[1024,512]{1,0:T(8,128)}, f32[1024,128]{1,0:T(8,128)}, bf16[64,1664]{1,0:T(...) custom-call(s32[1]{0:T(128)} %bitcast.1.refs_0_, ...), custom_call_target="tpu_custom_call" | custom-call | flops 130000003072 | bytes 1048576 | tf_op jit(solution)/shard_map/attend_back/pallas_call | solution.py:122
  117.1 4.3 %collective-permute-done.3.refs_2_.refs_4_ = bf16[8,96,768]{2,1,0:T(8,128)(2,1)S(1)} collective-permute-done((bf16[8,96,768]{2,1,0:T(8,128)(2,1)S(1)}, bf16[8,96,768]{2,1,0:T(8,128)(2,1)S(1)}, u32[]{:S(2)}, u32[]{:S(2)}) %collective-permute-start.3) | collective-permute-done | bytes 1179680 | tf_op jit(solution)/shard_map/ppermute | solution.py:920
  126.4 13.9 %attend_back.3 = (bf16[1024,256]{1,0:T(8,128)(2,1)}, f32[1024,256]{1,0:T(8,128)}, f32[1024,256]{1,0:T(8,128)}, f32[1024,128]{1,0:T(8,128)}, bf16[64,1664]{1,0:T(...) custom-call(s32[1]{0:T(128)} %bitcast.1.refs_0_, ...), custom_call_target="tpu_custom_call" | custom-call | flops 65000001536 | bytes 1048576 | tf_op jit(solution)/shard_map/attend_back/pallas_call | solution.py:122
  140.4 3.3 %advance.14 = (bf16[2,96,768]{2,1,0:T(8,128)(2,1)S(1)}, bf16[2,96,768]{2,1,0:T(8,128)(2,1)}, bf16[2,24,3072]{2,1,0:T(8,128)(2,1)S(1)}, bf16[2,24,3072]{2,1,0:T(8...) custom-call(s32[3]{0:T(128)S(1)} %pad_add_fusion.2.refs_0_, ...), custom_call_target="tpu_custom_call" | custom-call | flops 10000000000 | bytes 1048576 | tf_op jit(solution)/shard_map/advance/pallas_call | solution.py:122
  147.1 4.1 %all-to-all-start.1 = ((bf16[8,8,1664]{2,1,0:T(8,128)(2,1)}), bf16[8,8,1664]{2,1,0:T(8,128)(2,1)}, u32[]{:S(2)}, u32[]{:S(2)}) async-start(bf16[8,8,1664]{2,1,0:T(8,128)(2,1)} %bitcast.21), calls=%async_computation.1 | async-start | bytes 425984 | tf_op jit(solution)/shard_map/all_to_all | solution.py:1195
  153.4 3.2 %advance.15 = (bf16[1,96,768]{2,1,0:T(8,128)(2,1)}, bf16[1,96,768]{2,1,0:T(8,128)(2,1)}, bf16[1,24,3072]{2,1,0:T(8,128)(2,1)}, bf16[1,24,3072]{2,1,0:T(8,128)(2,...) custom-call(s32[3]{0:T(128)S(1)} %pad_add_fusion.1.refs_0_, ...), custom_call_target="tpu_custom_call" | custom-call | flops 10000000000 | bytes 1048576 | tf_op jit(solution)/shard_map/advance/pallas_call | solution.py:122
  160.8 12.7 %join.1 = (f32[1024,768]{1,0:T(8,128)}, f32[24,768]{1,0:T(8,128)}, f32[8,128]{1,0:T(8,128)}) custom-call(bf16[1024,768]{1,0:T(8,128)(2,1)} %bitcast.89, f32[1024,768]{1,0:T(8,128)} %get-tuple-element.200.refs_1_, f32[1024,128]{1,0:T(8,128)} %get-tuple-element.201.refs_2_, bf16[64,1664]{1,0:T(8,128)(2,1)} %collective-permute-done.15.refs_3_, ...), custom_call_target="tpu_custom_call" | custom-call | flops 70000001024 | bytes 1048576 | tf_op jit(solution)/shard_map/join/pallas_call | solution.py:122
  173.8 2.7 advance.16
  181.5 9.9 %finish.1 = (bf16[1024,768]{1,0:T(8,128)(2,1)}, f32[8,128]{1,0:T(8,128)}) custom-call(f32[1024,768]{1,0:T(8,128)} %get-tuple-element.153.refs_2_.refs_0_, bf16[1024,3072]{1,0:T(8,128)(2,1)} %get-tuple-element.154.refs_1_, bf16[3072,768]{1,0:T(8,128)(2,1)} %refs_2_.1, f32[768]{0:T(1024)} %refs_3_.3, f32[8,128]{1,0:T(8,128)} %get-tuple-element.214.refs_4_), custom_call_target="tpu_custom_call" | custom-call | flops 35000000512 | bytes 1048576 | tf_op jit(solution)/shard_map/finish/pallas_call | solution.py:122
  191.5 2.7 collective-permute-done.17.refs_4_
  199.5 5.1 %collective-permute-done.22.refs_6_.refs_8_ = bf16[2,24,1536]{2,1,0:T(8,128)(2,1)S(1)} collective-permute-done((bf16[2,24,1536]{2,1,0:T(8,128)(2,1)S(1)}, bf16[2,24,1536]{2,1,0:T(8,128)(2,1)S(1)}, u32[]{:S(2)}, u32[]{:S(2)}) %collective-permute-start.22) | collective-permute-done | bytes 147488 | tf_op jit(solution)/shard_map/ppermute | solution.py:920
  212.2 9.7 %collective-permute-done.26.refs_6_ = bf16[1,24,1536]{2,1,0:T(8,128)(2,1)S(1)} collective-permute-done((bf16[1,24,1536]{2,1,0:T(8,128)(2,1)S(1)}, bf16[1,24,1536]{2,1,0:T(8,128)(2,1)S(1)}, u32[]{:S(2)}, u32[]{:S(2)}) %collective-permute-start.26) | collective-permute-done | bytes 73760 | tf_op jit(solution)/shard_map/ppermute | solution.py:920
  233.6 2.8 collective-permute-start.34
  246.4 5.8 %collective-permute-done.39.refs_10_ = f32[24,768]{1,0:T(8,128)} collective-permute-done((f32[24,768]{1,0:T(8,128)}, f32[24,768]{1,0:T(8,128)}, u32[]{:S(2)}, u32[]{:S(2)}) %collective-permute-start.39) | collective-permute-done | bytes 73760 | tf_op jit(solution)/shard_map/ppermute | solution.py:920
  252.2 14.2 %collective-permute-done.37.refs_6_ = bf16[4,24,1536]{2,1,0:T(8,128)(2,1)} collective-permute-done((bf16[4,24,1536]{2,1,0:T(8,128)(2,1)}, bf16[4,24,1536]{2,1,0:T(8,128)(2,1)}, u32[]{:S(2)}, u32[]{:S(2)}) %collective-permute-start.37) | collective-permute-done | bytes 294944 | tf_op jit(solution)/shard_map/ppermute | solution.py:920
  266.5 3.6 %advance.22 = (bf16[2,8,96,768]{3,2,1,0:T(8,128)(2,1)S(1)}, bf16[2,8,24,3072]{3,2,1,0:T(8,128)(2,1)S(1)}, bf16[2,4,24,1536]{3,2,1,0:T(8,128)(2,1)S(1)}, bf16[2,4...) custom-call(s32[1]{0:T(128)} %constant.170.clone.1.refs_0_, ...), custom_call_target="tpu_custom_call" | custom-call | flops 10000000000 | bytes 1048576 | tf_op jit(solution)/shard_map/advance/pallas_call | solution.py:122
  293.5 4.1 %widen_joint.3 = (f32[32,24,2304]{2,1,0:T(8,128)}, f32[32,24,768]{2,1,0:T(8,128)}, f32[8,128]{1,0:T(8,128)}) custom-call(s32[1]{0:T(128)} %bitcast.39.refs_0_, s32[1]{0:T(128)} %bitcast.37.refs_0_.refs_1_, bf16[16,24,1536]{2,1,0:T(8,128)(2,1)S(1)} %collective-permute-done.45.refs_2_, ...), custom_call_target="tpu_custom_call", output_to_operand_aliasing={{0}: (4, {}), {1}: (5, {})} | custom-call | flops 20000000000 | bytes 1048576 | tf_op jit(solution)/shard_map/widen_joint/pallas_call | solution.py:122
  (120 shorter events, 83.6 us)
Async XLA Ops:
  11.9 14.8 %collective-permute-start = (bf16[64,2432]{1,0:T(8,128)(2,1)}, bf16[64,2432]{1,0:T(8,128)(2,1)S(1)}, u32[]{:S(2)}, u32[]{:S(2)}) collective-permute-start(bf16[64,2432]{1,0:T(8,128)(2,1)} %get-tuple-element.150), channel_id=1, source_target_pairs={{0,1},{1,2},{2,3},{3,4},{4,5},{5,6},{6,7},{8,9},{9,10},{10,11},{11... | collective-permute-start | bytes 933896 | tf_op jit(solution)/shard_map/ppermute | solution.py:145
  72.2 16.6 %collective-permute-start.1 = (bf16[16,96,768]{2,1,0:T(8,128)(2,1)}, bf16[16,96,768]{2,1,0:T(8,128)(2,1)S(1)}, u32[]{:S(2)}, u32[]{:S(2)}) collective-permute-start(bf16[16,96,768]{2,1,0:T(8,128)(2,1)} %bitcast.84), channel_id=1, source_target_pairs={{0,1},{1,0},{2,3},{3,2},{4,5},{5,4},{6,7},{7,6},{8,9},{9,8},{10,11... | collective-permute-start | bytes 7077896 | tf_op jit(solution)/shard_map/ppermute | solution.py:920
  72.2 16.5 %collective-permute-start.2 = (bf16[16,24,3072]{2,1,0:T(8,128)(2,1)}, bf16[16,24,3072]{2,1,0:T(8,128)(2,1)S(1)}, u32[]{:S(2)}, u32[]{:S(2)}) collective-permute-start(bf16[16,24,3072]{2,1,0:T(8,128)(2,1)} %bitcast.83), channel_id=1, source_target_pairs={{0,1},{1,0},{2,3},{3,2},{4,5},{5,4},{6,7},{7,6},{8,9},{9,8},{10,11... | collective-permute-start | bytes 7077896 | tf_op jit(solution)/shard_map/ppermute | solution.py:920
  93.4 27.9 %collective-permute-start.3 = (bf16[8,96,768]{2,1,0:T(8,128)(2,1)S(1)}, bf16[8,96,768]{2,1,0:T(8,128)(2,1)S(1)}, u32[]{:S(2)}, u32[]{:S(2)}) collective-permute-start(bf16[8,96,768]{2,1,0:T(8,128)(2,1)S(1)} %get-tuple-element.162), channel_id=1, source_target_pairs={{0,2},{1,3},{2,0},{3,1},{4,6},{5,7},{6,4},{7,5},{8,10},{9,11},{10,... | collective-permute-start | bytes 3538952 | tf_op jit(solution)/shard_map/ppermute | solution.py:920
  94.0 27.6 %collective-permute-start.4 = (bf16[8,24,3072]{2,1,0:T(8,128)(2,1)S(1)}, bf16[8,24,3072]{2,1,0:T(8,128)(2,1)S(1)}, u32[]{:S(2)}, u32[]{:S(2)}) collective-permute-start(bf16[8,24,3072]{2,1,0:T(8,128)(2,1)S(1)} %get-tuple-element.164), channel_id=1, source_target_pairs={{0,4},{1,5},{2,6},{3,7},{4,0},{5,1},{6,2},{7,3},{8,12},{9,13},{10,... | collective-permute-start | bytes 3538952 | tf_op jit(solution)/shard_map/ppermute | solution.py:920
  117.0 23.4 %collective-permute-start.7 = (bf16[16,24,1536]{2,1,0:T(8,128)(2,1)}, bf16[16,24,1536]{2,1,0:T(8,128)(2,1)S(1)}, u32[]{:S(2)}, u32[]{:S(2)}) collective-permute-start(bf16[16,24,1536]{2,1,0:T(8,128)(2,1)} %bitcast.91), channel_id=1, source_target_pairs={{0,1},{1,0},{2,3},{3,2},{4,5},{5,4},{6,7},{7,6},{8,9},{9,8},{10,11... | collective-permute-start | bytes 3538952 | tf_op jit(solution)/shard_map/ppermute | solution.py:920
  124.0 16.4 %collective-permute-start.5 = (bf16[4,96,768]{2,1,0:T(8,128)(2,1)S(1)}, bf16[4,96,768]{2,1,0:T(8,128)(2,1)S(1)}, u32[]{:S(2)}, u32[]{:S(2)}) collective-permute-start(bf16[4,96,768]{2,1,0:T(8,128)(2,1)S(1)} %get-tuple-element.171), channel_id=1, source_target_pairs={{0,4},{1,5},{2,6},{3,7},{4,0},{5,1},{6,2},{7,3},{8,12},{9,13},{10,... | collective-permute-start | bytes 1769480 | tf_op jit(solution)/shard_map/ppermute | solution.py:920
  124.8 15.6 %collective-permute-start.6 = (bf16[4,24,3072]{2,1,0:T(8,128)(2,1)S(1)}, bf16[4,24,3072]{2,1,0:T(8,128)(2,1)S(1)}, u32[]{:S(2)}, u32[]{:S(2)}) collective-permute-start(bf16[4,24,3072]{2,1,0:T(8,128)(2,1)S(1)} %get-tuple-element.173), channel_id=1, source_target_pairs={{0,8},{8,0},{16,24},{24,16},{1,9},{9,1},{17,25},{25,17},{2,10},{10... | collective-permute-start | bytes 1769480 | tf_op jit(solution)/shard_map/ppermute | solution.py:920
  145.8 15.0 %collective-permute-start.15 = (bf16[64,1664]{1,0:T(8,128)(2,1)}, bf16[64,1664]{1,0:T(8,128)(2,1)}, u32[]{:S(2)}, u32[]{:S(2)}) collective-permute-start(bf16[64,1664]{1,0:T(8,128)(2,1)} %get-tuple-element.202), channel_id=1, source_target_pairs={{1,0},{2,1},{3,2},{4,3},{5,4},{6,5},{7,6},{9,8},{10,9},{11,10},{12... | collective-permute-start | bytes 638984 | tf_op jit(solution)/shard_map/ppermute | solution.py:145
  147.1 13.7 %all-to-all-start.1 = ((bf16[8,8,1664]{2,1,0:T(8,128)(2,1)}), bf16[8,8,1664]{2,1,0:T(8,128)(2,1)}, u32[]{:S(2)}, u32[]{:S(2)}) async-start(bf16[8,8,1664]{2,1,0:T(8,128)(2,1)} %bitcast.21), calls=%async_computation.1 | async-start | bytes 425984 | tf_op jit(solution)/shard_map/all_to_all | solution.py:1195
  151.2 22.4 %collective-permute-start.13 = (bf16[8,24,1536]{2,1,0:T(8,128)(2,1)S(1)}, bf16[8,24,1536]{2,1,0:T(8,128)(2,1)S(1)}, u32[]{:S(2)}, u32[]{:S(2)}) collective-permute-start(bf16[8,24,1536]{2,1,0:T(8,128)(2,1)S(1)} %get-tuple-element.197), channel_id=1, source_target_pairs={{0,2},{1,3},{2,0},{3,1},{4,6},{5,7},{6,4},{7,5},{8,10},{9,11},{10,... | collective-permute-start | bytes 1769480 | tf_op jit(solution)/shard_map/ppermute | solution.py:920
  156.6 17.3 %collective-permute-start.14 = (bf16[8,24,1536]{2,1,0:T(8,128)(2,1)S(1)}, bf16[8,24,1536]{2,1,0:T(8,128)(2,1)S(1)}, u32[]{:S(2)}, u32[]{:S(2)}) collective-permute-start(bf16[8,24,1536]{2,1,0:T(8,128)(2,1)S(1)} %get-tuple-element.199), channel_id=1, source_target_pairs={{0,4},{1,5},{2,6},{3,7},{4,0},{5,1},{6,2},{7,3},{8,12},{9,13},{10,... | collective-permute-start | bytes 1769480 | tf_op jit(solution)/shard_map/ppermute | solution.py:920
  157.9 15.7 %collective-permute-start.11 = (bf16[1,96,768]{2,1,0:T(8,128)(2,1)}, bf16[1,96,768]{2,1,0:T(8,128)(2,1)S(1)}, u32[]{:S(2)}, u32[]{:S(2)}) collective-permute-start(bf16[1,96,768]{2,1,0:T(8,128)(2,1)} %get-tuple-element.193), channel_id=1, source_target_pairs={{0,16},{8,24},{16,0},{24,8},{1,17},{9,25},{17,1},{25,9},{2,18},{10... | collective-permute-start | bytes 442376 | tf_op jit(solution)/shard_map/ppermute | solution.py:920
  160.5 13.3 %collective-permute-start.12 = (bf16[1,24,3072]{2,1,0:T(8,128)(2,1)}, bf16[1,24,3072]{2,1,0:T(8,128)(2,1)S(1)}, u32[]{:S(2)}, u32[]{:S(2)}) collective-permute-start(bf16[1,24,3072]{2,1,0:T(8,128)(2,1)} %get-tuple-element.195), channel_id=1, source_target_pairs={{0,16},{8,24},{16,0},{24,8},{1,17},{9,25},{17,1},{25,9},{2,18},{10... | collective-permute-start | bytes 442376 | tf_op jit(solution)/shard_map/ppermute | solution.py:920
  176.6 17.6 %collective-permute-start.18 = (bf16[4,24,1536]{2,1,0:T(8,128)(2,1)S(1)}, bf16[4,24,1536]{2,1,0:T(8,128)(2,1)S(1)}, u32[]{:S(2)}, u32[]{:S(2)}) collective-permute-start(bf16[4,24,1536]{2,1,0:T(8,128)(2,1)S(1)} %get-tuple-element.220), channel_id=1, source_target_pairs={{0,4},{1,5},{2,6},{3,7},{4,0},{5,1},{6,2},{7,3},{8,12},{9,13},{10,... | collective-permute-start | bytes 884744 | tf_op jit(solution)/shard_map/ppermute | solution.py:920
  177.1 17.1 %collective-permute-start.19 = (bf16[4,24,1536]{2,1,0:T(8,128)(2,1)S(1)}, bf16[4,24,1536]{2,1,0:T(8,128)(2,1)S(1)}, u32[]{:S(2)}, u32[]{:S(2)}) collective-permute-start(bf16[4,24,1536]{2,1,0:T(8,128)(2,1)S(1)} %get-tuple-element.222), channel_id=1, source_target_pairs={{0,8},{8,0},{16,24},{24,16},{1,9},{9,1},{17,25},{25,17},{2,10},{10... | collective-permute-start | bytes 884744 | tf_op jit(solution)/shard_map/ppermute | solution.py:920
  207.4 15.3 %collective-permute-start.24 = (bf16[4,96,768]{2,1,0:T(8,128)(2,1)S(1)}, bf16[4,96,768]{2,1,0:T(8,128)(2,1)S(1)}, u32[]{:S(2)}, u32[]{:S(2)}) collective-permute-start(bf16[4,96,768]{2,1,0:T(8,128)(2,1)S(1)} %bitcast.65), channel_id=1, source_target_pairs={{0,4},{1,5},{2,6},{3,7},{4,0},{5,1},{6,2},{7,3},{8,12},{9,13},{10,... | collective-permute-start | bytes 1769480 | tf_op jit(solution)/shard_map/ppermute | solution.py:920
  209.0 15.6 %collective-permute-start.25 = (bf16[4,24,3072]{2,1,0:T(8,128)(2,1)S(1)}, bf16[4,24,3072]{2,1,0:T(8,128)(2,1)S(1)}, u32[]{:S(2)}, u32[]{:S(2)}) collective-permute-start(bf16[4,24,3072]{2,1,0:T(8,128)(2,1)S(1)} %bitcast.67), channel_id=1, source_target_pairs={{0,8},{8,0},{16,24},{24,16},{1,9},{9,1},{17,25},{25,17},{2,10},{10... | collective-permute-start | bytes 1769480 | tf_op jit(solution)/shard_map/ppermute | solution.py:920
  236.9 29.6 %collective-permute-start.29 = (bf16[8,96,768]{2,1,0:T(8,128)(2,1)S(1)}, bf16[8,96,768]{2,1,0:T(8,128)(2,1)S(1)}, u32[]{:S(2)}, u32[]{:S(2)}) collective-permute-start(bf16[8,96,768]{2,1,0:T(8,128)(2,1)S(1)} %bitcast.53), channel_id=1, source_target_pairs={{0,2},{1,3},{2,0},{3,1},{4,6},{5,7},{6,4},{7,5},{8,10},{9,11},{10,... | collective-permute-start | bytes 3538952 | tf_op jit(solution)/shard_map/ppermute | solution.py:920
  238.7 27.8 %collective-permute-start.30 = (bf16[8,24,3072]{2,1,0:T(8,128)(2,1)S(1)}, bf16[8,24,3072]{2,1,0:T(8,128)(2,1)}, u32[]{:S(2)}, u32[]{:S(2)}) collective-permute-start(bf16[8,24,3072]{2,1,0:T(8,128)(2,1)S(1)} %bitcast.55), channel_id=1, source_target_pairs={{0,4},{1,5},{2,6},{3,7},{4,0},{5,1},{6,2},{7,3},{8,12},{9,13},{10,... | collective-permute-start | bytes 3538952 | tf_op jit(solution)/shard_map/ppermute | solution.py:920
  244.0 22.5 %collective-permute-start.37 = (bf16[4,24,1536]{2,1,0:T(8,128)(2,1)}, bf16[4,24,1536]{2,1,0:T(8,128)(2,1)}, u32[]{:S(2)}, u32[]{:S(2)}) collective-permute-start(bf16[4,24,1536]{2,1,0:T(8,128)(2,1)} %bitcast.33.refs_5_), channel_id=1, source_target_pairs={{0,4},{1,5},{2,6},{3,7},{4,0},{5,1},{6,2},{7,3},{8,12},{9,13},{10,... | collective-permute-start | bytes 884744 | tf_op jit(solution)/shard_map/ppermute | solution.py:920
  244.4 22.1 %collective-permute-start.38 = (bf16[4,24,1536]{2,1,0:T(8,128)(2,1)}, bf16[4,24,1536]{2,1,0:T(8,128)(2,1)}, u32[]{:S(2)}, u32[]{:S(2)}) collective-permute-start(bf16[4,24,1536]{2,1,0:T(8,128)(2,1)} %bitcast.34.refs_7_), channel_id=1, source_target_pairs={{0,8},{8,0},{16,24},{24,16},{1,9},{9,1},{17,25},{25,17},{2,10},{10... | collective-permute-start | bytes 884744 | tf_op jit(solution)/shard_map/ppermute | solution.py:920
  270.6 15.2 %collective-permute-start.40 = (bf16[8,24,1536]{2,1,0:T(8,128)(2,1)S(1)}, bf16[8,24,1536]{2,1,0:T(8,128)(2,1)S(1)}, u32[]{:S(2)}, u32[]{:S(2)}) collective-permute-start(bf16[8,24,1536]{2,1,0:T(8,128)(2,1)S(1)} %bitcast.61), channel_id=1, source_target_pairs={{0,2},{1,3},{2,0},{3,1},{4,6},{5,7},{6,4},{7,5},{8,10},{9,11},{10,... | collective-permute-start | bytes 1769480 | tf_op jit(solution)/shard_map/ppermute | solution.py:920
  271.6 15.0 %collective-permute-start.41 = (bf16[8,24,1536]{2,1,0:T(8,128)(2,1)S(1)}, bf16[8,24,1536]{2,1,0:T(8,128)(2,1)S(1)}, u32[]{:S(2)}, u32[]{:S(2)}) collective-permute-start(bf16[8,24,1536]{2,1,0:T(8,128)(2,1)S(1)} %bitcast.63), channel_id=1, source_target_pairs={{0,4},{1,5},{2,6},{3,7},{4,0},{5,1},{6,2},{7,3},{8,12},{9,13},{10,... | collective-permute-start | bytes 1769480 | tf_op jit(solution)/shard_map/ppermute | solution.py:920
  (30 other events, 338.6 us)
